TPU v7x, 128 devices: a whole 4x4x4 slice. The times are simulated.
128 devices in a mesh: wide: 8 (over z, core), narrow: 16 (over y, x).
Axes of the slice: x: 4, y: 4, z: 4, core: 2. Of those that a mesh axis runs over, the one named last changes fastest.
Arguments:
- hidden_in: float32 [2, 64, 8192], P(None, None, 'narrow'), may hold values from -100 to 100
- attn_gain: float32 [8192], P('narrow'), may hold values from 0.1 to 1.9
- w_query: bfloat16 [8192, 8192], P('narrow', 'wide'), may hold values from -0.0625 to 0.0625
- w_key: bfloat16 [8192, 1024], P('narrow', 'wide'), may hold values from -0.0625 to 0.0625
- w_value: bfloat16 [8192, 1024], P('narrow', 'wide'), may hold values from -0.0625 to 0.0625
- w_out: bfloat16 [8192, 8192], P('wide', 'narrow'), may hold values from -0.0625 to 0.0625
- ffn_gain: float32 [8192], P('narrow'), may hold values from 0.1 to 1.9
- w_gate: bfloat16 [8192, 28672], P('narrow', 'wide'), may hold values from -0.0625 to 0.0625
- w_up: bfloat16 [8192, 28672], P('narrow', 'wide'), may hold values from -0.0625 to 0.0625
- w_down: bfloat16 [28672, 8192], P('wide', 'narrow'), may hold values from -0.03125 to 0.03125
- key_cache: bfloat16 [2, 64, 8, 2048, 128], P(None, 'narrow', 'wide'), may hold values from -256 to 256
- value_cache: bfloat16 [2, 64, 8, 2048, 128], P(None, 'narrow', 'wide'), may hold values from -6 to 6
- cache_len: int32 [2, 64], P(None, 'narrow'), may hold values from 1 to 2048, as said below
Outputs:
- hidden_out: float32 [2, 64, 8192], P(None, None, 'narrow')
Inputs may be any that keep to these rules, and one draw needn't show every extreme that they name: `cache_len`: in every micro-batch one row's cache holds exactly 2048 tokens.
All inputs are finite; a program needn't handle non-finite values.
Results may differ from a plain program's by a relative error of at most 0.0086.
Values may be sent and summed in bfloat16 or wider, within the bound.
No kernel may reach another device: no remote copies, remote signals or barrier semaphores. Data moves between devices by JAX's collectives and lax.ppermute only.
A program may use at most 128 MiB of HBM per device.

v0:
```python
import jax
import jax.numpy as jnp
from jax import lax
from jax.sharding import PartitionSpec as P

D = 8192


epsilon = 1e-05


def rotate(values, places):
    halfway = values.shape[-1] // 2
    angles_base = 500000.0 ** (-jnp.arange(halfway, dtype=jnp.float32) * 2.0 / values.shape[-1])
    angles = places * angles_base
    cosines = jnp.cos(angles)
    sinewave = jnp.sin(angles)
    lower_half = values[..., :halfway]
    upper_half = values[..., halfway:]
    return jnp.concatenate(
        [
            lower_half * cosines - upper_half * sinewave,
            upper_half * cosines + lower_half * sinewave,
        ],
        axis=-1,
    )


def attend(queries, key_new, value_new, key_rows, value_rows, length):
    scaling = queries.shape[-1] ** (-0.5)
    scores = (
        jnp.einsum("kgd,kld->kgl", queries, key_rows, preferred_element_type=jnp.float32) * scaling
    )
    visible = jnp.arange(key_rows.shape[1]) < length
    scores = jnp.where(visible, scores, -jnp.inf)
    own_score = (
        jnp.einsum("kgd,kd->kg", queries, key_new, preferred_element_type=jnp.float32) * scaling
    )
    highest = jnp.maximum(jnp.max(scores, axis=-1), own_score)
    shifted = jnp.exp(scores - highest[..., None])
    own_term = jnp.exp(own_score - highest)
    totals = jnp.sum(shifted, axis=-1) + own_term
    weights = (shifted / totals[..., None]).astype(jnp.bfloat16)
    own_weight = (own_term / totals).astype(jnp.bfloat16)
    attended = jnp.einsum("kgl,kld->kgd", weights, value_rows, preferred_element_type=jnp.float32)
    attended = (
        attended
        + own_weight.astype(jnp.float32)[..., None] * value_new.astype(jnp.float32)[:, None, :]
    )
    return attended.astype(jnp.bfloat16)


def body(
    hidden_in,
    attn_gain,
    w_query,
    w_key,
    w_value,
    w_out,
    ffn_gain,
    w_gate,
    w_up,
    w_down,
    key_cache,
    value_cache,
    cache_len,
):
    head_size = key_cache.shape[-1]
    local_rows = key_cache.shape[1]
    kv_here = key_cache.shape[2]
    results = []
    for micro_index in range(hidden_in.shape[0]):
        stream = hidden_in[micro_index]
        squares = jnp.sum(stream * stream, axis=-1)
        normed = (stream * attn_gain).astype(jnp.bfloat16)
        query_part = jnp.dot(normed, w_query, preferred_element_type=jnp.float32)
        key_part = jnp.dot(normed, w_key, preferred_element_type=jnp.float32)
        value_part = jnp.dot(normed, w_value, preferred_element_type=jnp.float32)
        all_squares = lax.psum(squares, "narrow")
        query_rows, key_rows_new, value_rows_new = (
            lax.psum_scatter(query_part, "narrow", scatter_dimension=0, tiled=True),
            lax.psum_scatter(key_part, "narrow", scatter_dimension=0, tiled=True),
            lax.psum_scatter(value_part, "narrow", scatter_dimension=0, tiled=True),
        )
        own_squares = lax.dynamic_slice_in_dim(
            all_squares, lax.axis_index("narrow") * local_rows, local_rows
        )
        factor = lax.rsqrt(own_squares / D + epsilon)[:, None]
        places = cache_len[micro_index].astype(jnp.float32)[:, None, None]
        queries = rotate((query_rows * factor).reshape(local_rows, -1, head_size), places).astype(
            jnp.bfloat16
        )
        keys_new = rotate(
            (key_rows_new * factor).reshape(local_rows, kv_here, head_size), places
        ).astype(jnp.bfloat16)
        values_new = (
            (value_rows_new * factor).reshape(local_rows, kv_here, head_size).astype(jnp.bfloat16)
        )
        queries = queries.reshape(local_rows, kv_here, -1, head_size)
        attended = jax.vmap(attend)(
            queries,
            keys_new,
            values_new,
            key_cache[micro_index],
            value_cache[micro_index],
            cache_len[micro_index],
        )
        attended = attended.reshape(local_rows, -1)
        out_terms = jnp.dot(
            lax.all_gather(attended, "narrow", axis=0, tiled=True),
            w_out,
            preferred_element_type=jnp.float32,
        )
        middle = stream + lax.psum(out_terms, "wide")
        squares_two = jnp.sum(middle * middle, axis=-1)
        normed_two = (middle * ffn_gain).astype(jnp.bfloat16)
        gate_part = jnp.dot(normed_two, w_gate, preferred_element_type=jnp.float32)
        up_part = jnp.dot(normed_two, w_up, preferred_element_type=jnp.float32)
        gate_sum, up_sum, summed_two = lax.psum((gate_part, up_part, squares_two), "narrow")
        factor_two = lax.rsqrt(summed_two / D + epsilon)[:, None]
        hidden = (jax.nn.silu(gate_sum * factor_two) * (up_sum * factor_two)).astype(jnp.bfloat16)
        down_terms = jnp.dot(hidden, w_down, preferred_element_type=jnp.float32)
        results.append(middle + lax.psum(down_terms, "wide"))
    return jnp.stack(results)


def solution(mesh):
    return jax.shard_map(
        body,
        mesh=mesh,
        in_specs=(
            P(None, None, "narrow"),
            P("narrow"),
            P("narrow", "wide"),
            P("narrow", "wide"),
            P("narrow", "wide"),
            P("wide", "narrow"),
            P("narrow"),
            P("narrow", "wide"),
            P("narrow", "wide"),
            P("wide", "narrow"),
            P(None, "narrow", "wide", None, None),
            P(None, "narrow", "wide", None, None),
            P(None, "narrow"),
        ),
        out_specs=P(None, None, "narrow"),
        check_vma=False,
    )
```

profile of v0, /device:TPU:1, one launch (start us, length us, event | category | flops | bytes accessed | tf_op | source)
XLA Modules:
  0.0 488.6 jit_solution(1164934020108054758)
XLA Ops:
  6.5 1.8 fusion.19
  8.3 1.7 fusion.80
  10.0 1.7 fusion.79
  11.7 1.7 fusion.76
  13.3 1.7 fusion.75
  15.1 1.0 fusion.74
  16.1 1.0 fusion.78
  18.6 81.9 %all-reduce.18.cloned.1.call-done = (f32[64]{0:T(128)}, f32[64,128]{1,0:T(8,128)}, f32[64,128]{1,0:T(8,128)}, f32[64]{0:T(128)}, f32[64,128]{1,0:T(8,128)}, /*index=5*/f32[64,128]{1,0:T(8,128)}) async-done(((f32[64]{0:T(128)}, f32[64,128]{1,0:T(8,128)}, f32[64,128]{1,0:T(8,128)}, f32[64]{0:T(128)}, f32[64,128]{1,0:T(8,128)}, /*index=5*/f32[64,128]{1,0:T(8,128)}), (f32[64]{0:T(128)}, f32[64,128]{1,0:T(8,128)}, ...) | async-done | bytes 131600 | tf_op jit(solution)/shard_map/psum | solution.py:79
  102.0 0.8 fusion.54
  103.0 85.8 %all-reduce.22.cloned.1.call-done = (f32[64,1024]{1,0:T(8,128)}, f32[64,1024]{1,0:T(8,128)}) async-done(((f32[64,1024]{1,0:T(8,128)}, f32[64,1024]{1,0:T(8,128)}), (f32[64,1024]{1,0:T(8,128)}, f32[64,1024]{1,0:T(8,128)})) %all-reduce.22.cloned.1.call-update) | async-done | bytes 524304
  188.8 0.8 fusion.28
  190.0 2.4 fusion.73
  192.6 2.0 fusion.7
  194.6 17.1 %all-gather = bf16[16,4,1024]{2,1,0:T(4,128)(2,1)S(1)} all-gather(bf16[1,4,1024]{2,1,0:T(4,128)(2,1)S(1)} %reshape.424), channel_id=1, replica_groups=mesh['wide'=8,'narrow'=16] {'narrow'}, dimensions={0}, use_global_device_ids=true | all-gather | bytes 139264 | tf_op jit(solution)/shard_map/all_gather | solution.py:110
  212.1 2.4 fusion.72
  214.7 2.0 fusion.6
  216.8 16.4 %all-gather.1 = bf16[16,4,1024]{2,1,0:T(4,128)(2,1)S(1)} all-gather(bf16[1,4,1024]{2,1,0:T(4,128)(2,1)S(1)} %reshape.426), channel_id=1, replica_groups=mesh['wide'=8,'narrow'=16] {'narrow'}, dimensions={0}, use_global_device_ids=true | all-gather | bytes 139264 | tf_op jit(solution)/shard_map/all_gather | solution.py:110
  233.2 0.9 fusion.77
  234.1 1.0 fusion.81
  235.2 69.8 %all-reduce.26.cloned.1.call-done = (f32[64,512]{1,0:T(8,128)}, f32[64,512]{1,0:T(8,128)}) async-done(((f32[64,512]{1,0:T(8,128)}, f32[64,512]{1,0:T(8,128)}), (f32[64,512]{1,0:T(8,128)}, f32[64,512]{1,0:T(8,128)})) %all-reduce.26.cloned.1.call-update) | async-done | bytes 262160 | tf_op jit(solution)/shard_map/psum | solution.py:114
  305.0 1.3 multiply_reduce_fusion.1
  306.2 3.9 fusion.24
  310.1 1.7 fusion.25
  311.8 1.7 fusion.26
  313.5 1.7 fusion.27
  315.3 33.9 %all-reduce.6 = (f32[64]{0:T(128)S(1)}, f32[64]{0:T(128)S(1)}) all-reduce(f32[64]{0:T(128)S(1)} %get-tuple-element.31, f32[64]{0:T(128)S(1)} %get-tuple-element.25), channel_id=1, replica_groups=mesh['wide'=8,'narrow'=16] {'narrow'}, use_global_device_ids=true, to_apply=%region_23.24 | all-reduce | flops 128 | bytes 1024 | tf_op jit(solution)/shard_map/psum | solution.py:119
  349.2 66.4 %all-reduce.20.cloned.1.call-done = (f32[64,3584]{1,0:T(8,128)}, f32[64,3584]{1,0:T(8,128)}, f32[64,3584]{1,0:T(8,128)}, f32[64,3584]{1,0:T(8,128)}) async-done(((f32[64,3584]{1,0:T(8,128)}, f32[64,3584]{1,0:T(8,128)}, f32[64,3584]{1,0:T(8,128)}, f32[64,3584]{1,0:T(8,128)}), (f32[64,3584]{1,0:T(8,128)}, f32[64,3584]{1,0:T(8,128)}, f32[64,3584]{1,0:T(8,128)}, ...) | async-done | bytes 3670032 | tf_op jit(solution)/shard_map/psum | solution.py:119
  415.6 4.2 fusion.9
  419.8 1.4 fusion.8
  421.2 58.3 %all-reduce.24.cloned.1.call-done = (f32[64,512]{1,0:T(8,128)}, f32[64,512]{1,0:T(8,128)}) async-done(((f32[64,512]{1,0:T(8,128)}, f32[64,512]{1,0:T(8,128)}), (f32[64,512]{1,0:T(8,128)}, f32[64,512]{1,0:T(8,128)})) %all-reduce.24.cloned.1.call-update) | async-done | bytes 262160 | tf_op jit(solution)/shard_map/psum | solution.py:123
  479.5 0.9 add_bitcast_fusion
  480.5 0.9 add_bitcast_fusion.1
  (61 shorter events, 4.6 us)
Async XLA Ops:
  6.5 8.5 %copy-start = (bf16[512,1024]{1,0:T(8,128)(2,1)S(1)}, bf16[512,1024]{1,0:T(8,128)(2,1)}, u32[]{:S(2)}) copy-start(bf16[512,1024]{1,0:T(8,128)(2,1)} %param.15) | copy-start | bytes 3145732
  6.5 10.7 %copy-start.10 = (u32[128]{0:T(128)S(1)}, u32[128]{0:T(128)}, u32[]{:S(2)}) copy-start(u32[128]{0:T(128)} %constant.43) | copy-start | bytes 1540
  6.5 10.7 %copy-start.6 = (s32[2,4]{1,0:T(2,128)S(1)}, s32[2,4]{1,0:T(2,128)}, u32[]{:S(2)}) copy-start(s32[2,4]{1,0:T(2,128)} %param.25) | copy-start | bytes 100
  6.5 94.0 %all-reduce.18.cloned.1.call-start = ((), (), s32[]{:S(2)}) async-start(), calls=%async_computation | async-start | bytes 264192 | tf_op jit(solution)/shard_map/psum | solution.py:79
  15.0 173.8 %all-reduce.22.cloned.1.call-start = ((), (), s32[]{:S(2)}) async-start(), calls=%async_computation.2 | async-start | bytes 1048576
  17.1 287.8 %all-reduce.26.cloned.1.call-start = ((), (), s32[]{:S(2)}) async-start(), calls=%async_computation.4 | async-start | bytes 524288 | tf_op jit(solution)/shard_map/psum | solution.py:114
  194.6 38.6 %copy-start.3 = (bf16[1024,512]{1,0:T(8,128)(2,1)S(1)}, bf16[1024,512]{1,0:T(8,128)(2,1)}, u32[]{:S(2)}) copy-start(bf16[1024,512]{1,0:T(8,128)(2,1)} %param.18) | copy-start | bytes 3145732
  214.5 90.5 %copy-start.4 = (f32[2,64,512]{2,1,0:T(8,128)S(1)}, f32[2,64,512]{2,1,0:T(8,128)}, u32[]{:S(2)}) copy-start(f32[2,64,512]{2,1,0:T(8,128)} %param.13) | copy-start | bytes 786436
  214.7 91.5 %copy-start.5 = (f32[512]{0:T(512)S(1)}, f32[512]{0:T(512)}, u32[]{:S(2)}) copy-start(f32[512]{0:T(512)} %param.19) | copy-start | bytes 6148
  235.1 180.4 %all-reduce.20.cloned.1.call-start = ((), (), s32[]{:S(2)}) async-start(), calls=%async_computation.1 | async-start | bytes 7340032 | tf_op jit(solution)/shard_map/psum | solution.py:119
  305.0 5.2 %copy-start.2 = (bf16[512,3584]{1,0:T(8,128)(2,1)S(1)}, bf16[512,3584]{1,0:T(8,128)(2,1)}, u32[]{:S(2)}) copy-start(bf16[512,3584]{1,0:T(8,128)(2,1)} %param.20) | copy-start | bytes 11010052
  306.2 5.6 %copy-start.1 = (bf16[512,3584]{1,0:T(8,128)(2,1)S(1)}, bf16[512,3584]{1,0:T(8,128)(2,1)}, u32[]{:S(2)}) copy-start(bf16[512,3584]{1,0:T(8,128)(2,1)} %param.21) | copy-start | bytes 11010052
  315.2 164.3 %all-reduce.24.cloned.1.call-start = ((), (), s32[]{:S(2)}) async-start(), calls=%async_computation.3 | async-start | bytes 524288 | tf_op jit(solution)/shard_map/psum | solution.py:123
  415.6 4.2 copy-start.7
  415.6 4.2 copy-start.8
  415.6 4.2 copy-start.9
Sparse Core Ops, SparseCore 0:
  15.2 85.3 all-reduce.17
  103.8 85.0 all-reduce.21
  235.2 69.6 all-reduce.25
  315.4 100.1 all-reduce.19
  421.3 58.1 all-reduce.23
where the time goes:
time: 490 us; the launch traced here: 489 us
  waiting for transfers between devices  362 us (74%)
  blocking collectives  67.4 us (14%)
  matrix products  34.3 us (7%)
  between operations  13.9 us (3%)
  other arithmetic  9.79 us (2%)
    unnamed x6, waiting for transfers between devices  85.9 us
    psum x1, waiting for transfers between devices, body(): all_squares = lax.psum(squares, 'narrow')  81.9 us
    psum x1, waiting for transfers between devices, body(): middle = stream + lax.psum(out_terms, 'wide')  69.8 us
    psum x1, waiting for transfers between devices, body(): lax.psum((gate_part, up_part, squares_two), 'narrow')  66.4 us
    psum x1, waiting for transfers between devices, body(): results.append(middle + lax.psum(down_terms, 'wide'))  58.3 us
    psum x1, blocking collectives, body(): lax.psum((gate_part, up_part, squares_two), 'narrow')  33.9 us
    all_gather x2, blocking collectives, body(): lax.all_gather(attended, 'narrow', axis=0, tiled=True)  33.5 us
  transfers between devices with their start and end apart: 5, of which 5 were waited for; matrix products, arithmetic and copies ran while one was open for 1% of the time, Pallas kernels for 0%

commit v1 on v0

v1 whole, which is shorter than its diff:
```python
import jax
import jax.numpy as jnp
from jax import lax
from jax.sharding import PartitionSpec as P

D = 8192
EPSILON = 1e-05
BF16 = jnp.bfloat16
F32 = jnp.float32


def swap_core():
    return [(z * 2 + c, z * 2 + 1 - c) for z in range(4) for c in range(2)]


def swap_z(partner):
    return [(z * 2 + c, partner[z] * 2 + c) for z in range(4) for c in range(2)]


STEPS = (swap_core(), swap_z((1, 0, 3, 2)), swap_z((3, 2, 1, 0)))


def rounded(values):
    return lax.reduce_precision(values, 8, 7)


def sum_wide(total):
    for pairs in STEPS:
        mine = rounded(total)
        other = lax.ppermute(mine.astype(BF16), "wide", pairs)
        total = mine + other.astype(F32)
    return total


def split_squares(squares, width):
    high = rounded(squares)
    low = squares - high
    lane = lax.broadcasted_iota(jnp.int32, (squares.shape[0], width), 1)
    return jnp.where(lane == 0, high[:, None], jnp.where(lane == 1, low[:, None], 0.0)).astype(BF16)


def exchange(payload):
    return lax.all_to_all(payload, "narrow", 0, 0, tiled=True)


def rotate(values, places):
    halfway = values.shape[-1] // 2
    angles_base = 500000.0 ** (-jnp.arange(halfway, dtype=F32) * 2.0 / values.shape[-1])
    angles = places * angles_base
    cosines = jnp.cos(angles)
    sinewave = jnp.sin(angles)
    a = values[..., :halfway]
    b = values[..., halfway:]
    return jnp.concatenate([a * cosines - b * sinewave, b * cosines + a * sinewave], axis=-1)


def body(
    hidden_in,
    attn_gain,
    w_query,
    w_key,
    w_value,
    w_out,
    ffn_gain,
    w_gate,
    w_up,
    w_down,
    key_cache,
    value_cache,
    cache_len,
):
    micro, _, width = hidden_in.shape
    rows = key_cache.shape[1]
    here = micro * rows
    parts = 16
    head = 128
    stream = hidden_in.reshape(micro, parts, rows, width).transpose(1, 0, 2, 3).reshape(-1, width)
    squares = jnp.sum(stream * stream, axis=-1)
    normed = (stream * attn_gain).astype(BF16)
    sums = [jnp.dot(normed, w, preferred_element_type=F32).astype(BF16) for w in (w_query, w_key, w_value)]
    payload = jnp.concatenate(sums + [split_squares(squares, head)], axis=-1)
    got = exchange(payload.reshape(parts, here, -1)).astype(F32).sum(axis=0)
    heads = w_query.shape[1] // head
    factor = lax.rsqrt((got[:, -head] + got[:, -head + 1]) / D + EPSILON)[:, None]
    lengths = cache_len.reshape(here)
    places = lengths.astype(F32)[:, None, None]
    split = heads * head
    queries = rotate((got[:, :split] * factor).reshape(here, heads, head), places).astype(BF16)
    key_new = rotate((got[:, split : split + head] * factor).reshape(here, 1, head), places).astype(BF16)
    value_new = (got[:, split + head : split + 2 * head] * factor).astype(BF16)

    keys = key_cache.reshape(here, -1, head)
    values = value_cache.reshape(here, -1, head)
    scaling = head ** (-0.5)
    scores = jnp.einsum("rgd,rld->rgl", queries, keys, preferred_element_type=F32) * scaling
    visible = jnp.arange(keys.shape[1])[None, None, :] < lengths[:, None, None]
    scores = jnp.where(visible, scores, -jnp.inf)
    own = jnp.sum(queries.astype(F32) * key_new.astype(F32), axis=-1) * scaling
    highest = jnp.maximum(jnp.max(scores, axis=-1), own)
    shifted = jnp.exp(scores - highest[..., None])
    own_term = jnp.exp(own - highest)
    totals = jnp.sum(shifted, axis=-1) + own_term
    weights = (shifted / totals[..., None]).astype(BF16)
    own_weight = rounded(own_term / totals)
    attended = jnp.einsum("rgl,rld->rgd", weights, values, preferred_element_type=F32)
    attended = attended + own_weight[..., None] * value_new.astype(F32)[:, None, :]
    attended = attended.astype(BF16).reshape(here, split)

    all_attended = exchange(jnp.broadcast_to(attended[None], (parts, here, split)))
    middle = stream + sum_wide(
        jnp.dot(all_attended.reshape(-1, split), w_out, preferred_element_type=F32)
    )
    squares_two = jnp.sum(middle * middle, axis=-1)
    normed_two = (middle * ffn_gain).astype(BF16)
    units = w_gate.shape[1]
    sums = [jnp.dot(normed_two, w, preferred_element_type=F32).astype(BF16) for w in (w_gate, w_up)]
    payload = jnp.concatenate(sums + [split_squares(squares_two, head)], axis=-1)
    got = exchange(payload.reshape(parts, here, -1)).astype(F32).sum(axis=0)
    factor_two = lax.rsqrt((got[:, -head] + got[:, -head + 1]) / D + EPSILON)[:, None]
    hidden = jax.nn.silu(got[:, :units] * factor_two) * (got[:, units : 2 * units] * factor_two)
    hidden = hidden.astype(BF16)
    all_hidden = exchange(jnp.broadcast_to(hidden[None], (parts, here, units)))
    result = middle + sum_wide(
        jnp.dot(all_hidden.reshape(-1, units), w_down, preferred_element_type=F32)
    )
    return result.reshape(parts, micro, rows, width).transpose(1, 0, 2, 3).reshape(hidden_in.shape)


def solution(mesh):
    return jax.shard_map(
        body,
        mesh=mesh,
        in_specs=(
            P(None, None, "narrow"),
            P("narrow"),
            P("narrow", "wide"),
            P("narrow", "wide"),
            P("narrow", "wide"),
            P("wide", "narrow"),
            P("narrow"),
            P("narrow", "wide"),
            P("narrow", "wide"),
            P("wide", "narrow"),
            P(None, "narrow", "wide", None, None),
            P(None, "narrow", "wide", None, None),
            P(None, "narrow"),
        ),
        out_specs=P(None, None, "narrow"),
        check_vma=False,
    )
```

time: 490 us -> 117 us (0.24)
  waiting for transfers between devices: 362 us -> 24 us
  matrix products: 34.3 us -> 9.35 us
  starting transfers between devices: 0.17 us -> 22.8 us
  blocking collectives: 67.4 us -> 52.3 us
  between operations: 13.9 us -> 0.31 us
  other arithmetic: 9.79 us -> 4.29 us
    psum x4 -> x0, waiting for transfers between devices: 276 us -> none  [the longest x1 81.9 us: body(): all_squares = lax.psum(squares, 'narrow')]
    unnamed x6 -> x0, waiting for transfers between devices: 85.9 us -> none
    all_to_all x0 -> x3, blocking collectives: none -> 52.3 us  [exchange(): return lax.all_to_all(payload, 'narrow', 0, 0, tiled=True)]
    psum x1 -> x0, blocking collectives: 33.9 us -> none  [body(): lax.psum((gate_part, up_part, squares_two), 'narrow')]
    all_gather x2 -> x0, blocking collectives: 33.5 us -> none  [body(): lax.all_gather(attended, 'narrow', axis=0, tiled=True)]
    dot_general x20 -> x9, matrix products: 34.3 us -> 9.35 us  [the longest x1 3.9 us: body(): jnp.einsum('rgd,rld->rgl', queries, keys, preferred_element_type=F32)]
    ppermute x0 -> x6, waiting for transfers between devices: none -> 15.5 us  [sum_wide(): other = lax.ppermute(mine.astype(BF16), 'wide', pairs)]
    ppermute x0 -> x6, starting transfers between devices: none -> 15.2 us  [sum_wide(): other = lax.ppermute(mine.astype(BF16), 'wide', pairs)]
  transfers between devices with their start and end apart: 5 -> 7, of which waited for: 5 -> 7; matrix products, arithmetic and copies ran while one was open for 1% -> 0% of each run, Pallas kernels for 0% -> 0%
where the time goes in v1:
time: 117 us; the launch traced here: 116 us
  blocking collectives  52.3 us (45%)
  waiting for transfers between devices  24 us (21%)
  starting transfers between devices  22.8 us (19%)
  matrix products  9.35 us (8%)
  other arithmetic  4.29 us (4%)
  local copies, waits for them, and re-layouts  2.45 us (2%)
    all_to_all x3, blocking collectives, exchange(): return lax.all_to_all(payload, 'narrow', 0, 0, tiled=True)  52.3 us
    ppermute x6, waiting for transfers between devices, sum_wide(): other = lax.ppermute(mine.astype(BF16), 'wide', pairs)  15.5 us
    ppermute x6, starting transfers between devices, sum_wide(): other = lax.ppermute(mine.astype(BF16), 'wide', pairs)  15.2 us
    all_to_all x1, waiting for transfers between devices, exchange(): return lax.all_to_all(payload, 'narrow', 0, 0, tiled=True)  8.51 us
    all_to_all x1, starting transfers between devices, exchange(): return lax.all_to_all(payload, 'narrow', 0, 0, tiled=True)  7.58 us
    dot_general x1, matrix products, body(): jnp.einsum('rgd,rld->rgl', queries, keys, preferred_element_type=F32)  3.9 us
    dot_general x3, matrix products, body(): jnp.dot(normed, w, preferred_element_type=F32).astype(BF16)  2.48 us
  transfers between devices with their start and end apart: 7, of which 7 were waited for; matrix products, arithmetic and copies ran while one was open for 0% of the time, Pallas kernels for 0%

profile of v1, /device:TPU:1, one launch (start us, length us, event | category | flops | bytes accessed | tf_op | source)
XLA Modules:
  0.0 115.6 jit_solution(869487554351457668)
XLA Ops:
  0.0 1.1 reshape.247
  1.5 0.7 multiply_convert_fusion.1
  2.2 1.1 convolution_convert_fusion.3
  3.3 1.1 convolution_convert_fusion.4
  4.4 0.3 convolution_convert_fusion.2
  4.8 0.8 maximum_bitcast_fusion.1
  5.6 7.6 %all-to-all-start = ((bf16[16,8,1408]{2,1,0:T(8,128)(2,1)}), bf16[16,8,1408]{2,1,0:T(8,128)(2,1)S(1)}, u32[]{:S(2)}, u32[]{:S(2)}) async-start(bf16[16,8,1408]{2,1,0:T(8,128)(2,1)} %maximum_bitcast_fusion.1), calls=%async_computation | async-start | bytes 720896 | tf_op jit(solution)/shard_map/all_to_all | solution.py:43
  13.5 8.5 %all-to-all-done = bf16[16,8,1408]{2,1,0:T(8,128)(2,1)S(1)} async-done(((bf16[16,8,1408]{2,1,0:T(8,128)(2,1)}), bf16[16,8,1408]{2,1,0:T(8,128)(2,1)S(1)}, u32[]{:S(2)}, u32[]{:S(2)}) %all-to-all-start) | async-done | bytes 360480 | tf_op jit(solution)/shard_map/all_to_all | solution.py:43
  22.1 0.2 fusion.32
  22.9 3.9 %fusion.40 = (f32[8,8]{1,0:T(8,128)S(1)}, f32[8,8,2048]{2,1,0:T(8,128)S(1)}) fusion(bf16[8,2048,128]{2,1,0:T(8,128)(2,1)} %bitcast.51, bf16[8,8,64]{2,1,0:T(8,128)(2,1)S(1)} %get-tuple-element.10, bf16[8,8,64]{2,1,0:T(8,128)(2,1)S(1)} %get-tuple-element.9, pred[8,2048]{1,0:T(8,128)(4,1)S(1)} %iota_compare_fusion), kind=kOutput, calls=%fused_computation.95 | convolution fusion | flops 33980352 | bytes 4751616 | tf_op jit(solution)/shard_map/rgd,rld->rgl/dot_general | solution.py:95
  26.8 0.2 fusion.4
  27.1 0.7 fusion.2
  27.8 10.5 %all_to_all.20 = bf16[16,8,1024]{2,1,0:T(8,128)(2,1)S(1)} all-to-all(bf16[16,8,1024]{2,1,0:T(8,128)(2,1)S(1)} %broadcast_in_dim.78), channel_id=1, replica_groups=mesh['wide'=8,'narrow'=16] {'narrow'}, dimensions={0} | all-to-all | bytes 524288 | tf_op jit(solution)/shard_map/all_to_all | solution.py:43
  38.4 0.3 fusion.41
  38.7 3.1 %collective-permute-start = (bf16[128,512]{1,0:T(8,128)(2,1)S(1)}, bf16[128,512]{1,0:T(8,128)(2,1)S(1)}, u32[]{:S(2)}, u32[]{:S(2)}) collective-permute-start(bf16[128,512]{1,0:T(8,128)(2,1)S(1)} %get-tuple-element.23), channel_id=1, source_target_pairs={{0,16},{16,0},{32,48},{48,32},{64,80},{80,64},{96,112},{112,96},{1... | collective-permute-start | bytes 393224 | tf_op jit(solution)/shard_map/ppermute | solution.py:30
  41.8 1.0 collective-permute-done
  42.9 1.7 %collective-permute-start.1 = (bf16[128,512]{1,0:T(8,128)(2,1)S(1)}, bf16[128,512]{1,0:T(8,128)(2,1)S(1)}, u32[]{:S(2)}, u32[]{:S(2)}) collective-permute-start(bf16[128,512]{1,0:T(8,128)(2,1)S(1)} %fusion.8), channel_id=1, source_target_pairs={{0,32},{16,48},{32,0},{48,16},{64,96},{80,112},{96,64},{112,80},{1... | collective-permute-start | bytes 393224 | tf_op jit(solution)/shard_map/ppermute | solution.py:30
  44.6 3.5 %collective-permute-done.1 = bf16[128,512]{1,0:T(8,128)(2,1)S(1)} collective-permute-done((bf16[128,512]{1,0:T(8,128)(2,1)S(1)}, bf16[128,512]{1,0:T(8,128)(2,1)S(1)}, u32[]{:S(2)}, u32[]{:S(2)}) %collective-permute-start.1) | collective-permute-done | bytes 131104 | tf_op jit(solution)/shard_map/ppermute | solution.py:30
  48.1 3.5 %collective-permute-start.2 = (bf16[128,512]{1,0:T(8,128)(2,1)S(1)}, bf16[128,512]{1,0:T(8,128)(2,1)S(1)}, u32[]{:S(2)}, u32[]{:S(2)}) collective-permute-start(bf16[128,512]{1,0:T(8,128)(2,1)S(1)} %fusion.12), channel_id=1, source_target_pairs={{0,96},{16,112},{32,64},{48,80},{64,32},{80,48},{96,0},{112,16},{1... | collective-permute-start | bytes 393224 | tf_op jit(solution)/shard_map/ppermute | solution.py:30
  51.6 2.4 %collective-permute-done.2 = bf16[128,512]{1,0:T(8,128)(2,1)S(1)} collective-permute-done((bf16[128,512]{1,0:T(8,128)(2,1)S(1)}, bf16[128,512]{1,0:T(8,128)(2,1)S(1)}, u32[]{:S(2)}, u32[]{:S(2)}) %collective-permute-start.2) | collective-permute-done | bytes 131104 | tf_op jit(solution)/shard_map/ppermute | solution.py:30
  54.1 0.7 convolution_convert_fusion
  54.8 0.7 convolution_convert_fusion.1
  55.7 26.9 %all_to_all.21 = bf16[16,8,7296]{2,1,0:T(8,128)(2,1)S(1)} all-to-all(bf16[16,8,7296]{2,1,0:T(8,128)(2,1)S(1)} %maximum_bitcast_fusion), channel_id=1, replica_groups=mesh['wide'=8,'narrow'=16] {'narrow'}, dimensions={0} | all-to-all | bytes 3735552 | tf_op jit(solution)/shard_map/all_to_all | solution.py:43
  82.6 0.3 convert_reduce_fusion
  83.3 14.9 %all_to_all.22 = bf16[16,8,3584]{2,1,0:T(8,128)(2,1)S(1)} all-to-all(bf16[16,8,3584]{2,1,0:T(8,128)(2,1)S(1)} %broadcast_in_dim.81), channel_id=1, replica_groups=mesh['wide'=8,'narrow'=16] {'narrow'}, dimensions={0} | all-to-all | bytes 1835008 | tf_op jit(solution)/shard_map/all_to_all | solution.py:43
  98.2 0.6 fusion.42
  98.8 4.7 %collective-permute-start.3 = (bf16[128,512]{1,0:T(8,128)(2,1)S(1)}, bf16[128,512]{1,0:T(8,128)(2,1)S(1)}, u32[]{:S(2)}, u32[]{:S(2)}) collective-permute-start(bf16[128,512]{1,0:T(8,128)(2,1)S(1)} %get-tuple-element.25), channel_id=1, source_target_pairs={{0,16},{16,0},{32,48},{48,32},{64,80},{80,64},{96,112},{112,96},{1... | collective-permute-start | bytes 393224 | tf_op jit(solution)/shard_map/ppermute | solution.py:30
  103.6 1.0 collective-permute-done.3
  104.7 4.7 %collective-permute-done.4 = bf16[128,512]{1,0:T(8,128)(2,1)S(1)} collective-permute-done((bf16[128,512]{1,0:T(8,128)(2,1)S(1)}, bf16[128,512]{1,0:T(8,128)(2,1)S(1)}, u32[]{:S(2)}, u32[]{:S(2)}) %collective-permute-start.4) | collective-permute-done | bytes 131104 | tf_op jit(solution)/shard_map/ppermute | solution.py:30
  109.4 2.1 %collective-permute-start.5 = (bf16[128,512]{1,0:T(8,128)(2,1)S(1)}, bf16[128,512]{1,0:T(8,128)(2,1)S(1)}, u32[]{:S(2)}, u32[]{:S(2)}) collective-permute-start(bf16[128,512]{1,0:T(8,128)(2,1)S(1)} %fusion.13), channel_id=1, source_target_pairs={{0,96},{16,112},{32,64},{48,80},{64,32},{80,48},{96,0},{112,16},{1... | collective-permute-start | bytes 393224 | tf_op jit(solution)/shard_map/ppermute | solution.py:30
  111.6 3.0 %collective-permute-done.5 = bf16[128,512]{1,0:T(8,128)(2,1)S(1)} collective-permute-done((bf16[128,512]{1,0:T(8,128)(2,1)S(1)}, bf16[128,512]{1,0:T(8,128)(2,1)S(1)}, u32[]{:S(2)}, u32[]{:S(2)}) %collective-permute-start.5) | collective-permute-done | bytes 131104 | tf_op jit(solution)/shard_map/ppermute | solution.py:30
  114.8 0.8 reshape.258
  (55 shorter events, 2.8 us)
Async XLA Ops:
  0.0 4.4 %copy-start = (bf16[512,1024]{1,0:T(8,128)(2,1)S(1)}, bf16[512,1024]{1,0:T(8,128)(2,1)}, u32[]{:S(2)}) copy-start(bf16[512,1024]{1,0:T(8,128)(2,1)} %param.15) | copy-start | bytes 3145732
  0.0 13.2 %copy-start.7 = (s32[2,4]{1,0:T(2,128)S(1)}, s32[2,4]{1,0:T(2,128)}, u32[]{:S(2)}) copy-start(s32[2,4]{1,0:T(2,128)} %param.25) | copy-start | bytes 100
  5.6 16.4 %all-to-all-start = ((bf16[16,8,1408]{2,1,0:T(8,128)(2,1)}), bf16[16,8,1408]{2,1,0:T(8,128)(2,1)S(1)}, u32[]{:S(2)}, u32[]{:S(2)}) async-start(bf16[16,8,1408]{2,1,0:T(8,128)(2,1)} %maximum_bitcast_fusion.1), calls=%async_computation | async-start | bytes 720896 | tf_op jit(solution)/shard_map/all_to_all | solution.py:43
  22.0 5.0 %copy-start.1 = (bf16[2,4,1,2048,128]{4,3,2,1,0:T(8,128)(2,1)S(1)}, bf16[2,4,1,2048,128]{4,3,2,1,0:T(8,128)(2,1)}, u32[]{:S(2)}) copy-start(bf16[2,4,1,2048,128]{4,3,2,1,0:T(8,128)(2,1)} %param.24) | copy-start | bytes 12582916
  26.8 11.6 %copy-start.5 = (bf16[1024,512]{1,0:T(8,128)(2,1)S(1)}, bf16[1024,512]{1,0:T(8,128)(2,1)}, u32[]{:S(2)}) copy-start(bf16[1024,512]{1,0:T(8,128)(2,1)} %param.18) | copy-start | bytes 3145732
  27.1 27.1 %copy-start.3 = (bf16[512,3584]{1,0:T(8,128)(2,1)S(1)}, bf16[512,3584]{1,0:T(8,128)(2,1)}, u32[]{:S(2)}) copy-start(bf16[512,3584]{1,0:T(8,128)(2,1)} %param.21) | copy-start | bytes 11010052
  27.1 27.1 %copy-start.6 = (f32[512]{0:T(512)S(1)}, f32[512]{0:T(512)}, u32[]{:S(2)}) copy-start(f32[512]{0:T(512)} %param.19) | copy-start | bytes 6148
  38.7 16.1 %copy-start.4 = (bf16[512,3584]{1,0:T(8,128)(2,1)S(1)}, bf16[512,3584]{1,0:T(8,128)(2,1)}, u32[]{:S(2)}) copy-start(bf16[512,3584]{1,0:T(8,128)(2,1)} %param.20) | copy-start | bytes 11010052
  38.7 4.1 %collective-permute-start = (bf16[128,512]{1,0:T(8,128)(2,1)S(1)}, bf16[128,512]{1,0:T(8,128)(2,1)S(1)}, u32[]{:S(2)}, u32[]{:S(2)}) collective-permute-start(bf16[128,512]{1,0:T(8,128)(2,1)S(1)} %get-tuple-element.23), channel_id=1, source_target_pairs={{0,16},{16,0},{32,48},{48,32},{64,80},{80,64},{96,112},{112,96},{1... | collective-permute-start | bytes 393224 | tf_op jit(solution)/shard_map/ppermute | solution.py:30
  42.9 5.2 %collective-permute-start.1 = (bf16[128,512]{1,0:T(8,128)(2,1)S(1)}, bf16[128,512]{1,0:T(8,128)(2,1)S(1)}, u32[]{:S(2)}, u32[]{:S(2)}) collective-permute-start(bf16[128,512]{1,0:T(8,128)(2,1)S(1)} %fusion.8), channel_id=1, source_target_pairs={{0,32},{16,48},{32,0},{48,16},{64,96},{80,112},{96,64},{112,80},{1... | collective-permute-start | bytes 393224 | tf_op jit(solution)/shard_map/ppermute | solution.py:30
  48.1 5.8 %collective-permute-start.2 = (bf16[128,512]{1,0:T(8,128)(2,1)S(1)}, bf16[128,512]{1,0:T(8,128)(2,1)S(1)}, u32[]{:S(2)}, u32[]{:S(2)}) collective-permute-start(bf16[128,512]{1,0:T(8,128)(2,1)S(1)} %fusion.12), channel_id=1, source_target_pairs={{0,96},{16,112},{32,64},{48,80},{64,32},{80,48},{96,0},{112,16},{1... | collective-permute-start | bytes 393224 | tf_op jit(solution)/shard_map/ppermute | solution.py:30
  55.7 42.5 %copy-start.2 = (bf16[3584,512]{1,0:T(8,128)(2,1)S(1)}, bf16[3584,512]{1,0:T(8,128)(2,1)}, u32[]{:S(2)}) copy-start(bf16[3584,512]{1,0:T(8,128)(2,1)} %param.22) | copy-start | bytes 11010052
  98.8 5.7 %collective-permute-start.3 = (bf16[128,512]{1,0:T(8,128)(2,1)S(1)}, bf16[128,512]{1,0:T(8,128)(2,1)S(1)}, u32[]{:S(2)}, u32[]{:S(2)}) collective-permute-start(bf16[128,512]{1,0:T(8,128)(2,1)S(1)} %get-tuple-element.25), channel_id=1, source_target_pairs={{0,16},{16,0},{32,48},{48,32},{64,80},{80,64},{96,112},{112,96},{1... | collective-permute-start | bytes 393224 | tf_op jit(solution)/shard_map/ppermute | solution.py:30
  104.6 4.8 %collective-permute-start.4 = (bf16[128,512]{1,0:T(8,128)(2,1)S(1)}, bf16[128,512]{1,0:T(8,128)(2,1)S(1)}, u32[]{:S(2)}, u32[]{:S(2)}) collective-permute-start(bf16[128,512]{1,0:T(8,128)(2,1)S(1)} %fusion.9), channel_id=1, source_target_pairs={{0,32},{16,48},{32,0},{48,16},{64,96},{80,112},{96,64},{112,80},{1... | collective-permute-start | bytes 393224 | tf_op jit(solution)/shard_map/ppermute | solution.py:30
  109.4 5.1 %collective-permute-start.5 = (bf16[128,512]{1,0:T(8,128)(2,1)S(1)}, bf16[128,512]{1,0:T(8,128)(2,1)S(1)}, u32[]{:S(2)}, u32[]{:S(2)}) collective-permute-start(bf16[128,512]{1,0:T(8,128)(2,1)S(1)} %fusion.13), channel_id=1, source_target_pairs={{0,96},{16,112},{32,64},{48,80},{64,32},{80,48},{96,0},{112,16},{1... | collective-permute-start | bytes 393224 | tf_op jit(solution)/shard_map/ppermute | solution.py:30

commit v2 on v1

v2 whole, which is shorter than its diff:
```python
import functools

import jax
import jax.numpy as jnp
from jax import lax
from jax.experimental import pallas as pl
from jax.experimental.pallas import tpu as pltpu
from jax.sharding import PartitionSpec as P

D = 8192
EPSILON = 1e-05
BF16 = jnp.bfloat16
F32 = jnp.float32
SIDE = 4
PARTS = SIDE * SIDE
HEAD = 128
LANES = 128
VMEM = pl.BlockSpec(memory_space=pltpu.VMEM)
HBM = pl.BlockSpec(memory_space=pltpu.HBM)
SMEM = pl.BlockSpec(memory_space=pltpu.SMEM)
KIB = 1 << 10
MIB = 1 << 20


def wide_pairs(target):
    pairs = []
    for z in range(SIDE):
        for c in range(2):
            to_z, to_c = target(z, c)
            pairs.append((z * 2 + c, to_z % SIDE * 2 + to_c))
    return pairs


CORE_SWAP = wide_pairs(lambda z, c: (z, 1 - c))
NEXT_Z = wide_pairs(lambda z, c: (z + 1 if c == 0 else z - 1, c))
FAR_Z = wide_pairs(lambda z, c: (z + 2, c))


def plane_pairs(step, stage):
    pairs = []
    for w in range(2 * SIDE):
        for y in range(SIDE):
            for x in range(SIDE):
                along_x = (w % 2 == 0) == (stage == 0)
                to_y, to_x = (y, (x + step) % SIDE) if along_x else ((y + step) % SIDE, x)
                pairs.append((w * PARTS + y * SIDE + x, w * PARTS + to_y * SIDE + to_x))
    return pairs


def call(kernel, outs, limit, *operands, scratch=(), scalars=0, far=0, held=0):
    near = len(operands) - far
    specs = [SMEM] * scalars + [VMEM] * (near - scalars) + [HBM] * far
    size = sum(o.size * o.dtype.itemsize for o in operands)
    places = [None] * (near - held) + [pltpu.VMEM] * held + [pltpu.HBM] * far
    operands = [
        o if place is None else pltpu.with_memory_space_constraint(o, place)
        for o, place in zip(operands, places)
    ]
    return pl.pallas_call(
        kernel,
        out_shape=[jax.ShapeDtypeStruct(shape, kind) for shape, kind in outs],
        in_specs=specs,
        out_specs=[VMEM] * len(outs),
        scratch_shapes=scratch,
        compiler_params=pltpu.CompilerParams(vmem_limit_bytes=limit),
        cost_estimate=pl.CostEstimate(flops=0, bytes_accessed=size, transcendentals=0),
    )(*operands)


def place_squares(squares):
    high = squares.astype(BF16).astype(F32)
    low = squares - high
    lane = lax.broadcasted_iota(jnp.int32, (squares.shape[0], LANES), 1)
    return jnp.where(lane == 0, high, jnp.where(lane == 1, low, 0.0))


def project_kernel(
    len_ref, blocks_ref, core_ref, cos_ref, sin_ref, x_hbm, gain_hbm, wq_hbm, wk_hbm, wv_hbm, out_ref, stream_ref, x_ref, gain_ref, wq_ref, wk_ref,
    wv_ref, sems,
):
    pairs = ((x_hbm, x_ref), (gain_hbm, gain_ref), (wq_hbm, wq_ref), (wk_hbm, wk_ref), (wv_hbm, wv_ref))
    copies = [pltpu.make_async_copy(a, b, sems.at[i]) for i, (a, b) in enumerate(pairs)]
    for copy in copies:
        copy.start()
    copies[0].wait()
    copies[1].wait()
    rows = x_ref.shape[1] // PARTS
    for n in range(PARTS):
        for m in range(2):
            stream_ref[pl.ds((n * 2 + m) * rows, rows), :] = x_ref[m, pl.ds(n * rows, rows), :]
    stream = stream_ref[...]
    squares = jnp.sum(stream * stream, axis=-1, keepdims=True)
    normed = (stream * gain_ref[...]).astype(BF16)
    at = 0
    for copy, w_ref, exact in zip(copies[2:], (wq_ref, wk_ref, wv_ref), (True, True, False)):
        copy.wait()
        width = w_ref.shape[1]
        product = jnp.dot(normed, w_ref[...], preferred_element_type=F32)
        high = product.astype(BF16)
        out_ref[:, pl.ds(at, width)] = high
        at += width
        if exact:
            out_ref[:, pl.ds(at, width)] = (product - high.astype(F32)).astype(BF16)
            at += width
    out_ref[:, pl.ds(at, LANES)] = place_squares(squares).astype(out_ref.dtype)


def total_kernel(core_ref, mine_ref, other_ref, total_ref, half_ref):
    total = (mine_ref[...] + other_ref[...]).astype(BF16)
    total_ref[...] = total
    half = half_ref.shape[0]
    half_ref[...] = jnp.where(core_ref[0] == 0, total[:half, :], total[half:, :])


def pack_kernel(near_ref, far_ref, out_ref):
    rows = near_ref.shape[0]
    out_ref[pl.ds(0, rows), :] = near_ref[...]
    out_ref[pl.ds(rows, far_ref.shape[0]), :] = far_ref[...]


def attend_kernel(
    len_ref, got_ref, cos_ref, sin_ref, keys_hbm, values_hbm, out_ref, q_s, a_s, s_s, keys_s, values_s,
    key_sems, value_sems,
):
    here = got_ref.shape[1]
    cache = keys_s.shape[1]
    chunk = 512
    counts = [(len_ref[r] + chunk - 1) // chunk for r in range(here)]

    def fetch(far, near, sems, r, j):
        part = pl.ds(pl.multiple_of(j * chunk, chunk), chunk)
        return pltpu.make_async_copy(far.at[r, part], near.at[r, part], sems.at[r, j])

    def start(far, near, sems, r):
        @pl.loop(0, counts[r])
        def _(j):
            fetch(far, near, sems, r, j).start()

    def finish(far, near, sems, r):
        @pl.loop(0, counts[r])
        def _(j):
            fetch(far, near, sems, r, j).wait()

    for r in range(here):
        start(keys_hbm, keys_s, key_sems, r)
    for r in range(here):
        start(values_hbm, values_s, value_sems, r)
    for r in range(here):

        @pl.loop(counts[r], cache // chunk)
        def _(j):
            part = pl.ds(pl.multiple_of(j * chunk, chunk), chunk)
            values_s[r, part, :] = jnp.zeros((chunk, HEAD), BF16)

    total = got_ref[0].astype(F32)
    for n in range(1, PARTS):
        total = total + got_ref[n].astype(F32)
    heads = out_ref.shape[2] // HEAD
    split = heads * HEAD
    query = total[:, :split] + total[:, split : 2 * split]
    total = total[:, 2 * split :]
    squares = jnp.sum(total[:, 3 * HEAD :], axis=-1, keepdims=True)
    factor = lax.rsqrt(squares / D + EPSILON)
    cos, sin = cos_ref[...], sin_ref[...]

    def turned(part):
        part = part * factor
        return (part * cos + pltpu.roll(part, HEAD // 2, 1) * sin).astype(BF16).astype(F32)

    key_new = turned(total[:, :HEAD] + total[:, HEAD : 2 * HEAD])
    value_new = (total[:, 2 * HEAD : 3 * HEAD] * factor).astype(BF16).astype(F32)
    for h in range(heads):
        q_s[:, h, :] = turned(query[:, h * HEAD : (h + 1) * HEAD])
    scaling = HEAD ** (-0.5)
    position = lax.broadcasted_iota(jnp.int32, (1, cache), 1)
    for r in range(here):
        finish(keys_hbm, keys_s, key_sems, r)
    own = []
    for r in range(here):
        queries = q_s[r]
        scores = lax.dot_general(
            queries.astype(BF16),
            keys_s[r],
            (((1,), (1,)), ((), ())),
            preferred_element_type=F32,
        )
        s_s[pl.ds(r * heads, heads), :] = jnp.where(
            position < len_ref[r], scores * scaling, -jnp.inf
        )
        own.append(jnp.sum(queries * key_new[r : r + 1, :], axis=-1, keepdims=True) * scaling)
    weights, own_weights = [], []
    for r in range(here):
        scores = s_s[pl.ds(r * heads, heads), :]
        highest = jnp.maximum(jnp.max(scores, axis=-1, keepdims=True), own[r])
        shifted = jnp.exp(scores - highest)
        own_term = jnp.exp(own[r] - highest)
        totals = jnp.sum(shifted, axis=-1, keepdims=True) + own_term
        weights.append((shifted / totals).astype(BF16))
        own_weights.append((own_term / totals).astype(BF16).astype(F32))
    for r in range(here):
        finish(values_hbm, values_s, value_sems, r)
    for r in range(here):
        attended = jnp.dot(weights[r], values_s[r], preferred_element_type=F32)
        a_s[r] = attended + own_weights[r] * value_new[r : r + 1, :]
    for h in range(heads):
        part = a_s[:, h, :].astype(BF16)
        for n in range(PARTS):
            out_ref[n, :, pl.ds(h * HEAD, HEAD)] = part


def wide_total(refs):
    core_ref, mine_ref, near_ref, far_ref, other_ref = refs
    half = far_ref.shape[0]
    rows = mine_ref.shape[0]
    first = core_ref[0] == 0
    far, far_other = far_ref[...].astype(F32), other_ref[pl.ds(rows, half), :].astype(F32)
    opposite = jnp.concatenate(
        [jnp.where(first, far, far_other), jnp.where(first, far_other, far)], axis=0
    )
    sides = near_ref[...].astype(F32) + other_ref[pl.ds(0, rows), :].astype(F32)
    return (mine_ref[...].astype(F32) + opposite) + sides


def gate_kernel(
    core_ref, blocks_ref, mine_ref, near_ref, far_ref, other_ref, stream_ref, gain_ref, wg_ref,
    wu_ref, middle_ref, out0_ref, out1_ref, out2_ref, out3_ref, sorted_s, normed_s,
):
    middle_ref[...] = stream_ref[...] + wide_total(
        (core_ref, mine_ref, near_ref, far_ref, other_ref)
    )
    rows = middle_ref.shape[0] // PARTS
    for i in range(PARTS):
        start = pl.multiple_of(blocks_ref[i] * rows, rows)
        sorted_s[pl.ds(i * rows, rows), :] = middle_ref[pl.ds(start, rows), :]
    middle = sorted_s[...]
    squares = place_squares(jnp.sum(middle * middle, axis=-1, keepdims=True))
    normed_s[...] = (middle * gain_ref[...]).astype(BF16)
    outs = (out0_ref, out1_ref, out2_ref, out3_ref)
    units = wg_ref.shape[1]
    group = middle.shape[0] // SIDE
    tile = 512
    normed = normed_s[...]
    for at, w_ref in ((0, wg_ref), (units, wu_ref)):
        for j in range(0, units, tile):
            product = jnp.dot(normed, w_ref[:, pl.ds(j, tile)], preferred_element_type=F32)
            for d in range(SIDE):
                part = product[d * group : (d + 1) * group, :]
                outs[d][:, pl.ds(at + j, tile)] = part.astype(outs[d].dtype)
    for d in range(SIDE):
        part = squares[d * group : (d + 1) * group, :]
        outs[d][:, pl.ds(2 * units, LANES)] = part.astype(outs[d].dtype)


def middle_sum_kernel(a_ref, b_ref, c_ref, d_ref, own_ref, out1_ref, out2_ref, out3_ref):
    width = a_ref.shape[1]
    last = width - LANES
    tile = 1024
    rows = a_ref.shape[0] // SIDE

    def total(at, size):
        parts = [ref[:, pl.ds(at, size)].astype(F32) for ref in (a_ref, b_ref, c_ref, d_ref)]
        return (parts[0] + parts[1]) + (parts[2] + parts[3])

    outs = (own_ref, out1_ref, out2_ref, out3_ref)

    def put(at, size, value):
        for k in range(SIDE):
            outs[k][:, pl.ds(at, size)] = value[k * rows : (k + 1) * rows, :].astype(outs[k].dtype)

    for at in range(0, last, tile):
        put(at, tile, total(at, tile))
    put(last, LANES, place_squares(jnp.sum(total(last, LANES), axis=-1, keepdims=True)))


def hidden_kernel(a_ref, b_ref, c_ref, d_ref, out_ref):
    units = out_ref.shape[2]
    tile = 512

    def total(at, size):
        parts = [ref[:, pl.ds(at, size)].astype(F32) for ref in (a_ref, b_ref, c_ref, d_ref)]
        return (parts[0] + parts[1]) + (parts[2] + parts[3])

    squares = jnp.sum(total(2 * units, LANES), axis=-1, keepdims=True)
    factor = lax.rsqrt(squares / D + EPSILON)
    for at in range(0, units, tile):
        gate = total(at, tile) * factor
        up = total(units + at, tile) * factor
        hidden = (gate / (1.0 + jnp.exp(-gate)) * up).astype(BF16)
        for n in range(PARTS):
            out_ref[n, :, pl.ds(at, tile)] = hidden


def finish_kernel(core_ref, mine_ref, near_ref, far_ref, other_ref, middle_ref, out_ref):
    result = middle_ref[...] + wide_total((core_ref, mine_ref, near_ref, far_ref, other_ref))
    rows = out_ref.shape[1] // PARTS
    for n in range(PARTS):
        for m in range(2):
            at = (n * 2 + m) * rows
            out_ref[m, pl.ds(n * rows, rows), :] = result[at : at + rows, :]


def exchange(payload):
    return lax.all_to_all(payload, "narrow", 0, 0, tiled=True)


def sum_wide_parts(partial, core_flag):
    rows, width = partial.shape
    half = rows // 2
    mine, part = call(
        total_kernel,
        [((rows, width), BF16), ((half, width), BF16)],
        4 * MIB,
        core_flag,
        partial,
        lax.ppermute(partial, "wide", CORE_SWAP),
        scalars=1,
    )
    near = lax.ppermute(mine, "wide", NEXT_Z)
    far = lax.ppermute(part, "wide", FAR_Z)
    (both,) = call(pack_kernel, [((rows + half, width), BF16)], 4 * MIB, near, far)
    other = lax.ppermute(both, "wide", CORE_SWAP)
    return mine, near, far, other


def body(
    hidden_in,
    attn_gain,
    w_query,
    w_key,
    w_value,
    w_out,
    ffn_gain,
    w_gate,
    w_up,
    w_down,
    key_cache,
    value_cache,
    cache_len,
):
    micro, _, width = hidden_in.shape
    rows = key_cache.shape[1]
    here = micro * rows
    every = here * PARTS
    split = w_query.shape[1]
    units = w_gate.shape[1]
    core = lax.axis_index("wide") % 2
    at_y, at_x = lax.axis_index("narrow") // SIDE, lax.axis_index("narrow") % SIDE
    first, second = jnp.arange(PARTS) // SIDE, jnp.arange(PARTS) % SIDE
    step_y = jnp.where(core == 0, second, first)
    step_x = jnp.where(core == 0, first, second)
    blocks = ((at_y + step_y) % SIDE * SIDE + (at_x + step_x) % SIDE).astype(jnp.int32)
    core_flag = core.astype(jnp.int32)[None]

    lengths = cache_len.reshape(here)
    half = HEAD // 2
    base = 500000.0 ** (-jnp.arange(half, dtype=F32) * 2.0 / HEAD)
    angles = lengths.astype(F32)[:, None] * base[None]
    cosines, sines = jnp.cos(angles), jnp.sin(angles)
    cosines = jnp.concatenate([cosines, cosines], axis=-1)
    sines = jnp.concatenate([-sines, sines], axis=-1)

    payload, stream = call(
        project_kernel,
        [((every, 2 * split + 4 * HEAD), BF16), ((every, width), F32)],
        8 * MIB,
        lengths,
        blocks,
        core_flag,
        cosines,
        sines,
        hidden_in,
        attn_gain[None],
        w_query,
        w_key,
        w_value,
        scalars=3,
        far=5,
        scratch=[pltpu.VMEM(hidden_in.shape, F32), pltpu.VMEM((1, width), F32)]
        + [pltpu.VMEM(w.shape, BF16) for w in (w_query, w_key, w_value)]
        + [pltpu.SemaphoreType.DMA((5,))],
    )
    got = exchange(payload.reshape(PARTS, here, -1))

    (attended,) = call(
        attend_kernel,
        [((PARTS, here, split), BF16)],
        16 * MIB,
        lengths,
        got,
        cosines,
        sines,
        key_cache.reshape(here, -1, HEAD),
        value_cache.reshape(here, -1, HEAD),
        scalars=1,
        far=2,
        scratch=[pltpu.VMEM((here, split // HEAD, HEAD), F32)] * 2
        + [pltpu.VMEM((here * split // HEAD, key_cache.shape[3]), F32)]
        + [pltpu.VMEM((here, key_cache.shape[3], HEAD), BF16)] * 2
        + [pltpu.SemaphoreType.DMA((here, key_cache.shape[3] // 512))] * 2,
    )
    gathered = exchange(attended).reshape(every, split)
    parts = sum_wide_parts(jnp.dot(gathered, w_out, preferred_element_type=F32), core_flag)
    group = every // SIDE
    full = 2 * units + LANES
    middle, own, *sends = call(
        gate_kernel,
        [((every, width), F32), ((group, full), F32)] + [((group, full), BF16)] * (SIDE - 1),
        8 * MIB,
        core_flag,
        blocks,
        *parts,
        stream,
        ffn_gain[None],
        w_gate,
        w_up,
        scalars=2,
        held=2,
        scratch=[pltpu.VMEM((every, width), F32), pltpu.VMEM((every, width), BF16)],
    )
    axes = ("wide", "narrow")
    taken = {}
    for step in (1, 3, 2):
        taken[step] = lax.ppermute(sends[step - 1], axes, plane_pairs(step, 0))
    own, *sends = call(
        middle_sum_kernel,
        [((here, full), F32)] + [((here, full), BF16)] * (SIDE - 1),
        8 * MIB,
        own,
        taken[1],
        taken[2],
        taken[3],
    )
    for step in (1, 3, 2):
        taken[step] = lax.ppermute(sends[step - 1], axes, plane_pairs(step, 1))
    (hidden,) = call(
        hidden_kernel, [((PARTS, here, units), BF16)], 8 * MIB, own, taken[1], taken[2], taken[3]
    )
    gathered = exchange(hidden).reshape(every, units)
    parts = sum_wide_parts(jnp.dot(gathered, w_down, preferred_element_type=F32), core_flag)
    (result,) = call(
        finish_kernel, [(hidden_in.shape, F32)], 8 * MIB, core_flag, *parts, middle, scalars=1
    )
    return result


def solution(mesh):
    return jax.shard_map(
        body,
        mesh=mesh,
        in_specs=(
            P(None, None, "narrow"),
            P("narrow"),
            P("narrow", "wide"),
            P("narrow", "wide"),
            P("narrow", "wide"),
            P("wide", "narrow"),
            P("narrow"),
            P("narrow", "wide"),
            P("narrow", "wide"),
            P("wide", "narrow"),
            P(None, "narrow", "wide", None, None),
            P(None, "narrow", "wide", None, None),
            P(None, "narrow"),
        ),
        out_specs=P(None, None, "narrow"),
        check_vma=False,
    )
```

time: 117 us -> 113 us (0.966)
  Pallas kernels: 0 us -> 10.8 us
  matrix products: 9.35 us -> 0.95 us
  waiting for transfers between devices: 24 us -> 30.9 us
  blocking collectives: 52.3 us -> 46.9 us
  other arithmetic: 4.29 us -> 0.22 us
  local copies, waits for them, and re-layouts: 2.45 us -> 0.87 us
  starting transfers between devices: 22.8 us -> 21.6 us
    ppermute x6 -> x14, waiting for transfers between devices: 15.5 us -> 30.9 us  [the longest x3 11.9 us: body(): taken[step] = lax.ppermute(sends[step - 1], axes, plane_pairs(step, 0))]
    pallas_call x0 -> x10, Pallas kernels: none -> 10.8 us  [call(): pl.pallas_call(kernel, out_shape=[jax.ShapeDtypeStruct(shape, kind) for s...]
    all_to_all x1 -> x0, waiting for transfers between devices: 8.51 us -> none  [exchange(): return lax.all_to_all(payload, 'narrow', 0, 0, tiled=True)]
    dot_general x9 -> x2, matrix products: 9.35 us -> 0.95 us  [the longest x1 0.64 us: body(): jnp.dot(gathered, w_down, preferred_element_type=F32)]
    all_to_all x1 -> x0, starting transfers between devices: 7.58 us -> none  [exchange(): return lax.all_to_all(payload, 'narrow', 0, 0, tiled=True)]
    ppermute x6 -> x14, starting transfers between devices: 15.2 us -> 21.6 us  [the longest x2 7.98 us: sum_wide_parts(): lax.ppermute(partial, 'wide', CORE_SWAP)]
    all_to_all x3, blocking collectives: 52.3 us -> 46.9 us  [exchange(): return lax.all_to_all(payload, 'narrow', 0, 0, tiled=True)]
    convert_element_type x11 -> x1, other arithmetic: 1.37 us -> 0.01 us  [body(): angles = lengths.astype(F32)[:, None] * base[None]]
  transfers between devices with their start and end apart: 7 -> 14, of which waited for: 7 -> 10; matrix products, arithmetic and copies ran while one was open for 0% -> 0% of each run, Pallas kernels for 0% -> 0%
where the time goes in v2:
time: 113 us; the launch traced here: 112 us
  blocking collectives  46.9 us (42%)
  waiting for transfers between devices  30.9 us (27%)
  starting transfers between devices  21.6 us (19%)
  Pallas kernels  10.8 us (10%)
    all_to_all x3, blocking collectives, exchange(): return lax.all_to_all(payload, 'narrow', 0, 0, tiled=True)  46.9 us
    ppermute x3, waiting for transfers between devices, body(): taken[step] = lax.ppermute(sends[step - 1], axes, plane_pairs(step, 0))  11.9 us
    pallas_call x10, Pallas kernels, call(): pl.pallas_call(kernel, out_shape=[jax.ShapeDtypeStruct(shape, kind) for s...  10.8 us
    ppermute x2, waiting for transfers between devices, sum_wide_parts(): far = lax.ppermute(part, 'wide', FAR_Z)  10.3 us
    ppermute x2, starting transfers between devices, sum_wide_parts(): lax.ppermute(partial, 'wide', CORE_SWAP)  7.98 us
    ppermute x3, waiting for transfers between devices, body(): taken[step] = lax.ppermute(sends[step - 1], axes, plane_pairs(step, 1))  4.28 us
    ppermute x2, starting transfers between devices, sum_wide_parts(): near = lax.ppermute(mine, 'wide', NEXT_Z)  4.23 us
    ppermute x2, starting transfers between devices, sum_wide_parts(): other = lax.ppermute(both, 'wide', CORE_SWAP)  2.93 us
  transfers between devices with their start and end apart: 14, of which 10 were waited for; matrix products, arithmetic and copies ran while one was open for 0% of the time, Pallas kernels for 0%

profile of v2, /device:TPU:1, one launch (start us, length us, event | category | flops | bytes accessed | tf_op | source)
XLA Modules:
  0.0 112.3 jit_solution(1894007388288785248)
XLA Ops:
  0.0 0.8 reshape.29.len_ref
  1.1 2.6 %shard_map.127 = (bf16[128,2560]{1,0:T(8,128)(2,1)S(1)}, f32[128,512]{1,0:T(8,128)S(1)}) custom-call(s32[8]{0:T(128)S(1)} %reshape.29.len_ref, s32[16]{0:T(128)S(1)} %fusion.5.blocks_ref, s32[1]{0:T(128)} %bitcast.core_ref, f32[8,128]{1,0:T(8,128)S(1)} %get-tuple-element.38.cos_ref, f32[8,128]{1,0:T(8,128)S(1)} %get-tuple-element.39.sin_ref, ...), custom_call_target="tpu_custom_call" | custom-call | bytes 1583204 | tf_op jit(solution)/shard_map/pallas_call | solution.py:59
  3.7 19.2 %all_to_all.15.got_ref = bf16[16,8,2560]{2,1,0:T(8,128)(2,1)S(1)} all-to-all(bf16[16,8,2560]{2,1,0:T(8,128)(2,1)S(1)} %bitcast.14), channel_id=1, replica_groups=mesh['wide'=8,'narrow'=16] {'narrow'}, dimensions={0} | all-to-all | bytes 1310720 | tf_op jit(solution)/shard_map/all_to_all | solution.py:303
  22.9 5.0 %shard_map.128 = bf16[16,8,1024]{2,1,0:T(8,128)(2,1)S(1)} custom-call(s32[8]{0:T(128)S(1)} %reshape.29.len_ref, bf16[16,8,2560]{2,1,0:T(8,128)(2,1)S(1)} %all_to_all.15.got_ref, f32[8,128]{1,0:T(8,128)S(1)} %get-tuple-element.38.cos_ref, f32[8,128]{1,0:T(8,128)S(1)} %get-tuple-element.39.sin_ref, bf16[8,2048,128]{2,1,0:T(8,128)(2,1)} %bitcast.16, ...), custom_call_target="tpu_custom_call" | custom-call | bytes 9052192 | tf_op jit(solution)/shard_map/pallas_call | solution.py:59
  27.9 10.7 %all_to_all.16 = bf16[16,8,1024]{2,1,0:T(8,128)(2,1)S(1)} all-to-all(bf16[16,8,1024]{2,1,0:T(8,128)(2,1)S(1)} %shard_map.128), channel_id=1, replica_groups=mesh['wide'=8,'narrow'=16] {'narrow'}, dimensions={0} | all-to-all | bytes 524288 | tf_op jit(solution)/shard_map/all_to_all | solution.py:303
  38.6 0.3 fusion.2.mine_ref
  38.9 3.4 %collective-permute-start = (f32[128,512]{1,0:T(8,128)S(1)}, f32[128,512]{1,0:T(8,128)S(1)}, u32[]{:S(2)}, u32[]{:S(2)}) collective-permute-start(f32[128,512]{1,0:T(8,128)S(1)} %fusion.2.mine_ref), channel_id=1, source_target_pairs={{0,16},{16,0},{32,48},{48,32},{64,80},{80,64},{96,112},{112,96},{1... | collective-permute-start | bytes 786440 | tf_op jit(solution)/shard_map/ppermute | solution.py:315
  42.3 1.2 %collective-permute-done.other_ref = f32[128,512]{1,0:T(8,128)S(1)} collective-permute-done((f32[128,512]{1,0:T(8,128)S(1)}, f32[128,512]{1,0:T(8,128)S(1)}, u32[]{:S(2)}, u32[]{:S(2)}) %collective-permute-start) | collective-permute-done | bytes 262176 | tf_op jit(solution)/shard_map/ppermute | solution.py:315
  43.5 3.8 %collective-permute-start.1 = (bf16[128,512]{1,0:T(8,128)(2,1)S(1)}, bf16[128,512]{1,0:T(8,128)(2,1)S(1)}, u32[]{:S(2)}, u32[]{:S(2)}) collective-permute-start(bf16[128,512]{1,0:T(8,128)(2,1)S(1)} %get-tuple-element.21.mine_ref), channel_id=1, source_target_pairs={{0,32},{16,112},{32,64},{48,16},{64,96},{80,48},{96,0},{112,80},{1... | collective-permute-start | bytes 393224 | tf_op jit(solution)/shard_map/ppermute | solution.py:318
  47.4 5.6 %collective-permute-done.2.far_ref = bf16[64,512]{1,0:T(8,128)(2,1)S(1)} collective-permute-done((bf16[64,512]{1,0:T(8,128)(2,1)S(1)}, bf16[64,512]{1,0:T(8,128)(2,1)S(1)}, u32[]{:S(2)}, u32[]{:S(2)}) %collective-permute-start.2) | collective-permute-done | bytes 65568 | tf_op jit(solution)/shard_map/ppermute | solution.py:319
  53.0 0.9 collective-permute-start.3
  53.9 1.1 collective-permute-done.3.other_ref
  55.0 1.8 %shard_map.131 = (f32[128,512]{1,0:T(8,128)S(1)}, f32[32,7296]{1,0:T(8,128)S(1)}, bf16[32,7296]{1,0:T(8,128)(2,1)S(1)}, bf16[32,7296]{1,0:T(8,128)(2,1)S(1)}, bf16[32,7296]{1,0:T(8,128)(2,1)S(1)}) custom-call(s32[1]{0:T(128)} %bitcast.core_ref, s32[16]{0:T(128)S(1)} %fusion.5.blocks_ref, bf16[128,512]{1,0:T(8,128)(2,1)S(1)} %get-tuple-element.21.mine_ref, ...), custom_call_target="tpu_custom_call" | custom-call | bytes 8128580 | tf_op jit(solution)/shard_map/pallas_call | solution.py:59
  56.9 1.7 %collective-permute-start.5 = (bf16[32,7296]{1,0:T(8,128)(2,1)S(1)}, bf16[32,7296]{1,0:T(8,128)(2,1)S(1)}, u32[]{:S(2)}, u32[]{:S(2)}) collective-permute-start(bf16[32,7296]{1,0:T(8,128)(2,1)S(1)} %get-tuple-element.26), channel_id=1, source_target_pairs={{0,2},{1,3},{2,0},{3,1},{4,6},{5,7},{6,4},{7,5},{8,10},{9,11},{10,... | collective-permute-start | bytes 1400840 | tf_op jit(solution)/shard_map/ppermute | solution.py:423
  58.6 0.9 collective-permute-start.6
  59.6 11.2 %collective-permute-done.4.b_ref = bf16[32,7296]{1,0:T(8,128)(2,1)S(1)} collective-permute-done((bf16[32,7296]{1,0:T(8,128)(2,1)S(1)}, bf16[32,7296]{1,0:T(8,128)(2,1)S(1)}, u32[]{:S(2)}, u32[]{:S(2)}) %collective-permute-start.4) | collective-permute-done | bytes 466976 | tf_op jit(solution)/shard_map/ppermute | solution.py:423
  70.8 0.6 collective-permute-done.6.d_ref
  71.7 0.3 collective-permute-start.7
  72.1 1.4 %collective-permute-start.8 = (bf16[8,7296]{1,0:T(8,128)(2,1)S(1)}, bf16[8,7296]{1,0:T(8,128)(2,1)S(1)}, u32[]{:S(2)}, u32[]{:S(2)}) collective-permute-start(bf16[8,7296]{1,0:T(8,128)(2,1)S(1)} %get-tuple-element.30), channel_id=1, source_target_pairs={{0,8},{1,9},{2,10},{3,11},{4,12},{5,13},{6,14},{7,15},{8,0},{9,1},... | collective-permute-start | bytes 350216 | tf_op jit(solution)/shard_map/ppermute | solution.py:434
  73.4 1.1 collective-permute-start.9
  74.5 3.7 %collective-permute-done.7.b_ref = bf16[8,7296]{1,0:T(8,128)(2,1)S(1)} collective-permute-done((bf16[8,7296]{1,0:T(8,128)(2,1)S(1)}, bf16[8,7296]{1,0:T(8,128)(2,1)S(1)}, u32[]{:S(2)}, u32[]{:S(2)}) %collective-permute-start.7) | collective-permute-done | bytes 116768 | tf_op jit(solution)/shard_map/ppermute | solution.py:434
  78.2 0.6 collective-permute-done.9.d_ref
  79.0 17.0 %all_to_all.17 = bf16[16,8,3584]{2,1,0:T(8,128)(2,1)S(1)} all-to-all(bf16[16,8,3584]{2,1,0:T(8,128)(2,1)S(1)} %shard_map.133), channel_id=1, replica_groups=mesh['wide'=8,'narrow'=16] {'narrow'}, dimensions={0} | all-to-all | bytes 1835008 | tf_op jit(solution)/shard_map/all_to_all | solution.py:303
  96.0 0.6 fusion.mine_ref
  96.6 4.6 %collective-permute-start.10 = (f32[128,512]{1,0:T(8,128)S(1)}, f32[128,512]{1,0:T(8,128)S(1)}, u32[]{:S(2)}, u32[]{:S(2)}) collective-permute-start(f32[128,512]{1,0:T(8,128)S(1)} %fusion.mine_ref), channel_id=1, source_target_pairs={{0,16},{16,0},{32,48},{48,32},{64,80},{80,64},{96,112},{112,96},{1... | collective-permute-start | bytes 786440 | tf_op jit(solution)/shard_map/ppermute | solution.py:315
  101.2 1.2 %collective-permute-done.10.other_ref = f32[128,512]{1,0:T(8,128)S(1)} collective-permute-done((f32[128,512]{1,0:T(8,128)S(1)}, f32[128,512]{1,0:T(8,128)S(1)}, u32[]{:S(2)}, u32[]{:S(2)}) %collective-permute-start.10) | collective-permute-done | bytes 262176 | tf_op jit(solution)/shard_map/ppermute | solution.py:315
  102.4 0.4 collective-permute-start.11
  102.8 0.9 collective-permute-start.12
  103.8 4.7 %collective-permute-done.12.far_ref = bf16[64,512]{1,0:T(8,128)(2,1)S(1)} collective-permute-done((bf16[64,512]{1,0:T(8,128)(2,1)S(1)}, bf16[64,512]{1,0:T(8,128)(2,1)S(1)}, u32[]{:S(2)}, u32[]{:S(2)}) %collective-permute-start.12) | collective-permute-done | bytes 65568 | tf_op jit(solution)/shard_map/ppermute | solution.py:319
  108.5 2.0 %collective-permute-start.13 = (bf16[192,512]{1,0:T(8,128)(2,1)S(1)}, bf16[192,512]{1,0:T(8,128)(2,1)S(1)}, u32[]{:S(2)}, u32[]{:S(2)}) collective-permute-start(bf16[192,512]{1,0:T(8,128)(2,1)S(1)} %shard_map.135), channel_id=1, source_target_pairs={{0,16},{16,0},{32,48},{48,32},{64,80},{80,64},{96,112},{112,96},{1... | collective-permute-start | bytes 589832 | tf_op jit(solution)/shard_map/ppermute | solution.py:321
  110.5 1.1 collective-permute-done.13.other_ref
  111.5 0.8 shard_map.136
  (27 shorter events, 0.9 us)
Async XLA Ops:
  0.0 38.6 %copy-start = (bf16[1024,512]{1,0:T(8,128)(2,1)S(1)}, bf16[1024,512]{1,0:T(8,128)(2,1)}, u32[]{:S(2)}) copy-start(bf16[1024,512]{1,0:T(8,128)(2,1)} %param.18) | copy-start | bytes 3145732
  22.9 32.1 %copy-start.1 = (bf16[512,3584]{1,0:T(8,128)(2,1)S(1)}, bf16[512,3584]{1,0:T(8,128)(2,1)}, u32[]{:S(2)}) copy-start(bf16[512,3584]{1,0:T(8,128)(2,1)} %wg_ref.1) | copy-start | bytes 11010052
  22.9 32.1 %copy-start.2 = (bf16[512,3584]{1,0:T(8,128)(2,1)S(1)}, bf16[512,3584]{1,0:T(8,128)(2,1)}, u32[]{:S(2)}) copy-start(bf16[512,3584]{1,0:T(8,128)(2,1)} %wu_ref.1) | copy-start | bytes 11010052
  22.9 32.1 %copy-start.3 = (f32[512]{0:T(512)S(1)}, f32[512]{0:T(512)}, u32[]{:S(2)}) copy-start(f32[512]{0:T(512)} %param.19) | copy-start | bytes 6148
  38.9 4.5 %collective-permute-start = (f32[128,512]{1,0:T(8,128)S(1)}, f32[128,512]{1,0:T(8,128)S(1)}, u32[]{:S(2)}, u32[]{:S(2)}) collective-permute-start(f32[128,512]{1,0:T(8,128)S(1)} %fusion.2.mine_ref), channel_id=1, source_target_pairs={{0,16},{16,0},{32,48},{48,32},{64,80},{80,64},{96,112},{112,96},{1... | collective-permute-start | bytes 786440 | tf_op jit(solution)/shard_map/ppermute | solution.py:315
  43.5 9.4 %collective-permute-start.1 = (bf16[128,512]{1,0:T(8,128)(2,1)S(1)}, bf16[128,512]{1,0:T(8,128)(2,1)S(1)}, u32[]{:S(2)}, u32[]{:S(2)}) collective-permute-start(bf16[128,512]{1,0:T(8,128)(2,1)S(1)} %get-tuple-element.21.mine_ref), channel_id=1, source_target_pairs={{0,32},{16,112},{32,64},{48,16},{64,96},{80,48},{96,0},{112,80},{1... | collective-permute-start | bytes 393224 | tf_op jit(solution)/shard_map/ppermute | solution.py:318
  47.4 5.6 %collective-permute-start.2 = (bf16[64,512]{1,0:T(8,128)(2,1)S(1)}, bf16[64,512]{1,0:T(8,128)(2,1)S(1)}, u32[]{:S(2)}, u32[]{:S(2)}) collective-permute-start(bf16[64,512]{1,0:T(8,128)(2,1)S(1)} %get-tuple-element.22), channel_id=1, source_target_pairs={{0,64},{16,80},{32,96},{48,112},{64,0},{80,16},{96,32},{112,48},{1... | collective-permute-start | bytes 196616 | tf_op jit(solution)/shard_map/ppermute | solution.py:319
  53.0 2.0 %collective-permute-start.3 = (bf16[192,512]{1,0:T(8,128)(2,1)S(1)}, bf16[192,512]{1,0:T(8,128)(2,1)S(1)}, u32[]{:S(2)}, u32[]{:S(2)}) collective-permute-start(bf16[192,512]{1,0:T(8,128)(2,1)S(1)} %shard_map.130), channel_id=1, source_target_pairs={{0,16},{16,0},{32,48},{48,32},{64,80},{80,64},{96,112},{112,96},{1... | collective-permute-start | bytes 589832 | tf_op jit(solution)/shard_map/ppermute | solution.py:321
  56.8 39.2 %copy-start.4 = (bf16[3584,512]{1,0:T(8,128)(2,1)S(1)}, bf16[3584,512]{1,0:T(8,128)(2,1)}, u32[]{:S(2)}) copy-start(bf16[3584,512]{1,0:T(8,128)(2,1)} %param.22) | copy-start | bytes 11010052
  56.8 14.0 %collective-permute-start.4 = (bf16[32,7296]{1,0:T(8,128)(2,1)S(1)}, bf16[32,7296]{1,0:T(8,128)(2,1)S(1)}, u32[]{:S(2)}, u32[]{:S(2)}) collective-permute-start(bf16[32,7296]{1,0:T(8,128)(2,1)S(1)} %get-tuple-element.25), channel_id=1, source_target_pairs={{0,1},{1,2},{2,3},{3,0},{4,5},{5,6},{6,7},{7,4},{8,9},{9,10},{10,1... | collective-permute-start | bytes 1400840 | tf_op jit(solution)/shard_map/ppermute | solution.py:423
  56.9 13.9 %collective-permute-start.5 = (bf16[32,7296]{1,0:T(8,128)(2,1)S(1)}, bf16[32,7296]{1,0:T(8,128)(2,1)S(1)}, u32[]{:S(2)}, u32[]{:S(2)}) collective-permute-start(bf16[32,7296]{1,0:T(8,128)(2,1)S(1)} %get-tuple-element.26), channel_id=1, source_target_pairs={{0,2},{1,3},{2,0},{3,1},{4,6},{5,7},{6,4},{7,5},{8,10},{9,11},{10,... | collective-permute-start | bytes 1400840 | tf_op jit(solution)/shard_map/ppermute | solution.py:423
  58.6 12.8 %collective-permute-start.6 = (bf16[32,7296]{1,0:T(8,128)(2,1)S(1)}, bf16[32,7296]{1,0:T(8,128)(2,1)S(1)}, u32[]{:S(2)}, u32[]{:S(2)}) collective-permute-start(bf16[32,7296]{1,0:T(8,128)(2,1)S(1)} %get-tuple-element.27), channel_id=1, source_target_pairs={{0,3},{1,0},{2,1},{3,2},{4,7},{5,4},{6,5},{7,6},{8,11},{9,8},{10,9... | collective-permute-start | bytes 1400840 | tf_op jit(solution)/shard_map/ppermute | solution.py:423
  71.7 6.5 %collective-permute-start.7 = (bf16[8,7296]{1,0:T(8,128)(2,1)S(1)}, bf16[8,7296]{1,0:T(8,128)(2,1)S(1)}, u32[]{:S(2)}, u32[]{:S(2)}) collective-permute-start(bf16[8,7296]{1,0:T(8,128)(2,1)S(1)} %get-tuple-element.29), channel_id=1, source_target_pairs={{0,4},{1,5},{2,6},{3,7},{4,8},{5,9},{6,10},{7,11},{8,12},{9,13},{1... | collective-permute-start | bytes 350216 | tf_op jit(solution)/shard_map/ppermute | solution.py:434
  72.1 6.1 %collective-permute-start.8 = (bf16[8,7296]{1,0:T(8,128)(2,1)S(1)}, bf16[8,7296]{1,0:T(8,128)(2,1)S(1)}, u32[]{:S(2)}, u32[]{:S(2)}) collective-permute-start(bf16[8,7296]{1,0:T(8,128)(2,1)S(1)} %get-tuple-element.30), channel_id=1, source_target_pairs={{0,8},{1,9},{2,10},{3,11},{4,12},{5,13},{6,14},{7,15},{8,0},{9,1},... | collective-permute-start | bytes 350216 | tf_op jit(solution)/shard_map/ppermute | solution.py:434
  73.4 5.4 %collective-permute-start.9 = (bf16[8,7296]{1,0:T(8,128)(2,1)S(1)}, bf16[8,7296]{1,0:T(8,128)(2,1)S(1)}, u32[]{:S(2)}, u32[]{:S(2)}) collective-permute-start(bf16[8,7296]{1,0:T(8,128)(2,1)S(1)} %get-tuple-element.31), channel_id=1, source_target_pairs={{0,12},{1,13},{2,14},{3,15},{4,0},{5,1},{6,2},{7,3},{8,4},{9,5},{1... | collective-permute-start | bytes 350216 | tf_op jit(solution)/shard_map/ppermute | solution.py:434
  96.6 5.8 %collective-permute-start.10 = (f32[128,512]{1,0:T(8,128)S(1)}, f32[128,512]{1,0:T(8,128)S(1)}, u32[]{:S(2)}, u32[]{:S(2)}) collective-permute-start(f32[128,512]{1,0:T(8,128)S(1)} %fusion.mine_ref), channel_id=1, source_target_pairs={{0,16},{16,0},{32,48},{48,32},{64,80},{80,64},{96,112},{112,96},{1... | collective-permute-start | bytes 786440 | tf_op jit(solution)/shard_map/ppermute | solution.py:315
  102.4 6.0 %collective-permute-start.11 = (bf16[128,512]{1,0:T(8,128)(2,1)S(1)}, bf16[128,512]{1,0:T(8,128)(2,1)S(1)}, u32[]{:S(2)}, u32[]{:S(2)}) collective-permute-start(bf16[128,512]{1,0:T(8,128)(2,1)S(1)} %get-tuple-element.32.mine_ref), channel_id=1, source_target_pairs={{0,32},{16,112},{32,64},{48,16},{64,96},{80,48},{96,0},{112,80},{1... | collective-permute-start | bytes 393224 | tf_op jit(solution)/shard_map/ppermute | solution.py:318
  102.8 5.6 %collective-permute-start.12 = (bf16[64,512]{1,0:T(8,128)(2,1)S(1)}, bf16[64,512]{1,0:T(8,128)(2,1)S(1)}, u32[]{:S(2)}, u32[]{:S(2)}) collective-permute-start(bf16[64,512]{1,0:T(8,128)(2,1)S(1)} %get-tuple-element.33), channel_id=1, source_target_pairs={{0,64},{16,80},{32,96},{48,112},{64,0},{80,16},{96,32},{112,48},{1... | collective-permute-start | bytes 196616 | tf_op jit(solution)/shard_map/ppermute | solution.py:319
  108.5 3.1 %collective-permute-start.13 = (bf16[192,512]{1,0:T(8,128)(2,1)S(1)}, bf16[192,512]{1,0:T(8,128)(2,1)S(1)}, u32[]{:S(2)}, u32[]{:S(2)}) collective-permute-start(bf16[192,512]{1,0:T(8,128)(2,1)S(1)} %shard_map.135), channel_id=1, source_target_pairs={{0,16},{16,0},{32,48},{48,32},{64,80},{80,64},{96,112},{112,96},{1... | collective-permute-start | bytes 589832 | tf_op jit(solution)/shard_map/ppermute | solution.py:321

commit v3 on v2

--- a/solution.py
+++ b/solution.py
@@ -10,6 +10,7 @@
 D = 8192
 EPSILON = 1e-05
 BF16 = jnp.bfloat16
+F16 = jnp.float16
 F32 = jnp.float32
 SIDE = 4
 PARTS = SIDE * SIDE
@@ -20,6 +21,8 @@
 SMEM = pl.BlockSpec(memory_space=pltpu.SMEM)
 KIB = 1 << 10
 MIB = 1 << 20
+REACH = 8192.0
+NORM_SCALES = (2.0**-2, 2.0**6, 2.0**16)
 
 
 def wide_pairs(target):
@@ -67,11 +70,40 @@
     )(*operands)
 
 
-def place_squares(squares):
-    high = squares.astype(BF16).astype(F32)
-    low = squares - high
+def reach(squares):
+    return REACH * lax.rsqrt(jnp.maximum(squares, 1e-30))
+
+
+def write_norm(squares):
+    rest = squares * lax.rsqrt(jnp.maximum(squares, 1e-30))
     lane = lax.broadcasted_iota(jnp.int32, (squares.shape[0], LANES), 1)
-    return jnp.where(lane == 0, high, jnp.where(lane == 1, low, 0.0))
+    tile = jnp.zeros((squares.shape[0], LANES), F32)
+    for i, factor in enumerate(NORM_SCALES):
+        part = rest * factor
+        if i < 2:
+            part = part.astype(BF16).astype(F32)
+            part = jnp.where(jnp.abs(part) < 2.0**-10, 0.0, part)
+        rest = rest - part * (1.0 / factor)
+        tile = jnp.where(lane == i, part, tile)
+    return tile
+
+
+def read_norm(tile):
+    parts = [tile[:, i : i + 1] * (1.0 / factor) for i, factor in enumerate(NORM_SCALES)]
+    return (parts[0] + parts[1]) + parts[2]
+
+
+def weighted(refs):
+    last = refs[0].shape[1] - LANES
+    norms = [read_norm(ref[:, pl.ds(last, LANES)]) for ref in refs]
+    squares = [norm * norm for norm in norms]
+    weights = [norm * (1.0 / REACH) for norm in norms]
+
+    def total(at, size):
+        parts = [ref[:, pl.ds(at, size)] * weight for ref, weight in zip(refs, weights)]
+        return (parts[0] + parts[1]) + (parts[2] + parts[3])
+
+    return total, (squares[0] + squares[1]) + (squares[2] + squares[3])
 
 
 def project_kernel(
@@ -90,19 +122,16 @@
             stream_ref[pl.ds((n * 2 + m) * rows, rows), :] = x_ref[m, pl.ds(n * rows, rows), :]
     stream = stream_ref[...]
     squares = jnp.sum(stream * stream, axis=-1, keepdims=True)
+    scale = reach(squares)
     normed = (stream * gain_ref[...]).astype(BF16)
     at = 0
-    for copy, w_ref, exact in zip(copies[2:], (wq_ref, wk_ref, wv_ref), (True, True, False)):
+    for copy, w_ref in zip(copies[2:], (wq_ref, wk_ref, wv_ref)):
         copy.wait()
         width = w_ref.shape[1]
         product = jnp.dot(normed, w_ref[...], preferred_element_type=F32)
-        high = product.astype(BF16)
-        out_ref[:, pl.ds(at, width)] = high
+        out_ref[:, pl.ds(at, width)] = product * scale
         at += width
-        if exact:
-            out_ref[:, pl.ds(at, width)] = (product - high.astype(F32)).astype(BF16)
-            at += width
-    out_ref[:, pl.ds(at, LANES)] = place_squares(squares).astype(out_ref.dtype)
+    out_ref[:, pl.ds(at, LANES)] = write_norm(squares)
 
 
 def total_kernel(core_ref, mine_ref, other_ref, total_ref, half_ref):
@@ -119,13 +148,13 @@
 
 
 def attend_kernel(
-    len_ref, got_ref, cos_ref, sin_ref, keys_hbm, values_hbm, out_ref, q_s, a_s, s_s, keys_s, values_s,
+    len_ref, total_ref, squares_ref, cos_ref, sin_ref, keys_hbm, values_hbm, out_ref, q_s, a_s, s_s, keys_s, values_s,
     key_sems, value_sems,
 ):
-    here = got_ref.shape[1]
+    here = total_ref.shape[0]
     cache = keys_s.shape[1]
     chunk = 512
-    counts = [(len_ref[r] + chunk - 1) // chunk for r in range(here)]
+    counts = [lax.shift_right_logical(len_ref[r] + (chunk - 1), 9) for r in range(here)]
 
     def fetch(far, near, sems, r, j):
         part = pl.ds(pl.multiple_of(j * chunk, chunk), chunk)
@@ -152,25 +181,20 @@
             part = pl.ds(pl.multiple_of(j * chunk, chunk), chunk)
             values_s[r, part, :] = jnp.zeros((chunk, HEAD), BF16)
 
-    total = got_ref[0].astype(F32)
-    for n in range(1, PARTS):
-        total = total + got_ref[n].astype(F32)
+    total = total_ref[...]
     heads = out_ref.shape[2] // HEAD
     split = heads * HEAD
-    query = total[:, :split] + total[:, split : 2 * split]
-    total = total[:, 2 * split :]
-    squares = jnp.sum(total[:, 3 * HEAD :], axis=-1, keepdims=True)
-    factor = lax.rsqrt(squares / D + EPSILON)
+    factor = lax.rsqrt(squares_ref[...] / D + EPSILON)
     cos, sin = cos_ref[...], sin_ref[...]
 
     def turned(part):
         part = part * factor
         return (part * cos + pltpu.roll(part, HEAD // 2, 1) * sin).astype(BF16).astype(F32)
 
-    key_new = turned(total[:, :HEAD] + total[:, HEAD : 2 * HEAD])
-    value_new = (total[:, 2 * HEAD : 3 * HEAD] * factor).astype(BF16).astype(F32)
+    key_new = turned(total[:, split : split + HEAD])
+    value_new = (total[:, split + HEAD :] * factor).astype(BF16).astype(F32)
     for h in range(heads):
-        q_s[:, h, :] = turned(query[:, h * HEAD : (h + 1) * HEAD])
+        q_s[:, h, :] = turned(total[:, h * HEAD : (h + 1) * HEAD])
     scaling = HEAD ** (-0.5)
     position = lax.broadcasted_iota(jnp.int32, (1, cache), 1)
     for r in range(here):
@@ -233,7 +257,8 @@
         start = pl.multiple_of(blocks_ref[i] * rows, rows)
         sorted_s[pl.ds(i * rows, rows), :] = middle_ref[pl.ds(start, rows), :]
     middle = sorted_s[...]
-    squares = place_squares(jnp.sum(middle * middle, axis=-1, keepdims=True))
+    squares = jnp.sum(middle * middle, axis=-1, keepdims=True)
+    scale, norm = reach(squares), write_norm(squares)
     normed_s[...] = (middle * gain_ref[...]).astype(BF16)
     outs = (out0_ref, out1_ref, out2_ref, out3_ref)
     units = wg_ref.shape[1]
@@ -242,45 +267,34 @@
     normed = normed_s[...]
     for at, w_ref in ((0, wg_ref), (units, wu_ref)):
         for j in range(0, units, tile):
-            product = jnp.dot(normed, w_ref[:, pl.ds(j, tile)], preferred_element_type=F32)
+            product = jnp.dot(normed, w_ref[:, pl.ds(j, tile)], preferred_element_type=F32) * scale
             for d in range(SIDE):
-                part = product[d * group : (d + 1) * group, :]
-                outs[d][:, pl.ds(at + j, tile)] = part.astype(outs[d].dtype)
+                outs[d][:, pl.ds(at + j, tile)] = product[d * group : (d + 1) * group, :]
     for d in range(SIDE):
-        part = squares[d * group : (d + 1) * group, :]
-        outs[d][:, pl.ds(2 * units, LANES)] = part.astype(outs[d].dtype)
-
-
-def middle_sum_kernel(a_ref, b_ref, c_ref, d_ref, own_ref, out1_ref, out2_ref, out3_ref):
-    width = a_ref.shape[1]
-    last = width - LANES
+        outs[d][:, pl.ds(2 * units, LANES)] = norm[d * group : (d + 1) * group, :]
+
+
+def middle_sum_kernel(a_ref, b_ref, c_ref, d_ref, out0_ref, out1_ref, out2_ref, out3_ref):
+    last = a_ref.shape[1] - LANES
     tile = 1024
     rows = a_ref.shape[0] // SIDE
-
-    def total(at, size):
-        parts = [ref[:, pl.ds(at, size)].astype(F32) for ref in (a_ref, b_ref, c_ref, d_ref)]
-        return (parts[0] + parts[1]) + (parts[2] + parts[3])
-
-    outs = (own_ref, out1_ref, out2_ref, out3_ref)
+    total, squares = weighted((a_ref, b_ref, c_ref, d_ref))
+    scale = reach(squares)
+    outs = (out0_ref, out1_ref, out2_ref, out3_ref)
 
     def put(at, size, value):
         for k in range(SIDE):
-            outs[k][:, pl.ds(at, size)] = value[k * rows : (k + 1) * rows, :].astype(outs[k].dtype)
+            outs[k][:, pl.ds(at, size)] = value[k * rows : (k + 1) * rows, :]
 
     for at in range(0, last, tile):
-        put(at, tile, total(at, tile))
-    put(last, LANES, place_squares(jnp.sum(total(last, LANES), axis=-1, keepdims=True)))
+        put(at, tile, total(at, tile) * scale)
+    put(last, LANES, write_norm(squares))
 
 
 def hidden_kernel(a_ref, b_ref, c_ref, d_ref, out_ref):
     units = out_ref.shape[2]
     tile = 512
-
-    def total(at, size):
-        parts = [ref[:, pl.ds(at, size)].astype(F32) for ref in (a_ref, b_ref, c_ref, d_ref)]
-        return (parts[0] + parts[1]) + (parts[2] + parts[3])
-
-    squares = jnp.sum(total(2 * units, LANES), axis=-1, keepdims=True)
+    total, squares = weighted((a_ref, b_ref, c_ref, d_ref))
     factor = lax.rsqrt(squares / D + EPSILON)
     for at in range(0, units, tile):
         gate = total(at, tile) * factor
@@ -301,6 +315,14 @@
 
 def exchange(payload):
     return lax.all_to_all(payload, "narrow", 0, 0, tiled=True)
+
+
+def move(sends, stage):
+    taken = {}
+    for step in (1, 3, 2):
+        block = sends[step - 1].astype(F16)
+        taken[step] = lax.ppermute(block, ("wide", "narrow"), plane_pairs(step, stage)).astype(F32)
+    return [taken[step] for step in (1, 2, 3)]
 
 
 def sum_wide_parts(partial, core_flag):
@@ -361,7 +383,7 @@
 
     payload, stream = call(
         project_kernel,
-        [((every, 2 * split + 4 * HEAD), BF16), ((every, width), F32)],
+        [((every, split + 3 * HEAD), F32), ((every, width), F32)],
         8 * MIB,
         lengths,
         blocks,
@@ -379,14 +401,19 @@
         + [pltpu.VMEM(w.shape, BF16) for w in (w_query, w_key, w_value)]
         + [pltpu.SemaphoreType.DMA((5,))],
     )
-    got = exchange(payload.reshape(PARTS, here, -1))
+    got = exchange(payload.astype(F16).reshape(PARTS, here, -1)).astype(F32)
+    norms = got[:, :, split + 2 * HEAD :][:, :, : len(NORM_SCALES)]
+    norms = jnp.sum(norms * (1.0 / jnp.array(NORM_SCALES, F32)), axis=-1, keepdims=True)
+    total = jnp.sum(got[:, :, : split + 2 * HEAD] * (norms * (1.0 / REACH)), axis=0)
+    squares = jnp.sum(norms * norms, axis=0)
 
     (attended,) = call(
         attend_kernel,
         [((PARTS, here, split), BF16)],
         16 * MIB,
         lengths,
-        got,
+        total,
+        squares,
         cosines,
         sines,
         key_cache.reshape(here, -1, HEAD),
@@ -404,7 +431,7 @@
     full = 2 * units + LANES
     middle, own, *sends = call(
         gate_kernel,
-        [((every, width), F32), ((group, full), F32)] + [((group, full), BF16)] * (SIDE - 1),
+        [((every, width), F32)] + [((group, full), F32)] * SIDE,
         8 * MIB,
         core_flag,
         blocks,
@@ -417,24 +444,10 @@
         held=2,
         scratch=[pltpu.VMEM((every, width), F32), pltpu.VMEM((every, width), BF16)],
     )
-    axes = ("wide", "narrow")
-    taken = {}
-    for step in (1, 3, 2):
-        taken[step] = lax.ppermute(sends[step - 1], axes, plane_pairs(step, 0))
-    own, *sends = call(
-        middle_sum_kernel,
-        [((here, full), F32)] + [((here, full), BF16)] * (SIDE - 1),
-        8 * MIB,
-        own,
-        taken[1],
-        taken[2],
-        taken[3],
-    )
-    for step in (1, 3, 2):
-        taken[step] = lax.ppermute(sends[step - 1], axes, plane_pairs(step, 1))
-    (hidden,) = call(
-        hidden_kernel, [((PARTS, here, units), BF16)], 8 * MIB, own, taken[1], taken[2], taken[3]
-    )
+    taken = move(sends, 0)
+    own, *sends = call(middle_sum_kernel, [((here, full), F32)] * SIDE, 8 * MIB, own, *taken)
+    taken = move(sends, 1)
+    (hidden,) = call(hidden_kernel, [((PARTS, here, units), BF16)], 8 * MIB, own, *taken)
     gathered = exchange(hidden).reshape(every, units)
     parts = sum_wide_parts(jnp.dot(gathered, w_down, preferred_element_type=F32), core_flag)
     (result,) = call(

time: 113 us -> 109 us (0.965)
  blocking collectives: 46.9 us -> 42.1 us
  starting transfers between devices: 21.6 us -> 19 us
  waiting for transfers between devices: 30.9 us -> 33.2 us
    all_to_all x3, blocking collectives: 46.9 us -> 42.1 us  [exchange(): return lax.all_to_all(payload, 'narrow', 0, 0, tiled=True)]
    ppermute x6, waiting for transfers between devices: 16.1 us -> 18.5 us  [move(): lax.ppermute(block, ('wide', 'narrow'), plane_pairs(step, stage))]
    ppermute x6, starting transfers between devices: 5.58 us -> 3.61 us  [move(): lax.ppermute(block, ('wide', 'narrow'), plane_pairs(step, stage))]
  transfers between devices with their start and end apart: 14 -> 14, of which waited for: 10 -> 12; matrix products, arithmetic and copies ran while one was open for 0% -> 0% of each run, Pallas kernels for 0% -> 0%
where the time goes in v3:
time: 109 us; the launch traced here: 108 us
  blocking collectives  42.1 us (39%)
  waiting for transfers between devices  33.2 us (30%)
  starting transfers between devices  19 us (17%)
  Pallas kernels  11.2 us (10%)
    all_to_all x3, blocking collectives, exchange(): return lax.all_to_all(payload, 'narrow', 0, 0, tiled=True)  42.1 us
    ppermute x6, waiting for transfers between devices, move(): lax.ppermute(block, ('wide', 'narrow'), plane_pairs(step, stage))  18.5 us
    pallas_call x10, Pallas kernels, call(): pl.pallas_call(kernel, out_shape=[jax.ShapeDtypeStruct(shape, kind) for s...  11.2 us
    ppermute x2, waiting for transfers between devices, sum_wide_parts(): far = lax.ppermute(part, 'wide', FAR_Z)  10.2 us
    ppermute x2, starting transfers between devices, sum_wide_parts(): lax.ppermute(partial, 'wide', CORE_SWAP)  7.26 us
    ppermute x2, starting transfers between devices, sum_wide_parts(): near = lax.ppermute(mine, 'wide', NEXT_Z)  4.19 us
    ppermute x6, starting transfers between devices, move(): lax.ppermute(block, ('wide', 'narrow'), plane_pairs(step, stage))  3.61 us
    ppermute x2, starting transfers between devices, sum_wide_parts(): other = lax.ppermute(both, 'wide', CORE_SWAP)  2.95 us
  transfers between devices with their start and end apart: 14, of which 12 were waited for; matrix products, arithmetic and copies ran while one was open for 0% of the time, Pallas kernels for 0%

profile of v3, /device:TPU:1, one launch (start us, length us, event | category | flops | bytes accessed | tf_op | source)
XLA Modules:
  0.0 108.5 jit_solution(3693313876324983990)
XLA Ops:
  0.0 0.8 reshape.37.len_ref
  1.1 2.6 %shard_map.136 = (f32[128,1408]{1,0:T(8,128)S(1)}, f32[128,512]{1,0:T(8,128)S(1)}) custom-call(s32[8]{0:T(128)S(1)} %reshape.37.len_ref, s32[16]{0:T(128)S(1)} %fusion.7.blocks_ref, s32[1]{0:T(128)} %bitcast.core_ref, f32[8,128]{1,0:T(8,128)S(1)} %get-tuple-element.40.cos_ref, f32[8,128]{1,0:T(8,128)S(1)} %get-tuple-element.41.sin_ref, f32[2,64,512]{2,1,0:T(8,128)} %x_hbm.1, ...), custom_call_target="tpu_custom_call" | custom-call | bytes 1583204 | tf_op jit(solution)/shard_map/pallas_call | solution.py:62
  3.7 16.2 %all_to_all.15 = f16[16,8,1408]{2,1,0:T(8,128)(2,1)S(1)} all-to-all(f16[16,8,1408]{2,1,0:T(8,128)(2,1)S(1)} %convert_bitcast_fusion), channel_id=1, replica_groups=mesh['wide'=8,'narrow'=16] {'narrow'}, dimensions={0} | all-to-all | bytes 720896 | tf_op jit(solution)/shard_map/all_to_all | solution.py:317
  20.3 5.0 %shard_map.137 = bf16[16,8,1024]{2,1,0:T(8,128)(2,1)S(1)} custom-call(s32[8]{0:T(128)S(1)} %reshape.37.len_ref, f32[8,1280]{1,0:T(8,128)S(1)} %fusion.2.total_ref, f32[8,1]{1,0:T(8,128)S(1)} %copy.15.squares_ref, f32[8,128]{1,0:T(8,128)S(1)} %get-tuple-element.40.cos_ref, f32[8,128]{1,0:T(8,128)S(1)} %get-tuple-element.41.sin_ref, ...), custom_call_target="tpu_custom_call" | custom-call | bytes 8437824 | tf_op jit(solution)/shard_map/pallas_call | solution.py:62
  25.4 10.2 %all_to_all.16 = bf16[16,8,1024]{2,1,0:T(8,128)(2,1)S(1)} all-to-all(bf16[16,8,1024]{2,1,0:T(8,128)(2,1)S(1)} %shard_map.137), channel_id=1, replica_groups=mesh['wide'=8,'narrow'=16] {'narrow'}, dimensions={0} | all-to-all | bytes 524288 | tf_op jit(solution)/shard_map/all_to_all | solution.py:317
  35.9 3.1 %collective-permute-start = (f32[128,512]{1,0:T(8,128)S(1)}, f32[128,512]{1,0:T(8,128)S(1)}, u32[]{:S(2)}, u32[]{:S(2)}) collective-permute-start(f32[128,512]{1,0:T(8,128)S(1)} %fusion.3.mine_ref), channel_id=1, source_target_pairs={{0,16},{16,0},{32,48},{48,32},{64,80},{80,64},{96,112},{112,96},{1... | collective-permute-start | bytes 786440 | tf_op jit(solution)/shard_map/ppermute | solution.py:337
  39.0 1.2 %collective-permute-done.other_ref = f32[128,512]{1,0:T(8,128)S(1)} collective-permute-done((f32[128,512]{1,0:T(8,128)S(1)}, f32[128,512]{1,0:T(8,128)S(1)}, u32[]{:S(2)}, u32[]{:S(2)}) %collective-permute-start) | collective-permute-done | bytes 262176 | tf_op jit(solution)/shard_map/ppermute | solution.py:337
  40.2 3.8 %collective-permute-start.1 = (bf16[128,512]{1,0:T(8,128)(2,1)S(1)}, bf16[128,512]{1,0:T(8,128)(2,1)S(1)}, u32[]{:S(2)}, u32[]{:S(2)}) collective-permute-start(bf16[128,512]{1,0:T(8,128)(2,1)S(1)} %get-tuple-element.21.mine_ref), channel_id=1, source_target_pairs={{0,32},{16,112},{32,64},{48,16},{64,96},{80,48},{96,0},{112,80},{1... | collective-permute-start | bytes 393224 | tf_op jit(solution)/shard_map/ppermute | solution.py:340
  44.1 5.6 %collective-permute-done.2.far_ref = bf16[64,512]{1,0:T(8,128)(2,1)S(1)} collective-permute-done((bf16[64,512]{1,0:T(8,128)(2,1)S(1)}, bf16[64,512]{1,0:T(8,128)(2,1)S(1)}, u32[]{:S(2)}, u32[]{:S(2)}) %collective-permute-start.2) | collective-permute-done | bytes 65568 | tf_op jit(solution)/shard_map/ppermute | solution.py:341
  49.7 0.9 collective-permute-start.3
  50.6 1.1 collective-permute-done.3.other_ref
  51.7 1.8 %shard_map.140 = (f32[128,512]{1,0:T(8,128)S(1)}, f32[32,7296]{1,0:T(8,128)S(1)}, f32[32,7296]{1,0:T(8,128)S(1)}, f32[32,7296]{1,0:T(8,128)S(1)}, f32[32,7296]{1,0:T(8,128)S(1)}) custom-call(s32[1]{0:T(128)} %bitcast.core_ref, s32[16]{0:T(128)S(1)} %fusion.7.blocks_ref, bf16[128,512]{1,0:T(8,128)(2,1)S(1)} %get-tuple-element.21.mine_ref, ...), custom_call_target="tpu_custom_call" | custom-call | bytes 8128580 | tf_op jit(solution)/shard_map/pallas_call | solution.py:62
  53.6 0.6 collective-permute-start.6
  54.3 1.0 collective-permute-start.5
  55.4 6.0 %collective-permute-done.6 = f16[32,7296]{1,0:T(8,128)(2,1)S(1)} collective-permute-done((f16[32,7296]{1,0:T(8,128)(2,1)S(1)}, f16[32,7296]{1,0:T(8,128)(2,1)S(1)}, u32[]{:S(2)}, u32[]{:S(2)}) %collective-permute-start.6) | collective-permute-done | bytes 466976 | tf_op jit(solution)/shard_map/ppermute | solution.py:324
  61.5 2.1 %collective-permute-done.5 = f16[32,7296]{1,0:T(8,128)(2,1)S(1)} collective-permute-done((f16[32,7296]{1,0:T(8,128)(2,1)S(1)}, f16[32,7296]{1,0:T(8,128)(2,1)S(1)}, u32[]{:S(2)}, u32[]{:S(2)}) %collective-permute-start.5) | collective-permute-done | bytes 466976 | tf_op jit(solution)/shard_map/ppermute | solution.py:324
  63.6 4.9 %collective-permute-done.4 = f16[32,7296]{1,0:T(8,128)(2,1)S(1)} collective-permute-done((f16[32,7296]{1,0:T(8,128)(2,1)S(1)}, f16[32,7296]{1,0:T(8,128)(2,1)S(1)}, u32[]{:S(2)}, u32[]{:S(2)}) %collective-permute-start.4) | collective-permute-done | bytes 466976 | tf_op jit(solution)/shard_map/ppermute | solution.py:324
  68.5 0.5 shard_map.141
  69.2 0.8 collective-permute-start.9
  69.9 1.1 collective-permute-start.8
  71.1 1.8 %collective-permute-done.9 = f16[8,7296]{1,0:T(8,128)(2,1)S(1)} collective-permute-done((f16[8,7296]{1,0:T(8,128)(2,1)S(1)}, f16[8,7296]{1,0:T(8,128)(2,1)S(1)}, u32[]{:S(2)}, u32[]{:S(2)}) %collective-permute-start.9) | collective-permute-done | bytes 116768 | tf_op jit(solution)/shard_map/ppermute | solution.py:324
  72.9 2.2 %collective-permute-done.8 = f16[8,7296]{1,0:T(8,128)(2,1)S(1)} collective-permute-done((f16[8,7296]{1,0:T(8,128)(2,1)S(1)}, f16[8,7296]{1,0:T(8,128)(2,1)S(1)}, u32[]{:S(2)}, u32[]{:S(2)}) %collective-permute-start.8) | collective-permute-done | bytes 116768 | tf_op jit(solution)/shard_map/ppermute | solution.py:324
  75.2 1.5 %collective-permute-done.7 = f16[8,7296]{1,0:T(8,128)(2,1)S(1)} collective-permute-done((f16[8,7296]{1,0:T(8,128)(2,1)S(1)}, f16[8,7296]{1,0:T(8,128)(2,1)S(1)}, u32[]{:S(2)}, u32[]{:S(2)}) %collective-permute-start.7) | collective-permute-done | bytes 116768 | tf_op jit(solution)/shard_map/ppermute | solution.py:324
  77.0 15.7 %all_to_all.17 = bf16[16,8,3584]{2,1,0:T(8,128)(2,1)S(1)} all-to-all(bf16[16,8,3584]{2,1,0:T(8,128)(2,1)S(1)} %shard_map.142), channel_id=1, replica_groups=mesh['wide'=8,'narrow'=16] {'narrow'}, dimensions={0} | all-to-all | bytes 1835008 | tf_op jit(solution)/shard_map/all_to_all | solution.py:317
  92.6 0.6 fusion.mine_ref
  93.3 4.1 %collective-permute-start.10 = (f32[128,512]{1,0:T(8,128)S(1)}, f32[128,512]{1,0:T(8,128)S(1)}, u32[]{:S(2)}, u32[]{:S(2)}) collective-permute-start(f32[128,512]{1,0:T(8,128)S(1)} %fusion.mine_ref), channel_id=1, source_target_pairs={{0,16},{16,0},{32,48},{48,32},{64,80},{80,64},{96,112},{112,96},{1... | collective-permute-start | bytes 786440 | tf_op jit(solution)/shard_map/ppermute | solution.py:337
  97.4 1.2 %collective-permute-done.10.other_ref = f32[128,512]{1,0:T(8,128)S(1)} collective-permute-done((f32[128,512]{1,0:T(8,128)S(1)}, f32[128,512]{1,0:T(8,128)S(1)}, u32[]{:S(2)}, u32[]{:S(2)}) %collective-permute-start.10) | collective-permute-done | bytes 262176 | tf_op jit(solution)/shard_map/ppermute | solution.py:337
  99.0 1.0 collective-permute-start.12
  100.0 4.6 %collective-permute-done.12.far_ref = bf16[64,512]{1,0:T(8,128)(2,1)S(1)} collective-permute-done((bf16[64,512]{1,0:T(8,128)(2,1)S(1)}, bf16[64,512]{1,0:T(8,128)(2,1)S(1)}, u32[]{:S(2)}, u32[]{:S(2)}) %collective-permute-start.12) | collective-permute-done | bytes 65568 | tf_op jit(solution)/shard_map/ppermute | solution.py:341
  104.6 2.0 %collective-permute-start.13 = (bf16[192,512]{1,0:T(8,128)(2,1)S(1)}, bf16[192,512]{1,0:T(8,128)(2,1)S(1)}, u32[]{:S(2)}, u32[]{:S(2)}) collective-permute-start(bf16[192,512]{1,0:T(8,128)(2,1)S(1)} %shard_map.144), channel_id=1, source_target_pairs={{0,16},{16,0},{32,48},{48,32},{64,80},{80,64},{96,112},{112,96},{1... | collective-permute-start | bytes 589832 | tf_op jit(solution)/shard_map/ppermute | solution.py:343
  106.6 1.1 collective-permute-done.13.other_ref
  107.7 0.8 shard_map.145
  (47 shorter events, 2.3 us)
Async XLA Ops:
  0.0 35.6 %copy-start = (bf16[1024,512]{1,0:T(8,128)(2,1)S(1)}, bf16[1024,512]{1,0:T(8,128)(2,1)}, u32[]{:S(2)}) copy-start(bf16[1024,512]{1,0:T(8,128)(2,1)} %param.19) | copy-start | bytes 3145732
  0.0 20.0 %copy-start.5 = (f32[3]{0:T(128)S(1)}, f32[3]{0:T(128)}, u32[]{:S(2)}) copy-start(f32[3]{0:T(128)} %constant.94) | copy-start | bytes 40
  20.3 31.4 %copy-start.1 = (bf16[512,3584]{1,0:T(8,128)(2,1)S(1)}, bf16[512,3584]{1,0:T(8,128)(2,1)}, u32[]{:S(2)}) copy-start(bf16[512,3584]{1,0:T(8,128)(2,1)} %wg_ref.1) | copy-start | bytes 11010052
  20.3 31.4 %copy-start.2 = (bf16[512,3584]{1,0:T(8,128)(2,1)S(1)}, bf16[512,3584]{1,0:T(8,128)(2,1)}, u32[]{:S(2)}) copy-start(bf16[512,3584]{1,0:T(8,128)(2,1)} %wu_ref.1) | copy-start | bytes 11010052
  20.3 31.4 %copy-start.3 = (f32[512]{0:T(512)S(1)}, f32[512]{0:T(512)}, u32[]{:S(2)}) copy-start(f32[512]{0:T(512)} %param.20) | copy-start | bytes 6148
  35.9 4.3 %collective-permute-start = (f32[128,512]{1,0:T(8,128)S(1)}, f32[128,512]{1,0:T(8,128)S(1)}, u32[]{:S(2)}, u32[]{:S(2)}) collective-permute-start(f32[128,512]{1,0:T(8,128)S(1)} %fusion.3.mine_ref), channel_id=1, source_target_pairs={{0,16},{16,0},{32,48},{48,32},{64,80},{80,64},{96,112},{112,96},{1... | collective-permute-start | bytes 786440 | tf_op jit(solution)/shard_map/ppermute | solution.py:337
  40.2 9.4 %collective-permute-start.1 = (bf16[128,512]{1,0:T(8,128)(2,1)S(1)}, bf16[128,512]{1,0:T(8,128)(2,1)S(1)}, u32[]{:S(2)}, u32[]{:S(2)}) collective-permute-start(bf16[128,512]{1,0:T(8,128)(2,1)S(1)} %get-tuple-element.21.mine_ref), channel_id=1, source_target_pairs={{0,32},{16,112},{32,64},{48,16},{64,96},{80,48},{96,0},{112,80},{1... | collective-permute-start | bytes 393224 | tf_op jit(solution)/shard_map/ppermute | solution.py:340
  44.1 5.6 %collective-permute-start.2 = (bf16[64,512]{1,0:T(8,128)(2,1)S(1)}, bf16[64,512]{1,0:T(8,128)(2,1)S(1)}, u32[]{:S(2)}, u32[]{:S(2)}) collective-permute-start(bf16[64,512]{1,0:T(8,128)(2,1)S(1)} %get-tuple-element.22), channel_id=1, source_target_pairs={{0,64},{16,80},{32,96},{48,112},{64,0},{80,16},{96,32},{112,48},{1... | collective-permute-start | bytes 196616 | tf_op jit(solution)/shard_map/ppermute | solution.py:341
  49.7 2.0 %collective-permute-start.3 = (bf16[192,512]{1,0:T(8,128)(2,1)S(1)}, bf16[192,512]{1,0:T(8,128)(2,1)S(1)}, u32[]{:S(2)}, u32[]{:S(2)}) collective-permute-start(bf16[192,512]{1,0:T(8,128)(2,1)S(1)} %shard_map.139), channel_id=1, source_target_pairs={{0,16},{16,0},{32,48},{48,32},{64,80},{80,64},{96,112},{112,96},{1... | collective-permute-start | bytes 589832 | tf_op jit(solution)/shard_map/ppermute | solution.py:343
  53.6 7.8 %collective-permute-start.6 = (f16[32,7296]{1,0:T(8,128)(2,1)S(1)}, f16[32,7296]{1,0:T(8,128)(2,1)S(1)}, u32[]{:S(2)}, u32[]{:S(2)}) collective-permute-start(f16[32,7296]{1,0:T(8,128)(2,1)S(1)} %convert_element_type.56), channel_id=1, source_target_pairs={{0,3},{1,0},{2,1},{3,2},{4,7},{5,4},{6,5},{7,6},{8,11},{9,8},{10,9... | collective-permute-start | bytes 1400840 | tf_op jit(solution)/shard_map/ppermute | solution.py:324
  54.3 9.3 %collective-permute-start.5 = (f16[32,7296]{1,0:T(8,128)(2,1)S(1)}, f16[32,7296]{1,0:T(8,128)(2,1)S(1)}, u32[]{:S(2)}, u32[]{:S(2)}) collective-permute-start(f16[32,7296]{1,0:T(8,128)(2,1)S(1)} %convert_element_type.54), channel_id=1, source_target_pairs={{0,2},{1,3},{2,0},{3,1},{4,6},{5,7},{6,4},{7,5},{8,10},{9,11},{10,... | collective-permute-start | bytes 1400840 | tf_op jit(solution)/shard_map/ppermute | solution.py:324
  55.3 13.2 %collective-permute-start.4 = (f16[32,7296]{1,0:T(8,128)(2,1)S(1)}, f16[32,7296]{1,0:T(8,128)(2,1)S(1)}, u32[]{:S(2)}, u32[]{:S(2)}) collective-permute-start(f16[32,7296]{1,0:T(8,128)(2,1)S(1)} %convert_element_type.52), channel_id=1, source_target_pairs={{0,1},{1,2},{2,3},{3,0},{4,5},{5,6},{6,7},{7,4},{8,9},{9,10},{10,1... | collective-permute-start | bytes 1400840 | tf_op jit(solution)/shard_map/ppermute | solution.py:324
  69.1 23.5 %copy-start.4 = (bf16[3584,512]{1,0:T(8,128)(2,1)S(1)}, bf16[3584,512]{1,0:T(8,128)(2,1)}, u32[]{:S(2)}) copy-start(bf16[3584,512]{1,0:T(8,128)(2,1)} %param.23) | copy-start | bytes 11010052
  69.2 3.7 %collective-permute-start.9 = (f16[8,7296]{1,0:T(8,128)(2,1)S(1)}, f16[8,7296]{1,0:T(8,128)(2,1)S(1)}, u32[]{:S(2)}, u32[]{:S(2)}) collective-permute-start(f16[8,7296]{1,0:T(8,128)(2,1)S(1)} %convert_element_type.62), channel_id=1, source_target_pairs={{0,12},{1,13},{2,14},{3,15},{4,0},{5,1},{6,2},{7,3},{8,4},{9,5},{1... | collective-permute-start | bytes 350216 | tf_op jit(solution)/shard_map/ppermute | solution.py:324
  69.9 5.2 %collective-permute-start.8 = (f16[8,7296]{1,0:T(8,128)(2,1)S(1)}, f16[8,7296]{1,0:T(8,128)(2,1)S(1)}, u32[]{:S(2)}, u32[]{:S(2)}) collective-permute-start(f16[8,7296]{1,0:T(8,128)(2,1)S(1)} %convert_element_type.60), channel_id=1, source_target_pairs={{0,8},{1,9},{2,10},{3,11},{4,12},{5,13},{6,14},{7,15},{8,0},{9,1},... | collective-permute-start | bytes 350216 | tf_op jit(solution)/shard_map/ppermute | solution.py:324
  71.0 5.6 %collective-permute-start.7 = (f16[8,7296]{1,0:T(8,128)(2,1)S(1)}, f16[8,7296]{1,0:T(8,128)(2,1)S(1)}, u32[]{:S(2)}, u32[]{:S(2)}) collective-permute-start(f16[8,7296]{1,0:T(8,128)(2,1)S(1)} %convert_element_type.58), channel_id=1, source_target_pairs={{0,4},{1,5},{2,6},{3,7},{4,8},{5,9},{6,10},{7,11},{8,12},{9,13},{1... | collective-permute-start | bytes 350216 | tf_op jit(solution)/shard_map/ppermute | solution.py:324
  93.3 5.3 %collective-permute-start.10 = (f32[128,512]{1,0:T(8,128)S(1)}, f32[128,512]{1,0:T(8,128)S(1)}, u32[]{:S(2)}, u32[]{:S(2)}) collective-permute-start(f32[128,512]{1,0:T(8,128)S(1)} %fusion.mine_ref), channel_id=1, source_target_pairs={{0,16},{16,0},{32,48},{48,32},{64,80},{80,64},{96,112},{112,96},{1... | collective-permute-start | bytes 786440 | tf_op jit(solution)/shard_map/ppermute | solution.py:337
  98.6 6.0 %collective-permute-start.11 = (bf16[128,512]{1,0:T(8,128)(2,1)S(1)}, bf16[128,512]{1,0:T(8,128)(2,1)S(1)}, u32[]{:S(2)}, u32[]{:S(2)}) collective-permute-start(bf16[128,512]{1,0:T(8,128)(2,1)S(1)} %get-tuple-element.32.mine_ref), channel_id=1, source_target_pairs={{0,32},{16,112},{32,64},{48,16},{64,96},{80,48},{96,0},{112,80},{1... | collective-permute-start | bytes 393224 | tf_op jit(solution)/shard_map/ppermute | solution.py:340
  99.0 5.6 %collective-permute-start.12 = (bf16[64,512]{1,0:T(8,128)(2,1)S(1)}, bf16[64,512]{1,0:T(8,128)(2,1)S(1)}, u32[]{:S(2)}, u32[]{:S(2)}) collective-permute-start(bf16[64,512]{1,0:T(8,128)(2,1)S(1)} %get-tuple-element.33), channel_id=1, source_target_pairs={{0,64},{16,80},{32,96},{48,112},{64,0},{80,16},{96,32},{112,48},{1... | collective-permute-start | bytes 196616 | tf_op jit(solution)/shard_map/ppermute | solution.py:341
  104.6 3.1 %collective-permute-start.13 = (bf16[192,512]{1,0:T(8,128)(2,1)S(1)}, bf16[192,512]{1,0:T(8,128)(2,1)S(1)}, u32[]{:S(2)}, u32[]{:S(2)}) collective-permute-start(bf16[192,512]{1,0:T(8,128)(2,1)S(1)} %shard_map.144), channel_id=1, source_target_pairs={{0,16},{16,0},{32,48},{48,32},{64,80},{80,64},{96,112},{112,96},{1... | collective-permute-start | bytes 589832 | tf_op jit(solution)/shard_map/ppermute | solution.py:343

commit v4 on v3

--- a/solution.py
+++ b/solution.py
@@ -50,7 +50,7 @@
     return pairs
 
 
-def call(kernel, outs, limit, *operands, scratch=(), scalars=0, far=0, held=0):
+def call(kernel, outs, limit, *operands, scratch=(), scalars=0, far=0, held=0, kept=0):
     near = len(operands) - far
     specs = [SMEM] * scalars + [VMEM] * (near - scalars) + [HBM] * far
     size = sum(o.size * o.dtype.itemsize for o in operands)
@@ -61,7 +61,10 @@
     ]
     return pl.pallas_call(
         kernel,
-        out_shape=[jax.ShapeDtypeStruct(shape, kind) for shape, kind in outs],
+        out_shape=[
+            (jax.ShapeDtypeStruct if i < len(outs) - kept else pltpu.VMEM)(shape, kind)
+            for i, (shape, kind) in enumerate(outs)
+        ],
         in_specs=specs,
         out_specs=[VMEM] * len(outs),
         scratch_shapes=scratch,
@@ -107,13 +110,42 @@
 
 
 def project_kernel(
-    len_ref, blocks_ref, core_ref, cos_ref, sin_ref, x_hbm, gain_hbm, wq_hbm, wk_hbm, wv_hbm, out_ref, stream_ref, x_ref, gain_ref, wq_ref, wk_ref,
-    wv_ref, sems,
+    len_ref, blocks_ref, core_ref, cos_ref, sin_ref, x_hbm, gain_hbm, wq_hbm, wk_hbm, wv_hbm,
+    keys_hbm, values_hbm, out_ref, stream_ref, keys_s, values_s, x_ref, gain_ref, wq_ref, wk_ref,
+    wv_ref, sems, key_sems, value_sems,
 ):
     pairs = ((x_hbm, x_ref), (gain_hbm, gain_ref), (wq_hbm, wq_ref), (wk_hbm, wk_ref), (wv_hbm, wv_ref))
     copies = [pltpu.make_async_copy(a, b, sems.at[i]) for i, (a, b) in enumerate(pairs)]
     for copy in copies:
         copy.start()
+    chunk = 512
+    here, cache = keys_s.shape[0], keys_s.shape[1]
+    counts = [lax.shift_right_logical(len_ref[r] + (chunk - 1), 9) for r in range(here)]
+
+    def fetch(far, near, sems, r, j):
+        part = pl.ds(pl.multiple_of(j * chunk, chunk), chunk)
+        return pltpu.make_async_copy(far.at[r, part], near.at[r, part], sems.at[r, j])
+
+    def start(far, near, sems, r):
+        @pl.loop(0, counts[r])
+        def _(j):
+            fetch(far, near, sems, r, j).start()
+
+    def finish(far, near, sems, r):
+        @pl.loop(0, counts[r])
+        def _(j):
+            fetch(far, near, sems, r, j).wait()
+
+    for r in range(here):
+        start(keys_hbm, keys_s, key_sems, r)
+    for r in range(here):
+        start(values_hbm, values_s, value_sems, r)
+    for r in range(here):
+
+        @pl.loop(counts[r], cache // chunk)
+        def _(j):
+            part = pl.ds(pl.multiple_of(j * chunk, chunk), chunk)
+            values_s[r, part, :] = jnp.zeros((chunk, HEAD), BF16)
     copies[0].wait()
     copies[1].wait()
     rows = x_ref.shape[1] // PARTS
@@ -132,6 +164,9 @@
         out_ref[:, pl.ds(at, width)] = product * scale
         at += width
     out_ref[:, pl.ds(at, LANES)] = write_norm(squares)
+    for r in range(here):
+        finish(keys_hbm, keys_s, key_sems, r)
+        finish(values_hbm, values_s, value_sems, r)
 
 
 def total_kernel(core_ref, mine_ref, other_ref, total_ref, half_ref):
@@ -141,50 +176,15 @@
     half_ref[...] = jnp.where(core_ref[0] == 0, total[:half, :], total[half:, :])
 
 
-def pack_kernel(near_ref, far_ref, out_ref):
-    rows = near_ref.shape[0]
-    out_ref[pl.ds(0, rows), :] = near_ref[...]
-    out_ref[pl.ds(rows, far_ref.shape[0]), :] = far_ref[...]
-
-
 def attend_kernel(
-    len_ref, total_ref, squares_ref, cos_ref, sin_ref, keys_hbm, values_hbm, out_ref, q_s, a_s, s_s, keys_s, values_s,
-    key_sems, value_sems,
+    len_ref, total_ref, squares_ref, cos_ref, sin_ref, keys_ref, values_ref, out_ref, q_s, a_s, s_s,
 ):
     here = total_ref.shape[0]
-    cache = keys_s.shape[1]
-    chunk = 512
-    counts = [lax.shift_right_logical(len_ref[r] + (chunk - 1), 9) for r in range(here)]
-
-    def fetch(far, near, sems, r, j):
-        part = pl.ds(pl.multiple_of(j * chunk, chunk), chunk)
-        return pltpu.make_async_copy(far.at[r, part], near.at[r, part], sems.at[r, j])
-
-    def start(far, near, sems, r):
-        @pl.loop(0, counts[r])
-        def _(j):
-            fetch(far, near, sems, r, j).start()
-
-    def finish(far, near, sems, r):
-        @pl.loop(0, counts[r])
-        def _(j):
-            fetch(far, near, sems, r, j).wait()
-
-    for r in range(here):
-        start(keys_hbm, keys_s, key_sems, r)
-    for r in range(here):
-        start(values_hbm, values_s, value_sems, r)
-    for r in range(here):
-
-        @pl.loop(counts[r], cache // chunk)
-        def _(j):
-            part = pl.ds(pl.multiple_of(j * chunk, chunk), chunk)
-            values_s[r, part, :] = jnp.zeros((chunk, HEAD), BF16)
-
+    cache = keys_ref.shape[1]
     total = total_ref[...]
     heads = out_ref.shape[2] // HEAD
     split = heads * HEAD
-    factor = lax.rsqrt(squares_ref[...] / D + EPSILON)
+    factor = lax.rsqrt(squares_ref[:, 0:1] / D + EPSILON)
     cos, sin = cos_ref[...], sin_ref[...]
 
     def turned(part):
@@ -197,14 +197,12 @@
         q_s[:, h, :] = turned(total[:, h * HEAD : (h + 1) * HEAD])
     scaling = HEAD ** (-0.5)
     position = lax.broadcasted_iota(jnp.int32, (1, cache), 1)
-    for r in range(here):
-        finish(keys_hbm, keys_s, key_sems, r)
     own = []
     for r in range(here):
         queries = q_s[r]
         scores = lax.dot_general(
             queries.astype(BF16),
-            keys_s[r],
+            keys_ref[r],
             (((1,), (1,)), ((), ())),
             preferred_element_type=F32,
         )
@@ -222,9 +220,7 @@
         weights.append((shifted / totals).astype(BF16))
         own_weights.append((own_term / totals).astype(BF16).astype(F32))
     for r in range(here):
-        finish(values_hbm, values_s, value_sems, r)
-    for r in range(here):
-        attended = jnp.dot(weights[r], values_s[r], preferred_element_type=F32)
+        attended = jnp.dot(weights[r], values_ref[r], preferred_element_type=F32)
         a_s[r] = attended + own_weights[r] * value_new[r : r + 1, :]
     for h in range(heads):
         part = a_s[:, h, :].astype(BF16)
@@ -233,24 +229,22 @@
 
 
 def wide_total(refs):
-    core_ref, mine_ref, near_ref, far_ref, other_ref = refs
-    half = far_ref.shape[0]
-    rows = mine_ref.shape[0]
+    core_ref, mine_ref, near_ref, other_near_ref, far_ref, other_far_ref = refs
     first = core_ref[0] == 0
-    far, far_other = far_ref[...].astype(F32), other_ref[pl.ds(rows, half), :].astype(F32)
+    far, far_other = far_ref[...].astype(F32), other_far_ref[...].astype(F32)
     opposite = jnp.concatenate(
         [jnp.where(first, far, far_other), jnp.where(first, far_other, far)], axis=0
     )
-    sides = near_ref[...].astype(F32) + other_ref[pl.ds(0, rows), :].astype(F32)
+    sides = near_ref[...].astype(F32) + other_near_ref[...].astype(F32)
     return (mine_ref[...].astype(F32) + opposite) + sides
 
 
 def gate_kernel(
-    core_ref, blocks_ref, mine_ref, near_ref, far_ref, other_ref, stream_ref, gain_ref, wg_ref,
-    wu_ref, middle_ref, out0_ref, out1_ref, out2_ref, out3_ref, sorted_s, normed_s,
+    core_ref, blocks_ref, mine_ref, near_ref, other_near_ref, far_ref, other_far_ref, stream_ref, gain_ref,
+    wg_ref, wu_ref, middle_ref, out0_ref, out1_ref, out2_ref, out3_ref, sorted_s, normed_s,
 ):
     middle_ref[...] = stream_ref[...] + wide_total(
-        (core_ref, mine_ref, near_ref, far_ref, other_ref)
+        (core_ref, mine_ref, near_ref, other_near_ref, far_ref, other_far_ref)
     )
     rows = middle_ref.shape[0] // PARTS
     for i in range(PARTS):
@@ -304,8 +298,10 @@
             out_ref[n, :, pl.ds(at, tile)] = hidden
 
 
-def finish_kernel(core_ref, mine_ref, near_ref, far_ref, other_ref, middle_ref, out_ref):
-    result = middle_ref[...] + wide_total((core_ref, mine_ref, near_ref, far_ref, other_ref))
+def finish_kernel(
+    core_ref, mine_ref, near_ref, other_near_ref, far_ref, other_far_ref, middle_ref, out_ref
+):
+    result = middle_ref[...] + wide_total((core_ref, mine_ref, near_ref, other_near_ref, far_ref, other_far_ref))
     rows = out_ref.shape[1] // PARTS
     for n in range(PARTS):
         for m in range(2):
@@ -339,9 +335,9 @@
     )
     near = lax.ppermute(mine, "wide", NEXT_Z)
     far = lax.ppermute(part, "wide", FAR_Z)
-    (both,) = call(pack_kernel, [((rows + half, width), BF16)], 4 * MIB, near, far)
-    other = lax.ppermute(both, "wide", CORE_SWAP)
-    return mine, near, far, other
+    other_near = lax.ppermute(near, "wide", CORE_SWAP)
+    other_far = lax.ppermute(far, "wide", CORE_SWAP)
+    return mine, near, other_near, far, other_far
 
 
 def body(
@@ -381,9 +377,10 @@
     cosines = jnp.concatenate([cosines, cosines], axis=-1)
     sines = jnp.concatenate([-sines, sines], axis=-1)
 
-    payload, stream = call(
+    held = (here, key_cache.shape[3], HEAD)
+    payload, stream, keys, values = call(
         project_kernel,
-        [((every, split + 3 * HEAD), F32), ((every, width), F32)],
+        [((every, split + 3 * HEAD), F32), ((every, width), F32)] + [(held, BF16)] * 2,
         8 * MIB,
         lengths,
         blocks,
@@ -395,17 +392,22 @@
         w_query,
         w_key,
         w_value,
+        key_cache.reshape(held),
+        value_cache.reshape(held),
         scalars=3,
-        far=5,
+        far=7,
+        kept=2,
         scratch=[pltpu.VMEM(hidden_in.shape, F32), pltpu.VMEM((1, width), F32)]
         + [pltpu.VMEM(w.shape, BF16) for w in (w_query, w_key, w_value)]
-        + [pltpu.SemaphoreType.DMA((5,))],
-    )
-    got = exchange(payload.astype(F16).reshape(PARTS, here, -1)).astype(F32)
-    norms = got[:, :, split + 2 * HEAD :][:, :, : len(NORM_SCALES)]
+        + [pltpu.SemaphoreType.DMA((5,))]
+        + [pltpu.SemaphoreType.DMA((here, held[1] // 512))] * 2,
+    )
+    got = exchange(payload.astype(F16).reshape(PARTS, here, -1))
+    last = split + 2 * HEAD
+    norms = got[:, :, last : last + len(NORM_SCALES)].astype(F32)
     norms = jnp.sum(norms * (1.0 / jnp.array(NORM_SCALES, F32)), axis=-1, keepdims=True)
-    total = jnp.sum(got[:, :, : split + 2 * HEAD] * (norms * (1.0 / REACH)), axis=0)
-    squares = jnp.sum(norms * norms, axis=0)
+    total = jnp.sum(got[:, :, :last].astype(F32) * (norms * (1.0 / REACH)), axis=0)
+    squares = jnp.sum(jnp.broadcast_to(norms * norms, (PARTS, here, LANES)), axis=0)
 
     (attended,) = call(
         attend_kernel,
@@ -416,14 +418,12 @@
         squares,
         cosines,
         sines,
-        key_cache.reshape(here, -1, HEAD),
-        value_cache.reshape(here, -1, HEAD),
+        keys,
+        values,
         scalars=1,
-        far=2,
+        held=2,
         scratch=[pltpu.VMEM((here, split // HEAD, HEAD), F32)] * 2
-        + [pltpu.VMEM((here * split // HEAD, key_cache.shape[3]), F32)]
-        + [pltpu.VMEM((here, key_cache.shape[3], HEAD), BF16)] * 2
-        + [pltpu.SemaphoreType.DMA((here, key_cache.shape[3] // 512))] * 2,
+        + [pltpu.VMEM((here * split // HEAD, held[1]), F32)],
     )
     gathered = exchange(attended).reshape(every, split)
     parts = sum_wide_parts(jnp.dot(gathered, w_out, preferred_element_type=F32), core_flag)

time: 109 us -> 107 us (0.982)
  waiting for transfers between devices: 33.2 us -> 30.8 us
  starting transfers between devices: 19 us -> 21.3 us
  Pallas kernels: 11.2 us -> 9.75 us
    ppermute x2, waiting for transfers between devices: 10.2 us -> 2 us  [sum_wide_parts(): far = lax.ppermute(part, 'wide', FAR_Z)]
    ppermute x2, waiting for transfers between devices: 0.01 us -> 5.86 us  [sum_wide_parts(): near = lax.ppermute(mine, 'wide', NEXT_Z)]
    ppermute x2 -> x4, starting transfers between devices: 2.95 us -> 5.27 us  [the longest x2 4.41 us: sum_wide_parts(): other_near = lax.ppermute(near, 'wide', CORE_SWAP)]
    pallas_call x10 -> x8, Pallas kernels: 11.2 us -> 9.75 us  [call(): pl.pallas_call(kernel, out_shape=[(jax.ShapeDtypeStruct if i < len(outs)...]
  transfers between devices with their start and end apart: 14 -> 16, of which waited for: 12 -> 13; matrix products, arithmetic and copies ran while one was open for 0% -> 0% of each run, Pallas kernels for 0% -> 0%
where the time goes in v4:
time: 107 us
  blocking collectives  42 us (39%)
  waiting for transfers between devices  30.8 us (29%)
  starting transfers between devices  21.3 us (20%)
  Pallas kernels  9.75 us (9%)
    all_to_all x3, blocking collectives, exchange(): return lax.all_to_all(payload, 'narrow', 0, 0, tiled=True)  42 us
    ppermute x6, waiting for transfers between devices, move(): lax.ppermute(block, ('wide', 'narrow'), plane_pairs(step, stage))  18.5 us
    pallas_call x8, Pallas kernels, call(): pl.pallas_call(kernel, out_shape=[(jax.ShapeDtypeStruct if i < len(outs)...  9.75 us
    ppermute x2, starting transfers between devices, sum_wide_parts(): lax.ppermute(partial, 'wide', CORE_SWAP)  7.24 us
    ppermute x2, waiting for transfers between devices, sum_wide_parts(): near = lax.ppermute(mine, 'wide', NEXT_Z)  5.86 us
    ppermute x2, starting transfers between devices, sum_wide_parts(): near = lax.ppermute(mine, 'wide', NEXT_Z)  4.42 us
    ppermute x2, starting transfers between devices, sum_wide_parts(): other_near = lax.ppermute(near, 'wide', CORE_SWAP)  4.41 us
    ppermute x6, starting transfers between devices, move(): lax.ppermute(block, ('wide', 'narrow'), plane_pairs(step, stage))  3.62 us
  transfers between devices with their start and end apart: 16, of which 13 were waited for; matrix products, arithmetic and copies ran while one was open for 0% of the time, Pallas kernels for 0%

profile of v4, /device:TPU:1, one launch (start us, length us, event | category | flops | bytes accessed | tf_op | source)
XLA Modules:
  0.0 106.8 jit_solution(9221161352454801146)
XLA Ops:
  0.0 0.8 reshape.38.len_ref
  1.1 3.7 %shard_map.136 = (f32[128,1408]{1,0:T(8,128)S(1)}, f32[128,512]{1,0:T(8,128)S(1)}, bf16[8,2048,128]{2,1,0:T(8,128)(2,1)S(1)}, bf16[8,2048,128]{2,1,0:T(8,128)(2,1)S(1)}) custom-call(s32[8]{0:T(128)S(1)} %reshape.38.len_ref, s32[16]{0:T(128)S(1)} %fusion.5.blocks_ref, s32[1]{0:T(128)} %bitcast.core_ref, f32[8,128]{1,0:T(8,128)S(1)} %get-tuple-element.44.cos_ref, ...), custom_call_target="tpu_custom_call" | custom-call | bytes 9971812 | tf_op jit(solution)/shard_map/pallas_call | solution.py:62
  4.9 15.9 %all_to_all.15 = f16[16,8,1408]{2,1,0:T(8,128)(2,1)S(1)} all-to-all(f16[16,8,1408]{2,1,0:T(8,128)(2,1)S(1)} %convert_bitcast_fusion), channel_id=1, replica_groups=mesh['wide'=8,'narrow'=16] {'narrow'}, dimensions={0} | all-to-all | bytes 720896 | tf_op jit(solution)/shard_map/all_to_all | solution.py:313
  21.1 2.5 %shard_map.137 = bf16[16,8,1024]{2,1,0:T(8,128)(2,1)S(1)} custom-call(s32[8]{0:T(128)S(1)} %reshape.38.len_ref, f32[8,1280]{1,0:T(8,128)S(1)} %multiply_reduce_fusion.total_ref, f32[8,128]{1,0:T(8,128)S(1)} %reduce_sum.32.squares_ref, f32[8,128]{1,0:T(8,128)S(1)} %get-tuple-element.44.cos_ref, f32[8,128]{1,0:T(8,128)S(1)} %get-tuple-element.45.sin_ref, ...), custom_call_target="tpu_custom_call" | custom-call | bytes 8441888 | tf_op jit(solution)/shard_map/pallas_call | solution.py:62
  23.6 10.4 %all_to_all.16 = bf16[16,8,1024]{2,1,0:T(8,128)(2,1)S(1)} all-to-all(bf16[16,8,1024]{2,1,0:T(8,128)(2,1)S(1)} %shard_map.137), channel_id=1, replica_groups=mesh['wide'=8,'narrow'=16] {'narrow'}, dimensions={0} | all-to-all | bytes 524288 | tf_op jit(solution)/shard_map/all_to_all | solution.py:313
  34.3 3.1 %collective-permute-start = (f32[128,512]{1,0:T(8,128)S(1)}, f32[128,512]{1,0:T(8,128)S(1)}, u32[]{:S(2)}, u32[]{:S(2)}) collective-permute-start(f32[128,512]{1,0:T(8,128)S(1)} %fusion.2.mine_ref), channel_id=1, source_target_pairs={{0,16},{16,0},{32,48},{48,32},{64,80},{80,64},{96,112},{112,96},{1... | collective-permute-start | bytes 786440 | tf_op jit(solution)/shard_map/ppermute | solution.py:333
  37.4 1.2 %collective-permute-done.other_ref = f32[128,512]{1,0:T(8,128)S(1)} collective-permute-done((f32[128,512]{1,0:T(8,128)S(1)}, f32[128,512]{1,0:T(8,128)S(1)}, u32[]{:S(2)}, u32[]{:S(2)}) %collective-permute-start) | collective-permute-done | bytes 262176 | tf_op jit(solution)/shard_map/ppermute | solution.py:333
  38.6 3.8 %collective-permute-start.1 = (bf16[128,512]{1,0:T(8,128)(2,1)S(1)}, bf16[128,512]{1,0:T(8,128)(2,1)S(1)}, u32[]{:S(2)}, u32[]{:S(2)}) collective-permute-start(bf16[128,512]{1,0:T(8,128)(2,1)S(1)} %get-tuple-element.25.mine_ref), channel_id=1, source_target_pairs={{0,32},{16,112},{32,64},{48,16},{64,96},{80,48},{96,0},{112,80},{1... | collective-permute-start | bytes 393224 | tf_op jit(solution)/shard_map/ppermute | solution.py:336
  42.5 3.3 %collective-permute-done.1.near_ref = bf16[128,512]{1,0:T(8,128)(2,1)S(1)} collective-permute-done((bf16[128,512]{1,0:T(8,128)(2,1)S(1)}, bf16[128,512]{1,0:T(8,128)(2,1)S(1)}, u32[]{:S(2)}, u32[]{:S(2)}) %collective-permute-start.1) | collective-permute-done | bytes 131104 | tf_op jit(solution)/shard_map/ppermute | solution.py:336
  46.1 2.0 %collective-permute-done.3.far_ref = bf16[64,512]{1,0:T(8,128)(2,1)S(1)} collective-permute-done((bf16[64,512]{1,0:T(8,128)(2,1)S(1)}, bf16[64,512]{1,0:T(8,128)(2,1)S(1)}, u32[]{:S(2)}, u32[]{:S(2)}) %collective-permute-start.3) | collective-permute-done | bytes 65568 | tf_op jit(solution)/shard_map/ppermute | solution.py:337
  48.1 0.9 collective-permute-start.4
  48.9 0.9 collective-permute-done.4.other_far_ref
  49.9 1.8 %shard_map.139 = (f32[128,512]{1,0:T(8,128)S(1)}, f32[32,7296]{1,0:T(8,128)S(1)}, f32[32,7296]{1,0:T(8,128)S(1)}, f32[32,7296]{1,0:T(8,128)S(1)}, f32[32,7296]{1,0:T(8,128)S(1)}) custom-call(s32[1]{0:T(128)} %bitcast.core_ref, s32[16]{0:T(128)S(1)} %fusion.5.blocks_ref, bf16[128,512]{1,0:T(8,128)(2,1)S(1)} %get-tuple-element.25.mine_ref, ...), custom_call_target="tpu_custom_call" | custom-call | bytes 8128580 | tf_op jit(solution)/shard_map/pallas_call | solution.py:62
  51.8 0.6 collective-permute-start.7
  52.4 1.0 collective-permute-start.6
  53.5 6.0 %collective-permute-done.7 = f16[32,7296]{1,0:T(8,128)(2,1)S(1)} collective-permute-done((f16[32,7296]{1,0:T(8,128)(2,1)S(1)}, f16[32,7296]{1,0:T(8,128)(2,1)S(1)}, u32[]{:S(2)}, u32[]{:S(2)}) %collective-permute-start.7) | collective-permute-done | bytes 466976 | tf_op jit(solution)/shard_map/ppermute | solution.py:320
  59.6 2.1 %collective-permute-done.6 = f16[32,7296]{1,0:T(8,128)(2,1)S(1)} collective-permute-done((f16[32,7296]{1,0:T(8,128)(2,1)S(1)}, f16[32,7296]{1,0:T(8,128)(2,1)S(1)}, u32[]{:S(2)}, u32[]{:S(2)}) %collective-permute-start.6) | collective-permute-done | bytes 466976 | tf_op jit(solution)/shard_map/ppermute | solution.py:320
  61.7 4.9 %collective-permute-done.5 = f16[32,7296]{1,0:T(8,128)(2,1)S(1)} collective-permute-done((f16[32,7296]{1,0:T(8,128)(2,1)S(1)}, f16[32,7296]{1,0:T(8,128)(2,1)S(1)}, u32[]{:S(2)}, u32[]{:S(2)}) %collective-permute-start.5) | collective-permute-done | bytes 466976 | tf_op jit(solution)/shard_map/ppermute | solution.py:320
  67.3 0.8 collective-permute-start.10
  68.1 1.1 %collective-permute-start.9 = (f16[8,7296]{1,0:T(8,128)(2,1)S(1)}, f16[8,7296]{1,0:T(8,128)(2,1)S(1)}, u32[]{:S(2)}, u32[]{:S(2)}) collective-permute-start(f16[8,7296]{1,0:T(8,128)(2,1)S(1)} %convert_element_type.64), channel_id=1, source_target_pairs={{0,8},{1,9},{2,10},{3,11},{4,12},{5,13},{6,14},{7,15},{8,0},{9,1},... | collective-permute-start | bytes 350216 | tf_op jit(solution)/shard_map/ppermute | solution.py:320
  69.3 1.8 %collective-permute-done.10 = f16[8,7296]{1,0:T(8,128)(2,1)S(1)} collective-permute-done((f16[8,7296]{1,0:T(8,128)(2,1)S(1)}, f16[8,7296]{1,0:T(8,128)(2,1)S(1)}, u32[]{:S(2)}, u32[]{:S(2)}) %collective-permute-start.10) | collective-permute-done | bytes 116768 | tf_op jit(solution)/shard_map/ppermute | solution.py:320
  71.1 2.2 %collective-permute-done.9 = f16[8,7296]{1,0:T(8,128)(2,1)S(1)} collective-permute-done((f16[8,7296]{1,0:T(8,128)(2,1)S(1)}, f16[8,7296]{1,0:T(8,128)(2,1)S(1)}, u32[]{:S(2)}, u32[]{:S(2)}) %collective-permute-start.9) | collective-permute-done | bytes 116768 | tf_op jit(solution)/shard_map/ppermute | solution.py:320
  73.3 1.5 %collective-permute-done.8 = f16[8,7296]{1,0:T(8,128)(2,1)S(1)} collective-permute-done((f16[8,7296]{1,0:T(8,128)(2,1)S(1)}, f16[8,7296]{1,0:T(8,128)(2,1)S(1)}, u32[]{:S(2)}, u32[]{:S(2)}) %collective-permute-start.8) | collective-permute-done | bytes 116768 | tf_op jit(solution)/shard_map/ppermute | solution.py:320
  75.1 15.7 %all_to_all.17 = bf16[16,8,3584]{2,1,0:T(8,128)(2,1)S(1)} all-to-all(bf16[16,8,3584]{2,1,0:T(8,128)(2,1)S(1)} %shard_map.141), channel_id=1, replica_groups=mesh['wide'=8,'narrow'=16] {'narrow'}, dimensions={0} | all-to-all | bytes 1835008 | tf_op jit(solution)/shard_map/all_to_all | solution.py:313
  90.8 0.6 fusion.mine_ref
  91.4 4.1 %collective-permute-start.11 = (f32[128,512]{1,0:T(8,128)S(1)}, f32[128,512]{1,0:T(8,128)S(1)}, u32[]{:S(2)}, u32[]{:S(2)}) collective-permute-start(f32[128,512]{1,0:T(8,128)S(1)} %fusion.mine_ref), channel_id=1, source_target_pairs={{0,16},{16,0},{32,48},{48,32},{64,80},{80,64},{96,112},{112,96},{1... | collective-permute-start | bytes 786440 | tf_op jit(solution)/shard_map/ppermute | solution.py:333
  95.6 1.2 %collective-permute-done.11.other_ref = f32[128,512]{1,0:T(8,128)S(1)} collective-permute-done((f32[128,512]{1,0:T(8,128)S(1)}, f32[128,512]{1,0:T(8,128)S(1)}, u32[]{:S(2)}, u32[]{:S(2)}) %collective-permute-start.11) | collective-permute-done | bytes 262176 | tf_op jit(solution)/shard_map/ppermute | solution.py:333
  97.4 0.8 collective-permute-start.14
  98.1 2.5 %collective-permute-done.12.near_ref = bf16[128,512]{1,0:T(8,128)(2,1)S(1)} collective-permute-done((bf16[128,512]{1,0:T(8,128)(2,1)S(1)}, bf16[128,512]{1,0:T(8,128)(2,1)S(1)}, u32[]{:S(2)}, u32[]{:S(2)}) %collective-permute-start.12) | collective-permute-done | bytes 131104 | tf_op jit(solution)/shard_map/ppermute | solution.py:336
  100.7 4.1 %collective-permute-start.13 = (bf16[128,512]{1,0:T(8,128)(2,1)S(1)}, bf16[128,512]{1,0:T(8,128)(2,1)S(1)}, u32[]{:S(2)}, u32[]{:S(2)}) collective-permute-start(bf16[128,512]{1,0:T(8,128)(2,1)S(1)} %collective-permute-done.12.near_ref), channel_id=1, source_target_pairs={{0,16},{16,0},{32,48},{48,32},{64,80},{80,64},{96,112},{112,96},{1... | collective-permute-start | bytes 393224 | tf_op jit(solution)/shard_map/ppermute | solution.py:338
  104.8 1.3 %collective-permute-done.15.other_far_ref = bf16[64,512]{1,0:T(8,128)(2,1)S(1)} collective-permute-done((bf16[64,512]{1,0:T(8,128)(2,1)S(1)}, bf16[64,512]{1,0:T(8,128)(2,1)S(1)}, u32[]{:S(2)}, u32[]{:S(2)}) %collective-permute-start.15) | collective-permute-done | bytes 65568 | tf_op jit(solution)/shard_map/ppermute | solution.py:339
  106.0 0.8 shard_map.143
  (48 shorter events, 3.3 us)
Async XLA Ops:
  0.0 34.0 %copy-start = (bf16[1024,512]{1,0:T(8,128)(2,1)S(1)}, bf16[1024,512]{1,0:T(8,128)(2,1)}, u32[]{:S(2)}) copy-start(bf16[1024,512]{1,0:T(8,128)(2,1)} %param.19) | copy-start | bytes 3145732
  1.1 19.7 %copy-start.5 = (f32[3]{0:T(128)S(1)}, f32[3]{0:T(128)}, u32[]{:S(2)}) copy-start(f32[3]{0:T(128)} %constant.94) | copy-start | bytes 40
  21.1 28.8 %copy-start.1 = (bf16[512,3584]{1,0:T(8,128)(2,1)S(1)}, bf16[512,3584]{1,0:T(8,128)(2,1)}, u32[]{:S(2)}) copy-start(bf16[512,3584]{1,0:T(8,128)(2,1)} %wg_ref.1) | copy-start | bytes 11010052
  21.1 28.8 %copy-start.2 = (bf16[512,3584]{1,0:T(8,128)(2,1)S(1)}, bf16[512,3584]{1,0:T(8,128)(2,1)}, u32[]{:S(2)}) copy-start(bf16[512,3584]{1,0:T(8,128)(2,1)} %wu_ref.1) | copy-start | bytes 11010052
  21.1 28.8 %copy-start.3 = (f32[512]{0:T(512)S(1)}, f32[512]{0:T(512)}, u32[]{:S(2)}) copy-start(f32[512]{0:T(512)} %param.20) | copy-start | bytes 6148
  34.3 4.3 %collective-permute-start = (f32[128,512]{1,0:T(8,128)S(1)}, f32[128,512]{1,0:T(8,128)S(1)}, u32[]{:S(2)}, u32[]{:S(2)}) collective-permute-start(f32[128,512]{1,0:T(8,128)S(1)} %fusion.2.mine_ref), channel_id=1, source_target_pairs={{0,16},{16,0},{32,48},{48,32},{64,80},{80,64},{96,112},{112,96},{1... | collective-permute-start | bytes 786440 | tf_op jit(solution)/shard_map/ppermute | solution.py:333
  38.6 7.1 %collective-permute-start.1 = (bf16[128,512]{1,0:T(8,128)(2,1)S(1)}, bf16[128,512]{1,0:T(8,128)(2,1)S(1)}, u32[]{:S(2)}, u32[]{:S(2)}) collective-permute-start(bf16[128,512]{1,0:T(8,128)(2,1)S(1)} %get-tuple-element.25.mine_ref), channel_id=1, source_target_pairs={{0,32},{16,112},{32,64},{48,16},{64,96},{80,48},{96,0},{112,80},{1... | collective-permute-start | bytes 393224 | tf_op jit(solution)/shard_map/ppermute | solution.py:336
  42.5 5.6 %collective-permute-start.3 = (bf16[64,512]{1,0:T(8,128)(2,1)S(1)}, bf16[64,512]{1,0:T(8,128)(2,1)S(1)}, u32[]{:S(2)}, u32[]{:S(2)}) collective-permute-start(bf16[64,512]{1,0:T(8,128)(2,1)S(1)} %get-tuple-element.26), channel_id=1, source_target_pairs={{0,64},{16,80},{32,96},{48,112},{64,0},{80,16},{96,32},{112,48},{1... | collective-permute-start | bytes 196616 | tf_op jit(solution)/shard_map/ppermute | solution.py:337
  45.8 4.1 %collective-permute-start.2 = (bf16[128,512]{1,0:T(8,128)(2,1)S(1)}, bf16[128,512]{1,0:T(8,128)(2,1)S(1)}, u32[]{:S(2)}, u32[]{:S(2)}) collective-permute-start(bf16[128,512]{1,0:T(8,128)(2,1)S(1)} %collective-permute-done.1.near_ref), channel_id=1, source_target_pairs={{0,16},{16,0},{32,48},{48,32},{64,80},{80,64},{96,112},{112,96},{1... | collective-permute-start | bytes 393224 | tf_op jit(solution)/shard_map/ppermute | solution.py:338
  48.1 1.8 %collective-permute-start.4 = (bf16[64,512]{1,0:T(8,128)(2,1)S(1)}, bf16[64,512]{1,0:T(8,128)(2,1)S(1)}, u32[]{:S(2)}, u32[]{:S(2)}) collective-permute-start(bf16[64,512]{1,0:T(8,128)(2,1)S(1)} %collective-permute-done.3.far_ref), channel_id=1, source_target_pairs={{0,16},{16,0},{32,48},{48,32},{64,80},{80,64},{96,112},{112,96},{1... | collective-permute-start | bytes 196616 | tf_op jit(solution)/shard_map/ppermute | solution.py:339
  51.8 7.8 %collective-permute-start.7 = (f16[32,7296]{1,0:T(8,128)(2,1)S(1)}, f16[32,7296]{1,0:T(8,128)(2,1)S(1)}, u32[]{:S(2)}, u32[]{:S(2)}) collective-permute-start(f16[32,7296]{1,0:T(8,128)(2,1)S(1)} %convert_element_type.60), channel_id=1, source_target_pairs={{0,3},{1,0},{2,1},{3,2},{4,7},{5,4},{6,5},{7,6},{8,11},{9,8},{10,9... | collective-permute-start | bytes 1400840 | tf_op jit(solution)/shard_map/ppermute | solution.py:320
  52.4 9.3 %collective-permute-start.6 = (f16[32,7296]{1,0:T(8,128)(2,1)S(1)}, f16[32,7296]{1,0:T(8,128)(2,1)S(1)}, u32[]{:S(2)}, u32[]{:S(2)}) collective-permute-start(f16[32,7296]{1,0:T(8,128)(2,1)S(1)} %convert_element_type.58), channel_id=1, source_target_pairs={{0,2},{1,3},{2,0},{3,1},{4,6},{5,7},{6,4},{7,5},{8,10},{9,11},{10,... | collective-permute-start | bytes 1400840 | tf_op jit(solution)/shard_map/ppermute | solution.py:320
  53.4 13.2 %collective-permute-start.5 = (f16[32,7296]{1,0:T(8,128)(2,1)S(1)}, f16[32,7296]{1,0:T(8,128)(2,1)S(1)}, u32[]{:S(2)}, u32[]{:S(2)}) collective-permute-start(f16[32,7296]{1,0:T(8,128)(2,1)S(1)} %convert_element_type.56), channel_id=1, source_target_pairs={{0,1},{1,2},{2,3},{3,0},{4,5},{5,6},{6,7},{7,4},{8,9},{9,10},{10,1... | collective-permute-start | bytes 1400840 | tf_op jit(solution)/shard_map/ppermute | solution.py:320
  67.2 23.5 %copy-start.4 = (bf16[3584,512]{1,0:T(8,128)(2,1)S(1)}, bf16[3584,512]{1,0:T(8,128)(2,1)}, u32[]{:S(2)}) copy-start(bf16[3584,512]{1,0:T(8,128)(2,1)} %param.23) | copy-start | bytes 11010052
  67.3 3.7 %collective-permute-start.10 = (f16[8,7296]{1,0:T(8,128)(2,1)S(1)}, f16[8,7296]{1,0:T(8,128)(2,1)S(1)}, u32[]{:S(2)}, u32[]{:S(2)}) collective-permute-start(f16[8,7296]{1,0:T(8,128)(2,1)S(1)} %convert_element_type.66), channel_id=1, source_target_pairs={{0,12},{1,13},{2,14},{3,15},{4,0},{5,1},{6,2},{7,3},{8,4},{9,5},{1... | collective-permute-start | bytes 350216 | tf_op jit(solution)/shard_map/ppermute | solution.py:320
  68.1 5.2 %collective-permute-start.9 = (f16[8,7296]{1,0:T(8,128)(2,1)S(1)}, f16[8,7296]{1,0:T(8,128)(2,1)S(1)}, u32[]{:S(2)}, u32[]{:S(2)}) collective-permute-start(f16[8,7296]{1,0:T(8,128)(2,1)S(1)} %convert_element_type.64), channel_id=1, source_target_pairs={{0,8},{1,9},{2,10},{3,11},{4,12},{5,13},{6,14},{7,15},{8,0},{9,1},... | collective-permute-start | bytes 350216 | tf_op jit(solution)/shard_map/ppermute | solution.py:320
  69.2 5.6 %collective-permute-start.8 = (f16[8,7296]{1,0:T(8,128)(2,1)S(1)}, f16[8,7296]{1,0:T(8,128)(2,1)S(1)}, u32[]{:S(2)}, u32[]{:S(2)}) collective-permute-start(f16[8,7296]{1,0:T(8,128)(2,1)S(1)} %convert_element_type.62), channel_id=1, source_target_pairs={{0,4},{1,5},{2,6},{3,7},{4,8},{5,9},{6,10},{7,11},{8,12},{9,13},{1... | collective-permute-start | bytes 350216 | tf_op jit(solution)/shard_map/ppermute | solution.py:320
  91.4 5.3 %collective-permute-start.11 = (f32[128,512]{1,0:T(8,128)S(1)}, f32[128,512]{1,0:T(8,128)S(1)}, u32[]{:S(2)}, u32[]{:S(2)}) collective-permute-start(f32[128,512]{1,0:T(8,128)S(1)} %fusion.mine_ref), channel_id=1, source_target_pairs={{0,16},{16,0},{32,48},{48,32},{64,80},{80,64},{96,112},{112,96},{1... | collective-permute-start | bytes 786440 | tf_op jit(solution)/shard_map/ppermute | solution.py:333
  96.8 3.9 %collective-permute-start.12 = (bf16[128,512]{1,0:T(8,128)(2,1)S(1)}, bf16[128,512]{1,0:T(8,128)(2,1)S(1)}, u32[]{:S(2)}, u32[]{:S(2)}) collective-permute-start(bf16[128,512]{1,0:T(8,128)(2,1)S(1)} %get-tuple-element.36.mine_ref), channel_id=1, source_target_pairs={{0,32},{16,112},{32,64},{48,16},{64,96},{80,48},{96,0},{112,80},{1... | collective-permute-start | bytes 393224 | tf_op jit(solution)/shard_map/ppermute | solution.py:336
  97.4 7.4 %collective-permute-start.14 = (bf16[64,512]{1,0:T(8,128)(2,1)S(1)}, bf16[64,512]{1,0:T(8,128)(2,1)S(1)}, u32[]{:S(2)}, u32[]{:S(2)}) collective-permute-start(bf16[64,512]{1,0:T(8,128)(2,1)S(1)} %get-tuple-element.37), channel_id=1, source_target_pairs={{0,64},{16,80},{32,96},{48,112},{64,0},{80,16},{96,32},{112,48},{1... | collective-permute-start | bytes 196616 | tf_op jit(solution)/shard_map/ppermute | solution.py:337
  100.7 5.4 %collective-permute-start.13 = (bf16[128,512]{1,0:T(8,128)(2,1)S(1)}, bf16[128,512]{1,0:T(8,128)(2,1)S(1)}, u32[]{:S(2)}, u32[]{:S(2)}) collective-permute-start(bf16[128,512]{1,0:T(8,128)(2,1)S(1)} %collective-permute-done.12.near_ref), channel_id=1, source_target_pairs={{0,16},{16,0},{32,48},{48,32},{64,80},{80,64},{96,112},{112,96},{1... | collective-permute-start | bytes 393224 | tf_op jit(solution)/shard_map/ppermute | solution.py:338
  104.8 1.3 %collective-permute-start.15 = (bf16[64,512]{1,0:T(8,128)(2,1)S(1)}, bf16[64,512]{1,0:T(8,128)(2,1)S(1)}, u32[]{:S(2)}, u32[]{:S(2)}) collective-permute-start(bf16[64,512]{1,0:T(8,128)(2,1)S(1)} %collective-permute-done.14.far_ref), channel_id=1, source_target_pairs={{0,16},{16,0},{32,48},{48,32},{64,80},{80,64},{96,112},{112,96},{1... | collective-permute-start | bytes 196616 | tf_op jit(solution)/shard_map/ppermute | solution.py:339

commit v5 on v4

--- a/solution.py
+++ b/solution.py
@@ -2,6 +2,7 @@
 
 import jax
 import jax.numpy as jnp
+import numpy as np
 from jax import lax
 from jax.experimental import pallas as pl
 from jax.experimental.pallas import tpu as pltpu
@@ -110,14 +111,19 @@
 
 
 def project_kernel(
-    len_ref, blocks_ref, core_ref, cos_ref, sin_ref, x_hbm, gain_hbm, wq_hbm, wk_hbm, wv_hbm,
-    keys_hbm, values_hbm, out_ref, stream_ref, keys_s, values_s, x_ref, gain_ref, wq_ref, wk_ref,
-    wv_ref, sems, key_sems, value_sems,
+    blocks_ref, core_ref, len_hbm, base_hbm, x_hbm, gain_hbm, wq_hbm, wk_hbm, wv_hbm, keys_hbm, values_hbm,
+    out_ref, stream_ref, cos_ref, sin_ref, lengths_ref, keys_s, values_s, len_s, base_ref, x_ref, gain_ref,
+    wq_ref, wk_ref, wv_ref, sems, key_sems, value_sems,
 ):
     pairs = ((x_hbm, x_ref), (gain_hbm, gain_ref), (wq_hbm, wq_ref), (wk_hbm, wk_ref), (wv_hbm, wv_ref))
     copies = [pltpu.make_async_copy(a, b, sems.at[i]) for i, (a, b) in enumerate(pairs)]
-    for copy in copies:
+    first = pltpu.make_async_copy(len_hbm, len_s, sems.at[5])
+    table = pltpu.make_async_copy(base_hbm, base_ref, sems.at[6])
+    for copy in (first, *copies, table):
         copy.start()
+    first.wait()
+    local = len_s.shape[1]
+    len_ref = [len_s[r // local, r % local] for r in range(keys_s.shape[0])]
     chunk = 512
     here, cache = keys_s.shape[0], keys_s.shape[1]
     counts = [lax.shift_right_logical(len_ref[r] + (chunk - 1), 9) for r in range(here)]
@@ -146,6 +152,17 @@
         def _(j):
             part = pl.ds(pl.multiple_of(j * chunk, chunk), chunk)
             values_s[r, part, :] = jnp.zeros((chunk, HEAD), BF16)
+    row = lax.broadcasted_iota(jnp.int32, lengths_ref.shape, 0)
+    lengths = jnp.zeros(lengths_ref.shape, jnp.int32)
+    for r in range(here):
+        lengths = jnp.where(row == r, len_ref[r], lengths)
+    lengths_ref[...] = lengths
+    table.wait()
+    angles = lengths.astype(F32) * base_ref[...]
+    lane = lax.broadcasted_iota(jnp.int32, lengths_ref.shape, 1)
+    cos_ref[...] = jnp.cos(angles)
+    sines = jnp.sin(angles)
+    sin_ref[...] = jnp.where(lane < HEAD // 2, -sines, sines)
     copies[0].wait()
     copies[1].wait()
     rows = x_ref.shape[1] // PARTS
@@ -177,7 +194,7 @@
 
 
 def attend_kernel(
-    len_ref, total_ref, squares_ref, cos_ref, sin_ref, keys_ref, values_ref, out_ref, q_s, a_s, s_s,
+    lengths_ref, total_ref, squares_ref, cos_ref, sin_ref, keys_ref, values_ref, out_ref, q_s, a_s, s_s,
 ):
     here = total_ref.shape[0]
     cache = keys_ref.shape[1]
@@ -207,7 +224,7 @@
             preferred_element_type=F32,
         )
         s_s[pl.ds(r * heads, heads), :] = jnp.where(
-            position < len_ref[r], scores * scaling, -jnp.inf
+            position < lengths_ref[pl.ds(r, 1), pl.ds(0, 1)], scores * scaling, -jnp.inf
         )
         own.append(jnp.sum(queries * key_new[r : r + 1, :], axis=-1, keepdims=True) * scaling)
     weights, own_weights = [], []
@@ -369,24 +386,20 @@
     blocks = ((at_y + step_y) % SIDE * SIDE + (at_x + step_x) % SIDE).astype(jnp.int32)
     core_flag = core.astype(jnp.int32)[None]
 
-    lengths = cache_len.reshape(here)
-    half = HEAD // 2
-    base = 500000.0 ** (-jnp.arange(half, dtype=F32) * 2.0 / HEAD)
-    angles = lengths.astype(F32)[:, None] * base[None]
-    cosines, sines = jnp.cos(angles), jnp.sin(angles)
-    cosines = jnp.concatenate([cosines, cosines], axis=-1)
-    sines = jnp.concatenate([-sines, sines], axis=-1)
-
+    base = 500000.0 ** (-np.arange(HEAD // 2) * 2.0 / HEAD)
+    base = np.concatenate([base, base])[None].astype(np.float32)
     held = (here, key_cache.shape[3], HEAD)
-    payload, stream, keys, values = call(
+    payload, stream, cosines, sines, lengths, keys, values = call(
         project_kernel,
-        [((every, split + 3 * HEAD), F32), ((every, width), F32)] + [(held, BF16)] * 2,
+        [((every, split + 3 * HEAD), F32), ((every, width), F32)]
+        + [((here, HEAD), F32)] * 2
+        + [((here, HEAD), jnp.int32)]
+        + [(held, BF16)] * 2,
         8 * MIB,
-        lengths,
         blocks,
         core_flag,
-        cosines,
-        sines,
+        cache_len,
+        jnp.asarray(base),
         hidden_in,
         attn_gain[None],
         w_query,
@@ -394,12 +407,13 @@
         w_value,
         key_cache.reshape(held),
         value_cache.reshape(held),
-        scalars=3,
-        far=7,
+        scalars=2,
+        far=9,
         kept=2,
-        scratch=[pltpu.VMEM(hidden_in.shape, F32), pltpu.VMEM((1, width), F32)]
+        scratch=[pltpu.SMEM(cache_len.shape, jnp.int32), pltpu.VMEM((1, HEAD), F32)]
+        + [pltpu.VMEM(hidden_in.shape, F32), pltpu.VMEM((1, width), F32)]
         + [pltpu.VMEM(w.shape, BF16) for w in (w_query, w_key, w_value)]
-        + [pltpu.SemaphoreType.DMA((5,))]
+        + [pltpu.SemaphoreType.DMA((7,))]
         + [pltpu.SemaphoreType.DMA((here, held[1] // 512))] * 2,
     )
     got = exchange(payload.astype(F16).reshape(PARTS, here, -1))
@@ -420,7 +434,6 @@
         sines,
         keys,
         values,
-        scalars=1,
         held=2,
         scratch=[pltpu.VMEM((here, split // HEAD, HEAD), F32)] * 2
         + [pltpu.VMEM((here * split // HEAD, held[1]), F32)],

time: 107 us -> 106 us (level)
  no operation moved by 1% of the time
where the time goes in v5:
time: 106 us
  blocking collectives  42.6 us (40%)
  waiting for transfers between devices  30.8 us (29%)
  starting transfers between devices  21.3 us (20%)
  Pallas kernels  9.15 us (9%)
    all_to_all x3, blocking collectives, exchange(): return lax.all_to_all(payload, 'narrow', 0, 0, tiled=True)  42.6 us
    ppermute x6, waiting for transfers between devices, move(): lax.ppermute(block, ('wide', 'narrow'), plane_pairs(step, stage))  18.5 us
    pallas_call x8, Pallas kernels, call(): pl.pallas_call(kernel, out_shape=[(jax.ShapeDtypeStruct if i < len(outs)...  9.15 us
    ppermute x2, starting transfers between devices, sum_wide_parts(): lax.ppermute(partial, 'wide', CORE_SWAP)  7.23 us
    ppermute x2, waiting for transfers between devices, sum_wide_parts(): near = lax.ppermute(mine, 'wide', NEXT_Z)  5.86 us
    ppermute x2, starting transfers between devices, sum_wide_parts(): near = lax.ppermute(mine, 'wide', NEXT_Z)  4.41 us
    ppermute x2, starting transfers between devices, sum_wide_parts(): other_near = lax.ppermute(near, 'wide', CORE_SWAP)  4.41 us
    ppermute x6, starting transfers between devices, move(): lax.ppermute(block, ('wide', 'narrow'), plane_pairs(step, stage))  3.61 us
  transfers between devices with their start and end apart: 16, of which 13 were waited for; matrix products, arithmetic and copies ran while one was open for 0% of the time, Pallas kernels for 0%

profile of v5, /device:TPU:1, one launch (start us, length us, event | category | flops | bytes accessed | tf_op | source)
XLA Modules:
  0.0 105.8 jit_solution(13193398279283679483)
XLA Ops:
  0.0 3.7 %shard_map.145 = (f32[128,1408]{1,0:T(8,128)S(1)}, f32[128,512]{1,0:T(8,128)S(1)}, f32[8,128]{1,0:T(8,128)S(1)}, f32[8,128]{1,0:T(8,128)S(1)}, s32[8,128]{1,0:T(...) custom-call(s32[16]{0:T(128)S(1)} %fusion.4.blocks_ref, s32[1]{0:T(128)} %bitcast.core_ref, ...), custom_call_target="tpu_custom_call" | custom-call | bytes 9964132 | tf_op jit(solution)/shard_map/pallas_call | solution.py:63
  3.7 16.4 %all_to_all.15 = f16[16,8,1408]{2,1,0:T(8,128)(2,1)S(1)} all-to-all(f16[16,8,1408]{2,1,0:T(8,128)(2,1)S(1)} %convert_bitcast_fusion), channel_id=1, replica_groups=mesh['wide'=8,'narrow'=16] {'narrow'}, dimensions={0} | all-to-all | bytes 720896 | tf_op jit(solution)/shard_map/all_to_all | solution.py:330
  20.4 2.0 %shard_map.146 = bf16[16,8,1024]{2,1,0:T(8,128)(2,1)S(1)} custom-call(s32[8,128]{1,0:T(8,128)S(1)} %get-tuple-element.25.lengths_ref, f32[8,1280]{1,0:T(8,128)S(1)} %multiply_reduce_fusion.total_ref, f32[8,128]{1,0:T(8,128)S(1)} %reduce_sum.32.squares_ref, f32[8,128]{1,0:T(8,128)S(1)} %get-tuple-element.27.cos_ref, f32[8,128]{1,0:T(8,128)S(1)} %get-tuple-element.28.sin_ref, ...), custom_call_target="tpu_custom_call" | custom-call | bytes 8445952 | tf_op jit(solution)/shard_map/pallas_call | solution.py:63
  22.4 10.5 %all_to_all.16 = bf16[16,8,1024]{2,1,0:T(8,128)(2,1)S(1)} all-to-all(bf16[16,8,1024]{2,1,0:T(8,128)(2,1)S(1)} %shard_map.146), channel_id=1, replica_groups=mesh['wide'=8,'narrow'=16] {'narrow'}, dimensions={0} | all-to-all | bytes 524288 | tf_op jit(solution)/shard_map/all_to_all | solution.py:330
  33.3 3.1 %collective-permute-start = (f32[128,512]{1,0:T(8,128)S(1)}, f32[128,512]{1,0:T(8,128)S(1)}, u32[]{:S(2)}, u32[]{:S(2)}) collective-permute-start(f32[128,512]{1,0:T(8,128)S(1)} %fusion.2.mine_ref), channel_id=1, source_target_pairs={{0,16},{16,0},{32,48},{48,32},{64,80},{80,64},{96,112},{112,96},{1... | collective-permute-start | bytes 786440 | tf_op jit(solution)/shard_map/ppermute | solution.py:350
  36.4 1.2 %collective-permute-done.other_ref = f32[128,512]{1,0:T(8,128)S(1)} collective-permute-done((f32[128,512]{1,0:T(8,128)S(1)}, f32[128,512]{1,0:T(8,128)S(1)}, u32[]{:S(2)}, u32[]{:S(2)}) %collective-permute-start) | collective-permute-done | bytes 262176 | tf_op jit(solution)/shard_map/ppermute | solution.py:350
  37.6 3.8 %collective-permute-start.1 = (bf16[128,512]{1,0:T(8,128)(2,1)S(1)}, bf16[128,512]{1,0:T(8,128)(2,1)S(1)}, u32[]{:S(2)}, u32[]{:S(2)}) collective-permute-start(bf16[128,512]{1,0:T(8,128)(2,1)S(1)} %get-tuple-element.31.mine_ref), channel_id=1, source_target_pairs={{0,32},{16,112},{32,64},{48,16},{64,96},{80,48},{96,0},{112,80},{1... | collective-permute-start | bytes 393224 | tf_op jit(solution)/shard_map/ppermute | solution.py:353
  41.4 3.3 %collective-permute-done.1.near_ref = bf16[128,512]{1,0:T(8,128)(2,1)S(1)} collective-permute-done((bf16[128,512]{1,0:T(8,128)(2,1)S(1)}, bf16[128,512]{1,0:T(8,128)(2,1)S(1)}, u32[]{:S(2)}, u32[]{:S(2)}) %collective-permute-start.1) | collective-permute-done | bytes 131104 | tf_op jit(solution)/shard_map/ppermute | solution.py:353
  45.0 2.0 %collective-permute-done.3.far_ref = bf16[64,512]{1,0:T(8,128)(2,1)S(1)} collective-permute-done((bf16[64,512]{1,0:T(8,128)(2,1)S(1)}, bf16[64,512]{1,0:T(8,128)(2,1)S(1)}, u32[]{:S(2)}, u32[]{:S(2)}) %collective-permute-start.3) | collective-permute-done | bytes 65568 | tf_op jit(solution)/shard_map/ppermute | solution.py:354
  47.0 0.9 collective-permute-start.4
  47.9 0.9 collective-permute-done.4.other_far_ref
  48.8 1.8 %shard_map.148 = (f32[128,512]{1,0:T(8,128)S(1)}, f32[32,7296]{1,0:T(8,128)S(1)}, f32[32,7296]{1,0:T(8,128)S(1)}, f32[32,7296]{1,0:T(8,128)S(1)}, f32[32,7296]{1,0:T(8,128)S(1)}) custom-call(s32[1]{0:T(128)} %bitcast.core_ref, s32[16]{0:T(128)S(1)} %fusion.4.blocks_ref, bf16[128,512]{1,0:T(8,128)(2,1)S(1)} %get-tuple-element.31.mine_ref, ...), custom_call_target="tpu_custom_call" | custom-call | bytes 8128580 | tf_op jit(solution)/shard_map/pallas_call | solution.py:63
  50.7 0.6 collective-permute-start.7
  51.4 1.0 collective-permute-start.6
  52.5 6.0 %collective-permute-done.7 = f16[32,7296]{1,0:T(8,128)(2,1)S(1)} collective-permute-done((f16[32,7296]{1,0:T(8,128)(2,1)S(1)}, f16[32,7296]{1,0:T(8,128)(2,1)S(1)}, u32[]{:S(2)}, u32[]{:S(2)}) %collective-permute-start.7) | collective-permute-done | bytes 466976 | tf_op jit(solution)/shard_map/ppermute | solution.py:337
  58.6 2.1 %collective-permute-done.6 = f16[32,7296]{1,0:T(8,128)(2,1)S(1)} collective-permute-done((f16[32,7296]{1,0:T(8,128)(2,1)S(1)}, f16[32,7296]{1,0:T(8,128)(2,1)S(1)}, u32[]{:S(2)}, u32[]{:S(2)}) %collective-permute-start.6) | collective-permute-done | bytes 466976 | tf_op jit(solution)/shard_map/ppermute | solution.py:337
  60.7 4.9 %collective-permute-done.5 = f16[32,7296]{1,0:T(8,128)(2,1)S(1)} collective-permute-done((f16[32,7296]{1,0:T(8,128)(2,1)S(1)}, f16[32,7296]{1,0:T(8,128)(2,1)S(1)}, u32[]{:S(2)}, u32[]{:S(2)}) %collective-permute-start.5) | collective-permute-done | bytes 466976 | tf_op jit(solution)/shard_map/ppermute | solution.py:337
  66.3 0.8 collective-permute-start.10
  67.0 1.1 %collective-permute-start.9 = (f16[8,7296]{1,0:T(8,128)(2,1)S(1)}, f16[8,7296]{1,0:T(8,128)(2,1)S(1)}, u32[]{:S(2)}, u32[]{:S(2)}) collective-permute-start(f16[8,7296]{1,0:T(8,128)(2,1)S(1)} %convert_element_type.56), channel_id=1, source_target_pairs={{0,8},{1,9},{2,10},{3,11},{4,12},{5,13},{6,14},{7,15},{8,0},{9,1},... | collective-permute-start | bytes 350216 | tf_op jit(solution)/shard_map/ppermute | solution.py:337
  68.2 1.8 %collective-permute-done.10 = f16[8,7296]{1,0:T(8,128)(2,1)S(1)} collective-permute-done((f16[8,7296]{1,0:T(8,128)(2,1)S(1)}, f16[8,7296]{1,0:T(8,128)(2,1)S(1)}, u32[]{:S(2)}, u32[]{:S(2)}) %collective-permute-start.10) | collective-permute-done | bytes 116768 | tf_op jit(solution)/shard_map/ppermute | solution.py:337
  70.0 2.2 %collective-permute-done.9 = f16[8,7296]{1,0:T(8,128)(2,1)S(1)} collective-permute-done((f16[8,7296]{1,0:T(8,128)(2,1)S(1)}, f16[8,7296]{1,0:T(8,128)(2,1)S(1)}, u32[]{:S(2)}, u32[]{:S(2)}) %collective-permute-start.9) | collective-permute-done | bytes 116768 | tf_op jit(solution)/shard_map/ppermute | solution.py:337
  72.3 1.5 %collective-permute-done.8 = f16[8,7296]{1,0:T(8,128)(2,1)S(1)} collective-permute-done((f16[8,7296]{1,0:T(8,128)(2,1)S(1)}, f16[8,7296]{1,0:T(8,128)(2,1)S(1)}, u32[]{:S(2)}, u32[]{:S(2)}) %collective-permute-start.8) | collective-permute-done | bytes 116768 | tf_op jit(solution)/shard_map/ppermute | solution.py:337
  74.1 15.7 %all_to_all.17 = bf16[16,8,3584]{2,1,0:T(8,128)(2,1)S(1)} all-to-all(bf16[16,8,3584]{2,1,0:T(8,128)(2,1)S(1)} %shard_map.150), channel_id=1, replica_groups=mesh['wide'=8,'narrow'=16] {'narrow'}, dimensions={0} | all-to-all | bytes 1835008 | tf_op jit(solution)/shard_map/all_to_all | solution.py:330
  89.8 0.6 fusion.mine_ref
  90.4 4.1 %collective-permute-start.11 = (f32[128,512]{1,0:T(8,128)S(1)}, f32[128,512]{1,0:T(8,128)S(1)}, u32[]{:S(2)}, u32[]{:S(2)}) collective-permute-start(f32[128,512]{1,0:T(8,128)S(1)} %fusion.mine_ref), channel_id=1, source_target_pairs={{0,16},{16,0},{32,48},{48,32},{64,80},{80,64},{96,112},{112,96},{1... | collective-permute-start | bytes 786440 | tf_op jit(solution)/shard_map/ppermute | solution.py:350
  94.5 1.2 %collective-permute-done.11.other_ref = f32[128,512]{1,0:T(8,128)S(1)} collective-permute-done((f32[128,512]{1,0:T(8,128)S(1)}, f32[128,512]{1,0:T(8,128)S(1)}, u32[]{:S(2)}, u32[]{:S(2)}) %collective-permute-start.11) | collective-permute-done | bytes 262176 | tf_op jit(solution)/shard_map/ppermute | solution.py:350
  95.7 0.6 collective-permute-start.12
  96.3 0.8 collective-permute-start.14
  97.1 2.5 %collective-permute-done.12.near_ref = bf16[128,512]{1,0:T(8,128)(2,1)S(1)} collective-permute-done((bf16[128,512]{1,0:T(8,128)(2,1)S(1)}, bf16[128,512]{1,0:T(8,128)(2,1)S(1)}, u32[]{:S(2)}, u32[]{:S(2)}) %collective-permute-start.12) | collective-permute-done | bytes 131104 | tf_op jit(solution)/shard_map/ppermute | solution.py:353
  99.6 4.1 %collective-permute-start.13 = (bf16[128,512]{1,0:T(8,128)(2,1)S(1)}, bf16[128,512]{1,0:T(8,128)(2,1)S(1)}, u32[]{:S(2)}, u32[]{:S(2)}) collective-permute-start(bf16[128,512]{1,0:T(8,128)(2,1)S(1)} %collective-permute-done.12.near_ref), channel_id=1, source_target_pairs={{0,16},{16,0},{32,48},{48,32},{64,80},{80,64},{96,112},{112,96},{1... | collective-permute-start | bytes 393224 | tf_op jit(solution)/shard_map/ppermute | solution.py:355
  103.7 1.3 %collective-permute-done.15.other_far_ref = bf16[64,512]{1,0:T(8,128)(2,1)S(1)} collective-permute-done((bf16[64,512]{1,0:T(8,128)(2,1)S(1)}, bf16[64,512]{1,0:T(8,128)(2,1)S(1)}, u32[]{:S(2)}, u32[]{:S(2)}) %collective-permute-start.15) | collective-permute-done | bytes 65568 | tf_op jit(solution)/shard_map/ppermute | solution.py:356
  105.0 0.8 shard_map.152
  (43 shorter events, 2.5 us)
Async XLA Ops:
  0.0 32.9 %copy-start = (bf16[1024,512]{1,0:T(8,128)(2,1)S(1)}, bf16[1024,512]{1,0:T(8,128)(2,1)}, u32[]{:S(2)}) copy-start(bf16[1024,512]{1,0:T(8,128)(2,1)} %param.20) | copy-start | bytes 3145732
  0.0 20.1 %copy-start.5 = (f32[3]{0:T(128)S(1)}, f32[3]{0:T(128)}, u32[]{:S(2)}) copy-start(f32[3]{0:T(128)} %constant.90) | copy-start | bytes 40
  20.4 28.4 %copy-start.1 = (bf16[512,3584]{1,0:T(8,128)(2,1)S(1)}, bf16[512,3584]{1,0:T(8,128)(2,1)}, u32[]{:S(2)}) copy-start(bf16[512,3584]{1,0:T(8,128)(2,1)} %wg_ref.1) | copy-start | bytes 11010052
  20.4 28.4 %copy-start.2 = (bf16[512,3584]{1,0:T(8,128)(2,1)S(1)}, bf16[512,3584]{1,0:T(8,128)(2,1)}, u32[]{:S(2)}) copy-start(bf16[512,3584]{1,0:T(8,128)(2,1)} %wu_ref.1) | copy-start | bytes 11010052
  20.4 28.4 %copy-start.3 = (f32[512]{0:T(512)S(1)}, f32[512]{0:T(512)}, u32[]{:S(2)}) copy-start(f32[512]{0:T(512)} %param.21) | copy-start | bytes 6148
  33.3 4.3 %collective-permute-start = (f32[128,512]{1,0:T(8,128)S(1)}, f32[128,512]{1,0:T(8,128)S(1)}, u32[]{:S(2)}, u32[]{:S(2)}) collective-permute-start(f32[128,512]{1,0:T(8,128)S(1)} %fusion.2.mine_ref), channel_id=1, source_target_pairs={{0,16},{16,0},{32,48},{48,32},{64,80},{80,64},{96,112},{112,96},{1... | collective-permute-start | bytes 786440 | tf_op jit(solution)/shard_map/ppermute | solution.py:350
  37.6 7.1 %collective-permute-start.1 = (bf16[128,512]{1,0:T(8,128)(2,1)S(1)}, bf16[128,512]{1,0:T(8,128)(2,1)S(1)}, u32[]{:S(2)}, u32[]{:S(2)}) collective-permute-start(bf16[128,512]{1,0:T(8,128)(2,1)S(1)} %get-tuple-element.31.mine_ref), channel_id=1, source_target_pairs={{0,32},{16,112},{32,64},{48,16},{64,96},{80,48},{96,0},{112,80},{1... | collective-permute-start | bytes 393224 | tf_op jit(solution)/shard_map/ppermute | solution.py:353
  41.4 5.6 %collective-permute-start.3 = (bf16[64,512]{1,0:T(8,128)(2,1)S(1)}, bf16[64,512]{1,0:T(8,128)(2,1)S(1)}, u32[]{:S(2)}, u32[]{:S(2)}) collective-permute-start(bf16[64,512]{1,0:T(8,128)(2,1)S(1)} %get-tuple-element.32), channel_id=1, source_target_pairs={{0,64},{16,80},{32,96},{48,112},{64,0},{80,16},{96,32},{112,48},{1... | collective-permute-start | bytes 196616 | tf_op jit(solution)/shard_map/ppermute | solution.py:354
  44.7 4.1 %collective-permute-start.2 = (bf16[128,512]{1,0:T(8,128)(2,1)S(1)}, bf16[128,512]{1,0:T(8,128)(2,1)S(1)}, u32[]{:S(2)}, u32[]{:S(2)}) collective-permute-start(bf16[128,512]{1,0:T(8,128)(2,1)S(1)} %collective-permute-done.1.near_ref), channel_id=1, source_target_pairs={{0,16},{16,0},{32,48},{48,32},{64,80},{80,64},{96,112},{112,96},{1... | collective-permute-start | bytes 393224 | tf_op jit(solution)/shard_map/ppermute | solution.py:355
  47.0 1.8 %collective-permute-start.4 = (bf16[64,512]{1,0:T(8,128)(2,1)S(1)}, bf16[64,512]{1,0:T(8,128)(2,1)S(1)}, u32[]{:S(2)}, u32[]{:S(2)}) collective-permute-start(bf16[64,512]{1,0:T(8,128)(2,1)S(1)} %collective-permute-done.3.far_ref), channel_id=1, source_target_pairs={{0,16},{16,0},{32,48},{48,32},{64,80},{80,64},{96,112},{112,96},{1... | collective-permute-start | bytes 196616 | tf_op jit(solution)/shard_map/ppermute | solution.py:356
  50.7 7.8 %collective-permute-start.7 = (f16[32,7296]{1,0:T(8,128)(2,1)S(1)}, f16[32,7296]{1,0:T(8,128)(2,1)S(1)}, u32[]{:S(2)}, u32[]{:S(2)}) collective-permute-start(f16[32,7296]{1,0:T(8,128)(2,1)S(1)} %convert_element_type.52), channel_id=1, source_target_pairs={{0,3},{1,0},{2,1},{3,2},{4,7},{5,4},{6,5},{7,6},{8,11},{9,8},{10,9... | collective-permute-start | bytes 1400840 | tf_op jit(solution)/shard_map/ppermute | solution.py:337
  51.4 9.3 %collective-permute-start.6 = (f16[32,7296]{1,0:T(8,128)(2,1)S(1)}, f16[32,7296]{1,0:T(8,128)(2,1)S(1)}, u32[]{:S(2)}, u32[]{:S(2)}) collective-permute-start(f16[32,7296]{1,0:T(8,128)(2,1)S(1)} %convert_element_type.50), channel_id=1, source_target_pairs={{0,2},{1,3},{2,0},{3,1},{4,6},{5,7},{6,4},{7,5},{8,10},{9,11},{10,... | collective-permute-start | bytes 1400840 | tf_op jit(solution)/shard_map/ppermute | solution.py:337
  52.4 13.2 %collective-permute-start.5 = (f16[32,7296]{1,0:T(8,128)(2,1)S(1)}, f16[32,7296]{1,0:T(8,128)(2,1)S(1)}, u32[]{:S(2)}, u32[]{:S(2)}) collective-permute-start(f16[32,7296]{1,0:T(8,128)(2,1)S(1)} %convert_element_type.48), channel_id=1, source_target_pairs={{0,1},{1,2},{2,3},{3,0},{4,5},{5,6},{6,7},{7,4},{8,9},{9,10},{10,1... | collective-permute-start | bytes 1400840 | tf_op jit(solution)/shard_map/ppermute | solution.py:337
  66.2 23.6 %copy-start.4 = (bf16[3584,512]{1,0:T(8,128)(2,1)S(1)}, bf16[3584,512]{1,0:T(8,128)(2,1)}, u32[]{:S(2)}) copy-start(bf16[3584,512]{1,0:T(8,128)(2,1)} %param.24) | copy-start | bytes 11010052
  66.3 3.7 %collective-permute-start.10 = (f16[8,7296]{1,0:T(8,128)(2,1)S(1)}, f16[8,7296]{1,0:T(8,128)(2,1)S(1)}, u32[]{:S(2)}, u32[]{:S(2)}) collective-permute-start(f16[8,7296]{1,0:T(8,128)(2,1)S(1)} %convert_element_type.58), channel_id=1, source_target_pairs={{0,12},{1,13},{2,14},{3,15},{4,0},{5,1},{6,2},{7,3},{8,4},{9,5},{1... | collective-permute-start | bytes 350216 | tf_op jit(solution)/shard_map/ppermute | solution.py:337
  67.0 5.2 %collective-permute-start.9 = (f16[8,7296]{1,0:T(8,128)(2,1)S(1)}, f16[8,7296]{1,0:T(8,128)(2,1)S(1)}, u32[]{:S(2)}, u32[]{:S(2)}) collective-permute-start(f16[8,7296]{1,0:T(8,128)(2,1)S(1)} %convert_element_type.56), channel_id=1, source_target_pairs={{0,8},{1,9},{2,10},{3,11},{4,12},{5,13},{6,14},{7,15},{8,0},{9,1},... | collective-permute-start | bytes 350216 | tf_op jit(solution)/shard_map/ppermute | solution.py:337
  68.1 5.6 %collective-permute-start.8 = (f16[8,7296]{1,0:T(8,128)(2,1)S(1)}, f16[8,7296]{1,0:T(8,128)(2,1)S(1)}, u32[]{:S(2)}, u32[]{:S(2)}) collective-permute-start(f16[8,7296]{1,0:T(8,128)(2,1)S(1)} %convert_element_type.54), channel_id=1, source_target_pairs={{0,4},{1,5},{2,6},{3,7},{4,8},{5,9},{6,10},{7,11},{8,12},{9,13},{1... | collective-permute-start | bytes 350216 | tf_op jit(solution)/shard_map/ppermute | solution.py:337
  90.4 5.3 %collective-permute-start.11 = (f32[128,512]{1,0:T(8,128)S(1)}, f32[128,512]{1,0:T(8,128)S(1)}, u32[]{:S(2)}, u32[]{:S(2)}) collective-permute-start(f32[128,512]{1,0:T(8,128)S(1)} %fusion.mine_ref), channel_id=1, source_target_pairs={{0,16},{16,0},{32,48},{48,32},{64,80},{80,64},{96,112},{112,96},{1... | collective-permute-start | bytes 786440 | tf_op jit(solution)/shard_map/ppermute | solution.py:350
  95.7 3.9 %collective-permute-start.12 = (bf16[128,512]{1,0:T(8,128)(2,1)S(1)}, bf16[128,512]{1,0:T(8,128)(2,1)S(1)}, u32[]{:S(2)}, u32[]{:S(2)}) collective-permute-start(bf16[128,512]{1,0:T(8,128)(2,1)S(1)} %get-tuple-element.42.mine_ref), channel_id=1, source_target_pairs={{0,32},{16,112},{32,64},{48,16},{64,96},{80,48},{96,0},{112,80},{1... | collective-permute-start | bytes 393224 | tf_op jit(solution)/shard_map/ppermute | solution.py:353
  96.3 7.4 %collective-permute-start.14 = (bf16[64,512]{1,0:T(8,128)(2,1)S(1)}, bf16[64,512]{1,0:T(8,128)(2,1)S(1)}, u32[]{:S(2)}, u32[]{:S(2)}) collective-permute-start(bf16[64,512]{1,0:T(8,128)(2,1)S(1)} %get-tuple-element.43), channel_id=1, source_target_pairs={{0,64},{16,80},{32,96},{48,112},{64,0},{80,16},{96,32},{112,48},{1... | collective-permute-start | bytes 196616 | tf_op jit(solution)/shard_map/ppermute | solution.py:354
  99.6 5.4 %collective-permute-start.13 = (bf16[128,512]{1,0:T(8,128)(2,1)S(1)}, bf16[128,512]{1,0:T(8,128)(2,1)S(1)}, u32[]{:S(2)}, u32[]{:S(2)}) collective-permute-start(bf16[128,512]{1,0:T(8,128)(2,1)S(1)} %collective-permute-done.12.near_ref), channel_id=1, source_target_pairs={{0,16},{16,0},{32,48},{48,32},{64,80},{80,64},{96,112},{112,96},{1... | collective-permute-start | bytes 393224 | tf_op jit(solution)/shard_map/ppermute | solution.py:355
  103.7 1.3 %collective-permute-start.15 = (bf16[64,512]{1,0:T(8,128)(2,1)S(1)}, bf16[64,512]{1,0:T(8,128)(2,1)S(1)}, u32[]{:S(2)}, u32[]{:S(2)}) collective-permute-start(bf16[64,512]{1,0:T(8,128)(2,1)S(1)} %collective-permute-done.14.far_ref), channel_id=1, source_target_pairs={{0,16},{16,0},{32,48},{48,32},{64,80},{80,64},{96,112},{112,96},{1... | collective-permute-start | bytes 196616 | tf_op jit(solution)/shard_map/ppermute | solution.py:356

commit v6 on v5

--- a/solution.py
+++ b/solution.py
@@ -124,9 +124,9 @@
     first.wait()
     local = len_s.shape[1]
     len_ref = [len_s[r // local, r % local] for r in range(keys_s.shape[0])]
-    chunk = 512
+    chunk = 256
     here, cache = keys_s.shape[0], keys_s.shape[1]
-    counts = [lax.shift_right_logical(len_ref[r] + (chunk - 1), 9) for r in range(here)]
+    counts = [lax.shift_right_logical(len_ref[r] + (chunk - 1), 8) for r in range(here)]
 
     def fetch(far, near, sems, r, j):
         part = pl.ds(pl.multiple_of(j * chunk, chunk), chunk)
@@ -187,7 +187,7 @@
 
 
 def total_kernel(core_ref, mine_ref, other_ref, total_ref, half_ref):
-    total = (mine_ref[...] + other_ref[...]).astype(BF16)
+    total = (mine_ref[...].astype(F32) + other_ref[...].astype(F32)).astype(BF16)
     total_ref[...] = total
     half = half_ref.shape[0]
     half_ref[...] = jnp.where(core_ref[0] == 0, total[:half, :], total[half:, :])
@@ -414,7 +414,7 @@
         + [pltpu.VMEM(hidden_in.shape, F32), pltpu.VMEM((1, width), F32)]
         + [pltpu.VMEM(w.shape, BF16) for w in (w_query, w_key, w_value)]
         + [pltpu.SemaphoreType.DMA((7,))]
-        + [pltpu.SemaphoreType.DMA((here, held[1] // 512))] * 2,
+        + [pltpu.SemaphoreType.DMA((here, held[1] // 256))] * 2,
     )
     got = exchange(payload.astype(F16).reshape(PARTS, here, -1))
     last = split + 2 * HEAD
@@ -462,7 +462,9 @@
     taken = move(sends, 1)
     (hidden,) = call(hidden_kernel, [((PARTS, here, units), BF16)], 8 * MIB, own, *taken)
     gathered = exchange(hidden).reshape(every, units)
-    parts = sum_wide_parts(jnp.dot(gathered, w_down, preferred_element_type=F32), core_flag)
+    parts = sum_wide_parts(
+        jnp.dot(gathered, w_down, preferred_element_type=F32).astype(BF16), core_flag
+    )
     (result,) = call(
         finish_kernel, [(hidden_in.shape, F32)], 8 * MIB, core_flag, *parts, middle, scalars=1
     )

time: 106 us -> 106 us (level)
  Pallas kernels: 9.15 us -> 10.3 us
    pallas_call x8, Pallas kernels: 9.15 us -> 10.3 us  [call(): pl.pallas_call(kernel, out_shape=[(jax.ShapeDtypeStruct if i < len(outs)...]
where the time goes in v6:
time: 106 us
  blocking collectives  42 us (40%)
  waiting for transfers between devices  30.7 us (29%)
  starting transfers between devices  21.3 us (20%)
  Pallas kernels  10.3 us (10%)
    all_to_all x3, blocking collectives, exchange(): return lax.all_to_all(payload, 'narrow', 0, 0, tiled=True)  42 us
    ppermute x6, waiting for transfers between devices, move(): lax.ppermute(block, ('wide', 'narrow'), plane_pairs(step, stage))  18.5 us
    pallas_call x8, Pallas kernels, call(): pl.pallas_call(kernel, out_shape=[(jax.ShapeDtypeStruct if i < len(outs)...  10.3 us
    ppermute x2, starting transfers between devices, sum_wide_parts(): lax.ppermute(partial, 'wide', CORE_SWAP)  7.22 us
    ppermute x2, waiting for transfers between devices, sum_wide_parts(): near = lax.ppermute(mine, 'wide', NEXT_Z)  5.87 us
    ppermute x2, starting transfers between devices, sum_wide_parts(): near = lax.ppermute(mine, 'wide', NEXT_Z)  4.42 us
    ppermute x2, starting transfers between devices, sum_wide_parts(): other_near = lax.ppermute(near, 'wide', CORE_SWAP)  4.41 us
    ppermute x6, starting transfers between devices, move(): lax.ppermute(block, ('wide', 'narrow'), plane_pairs(step, stage))  3.61 us
  transfers between devices with their start and end apart: 16, of which 13 were waited for; matrix products, arithmetic and copies ran while one was open for 0% of the time, Pallas kernels for 0%

profile of v6, /device:TPU:1, one launch (start us, length us, event | category | flops | bytes accessed | tf_op | source)
XLA Modules:
  0.0 106.2 jit_solution(1365110363486942728)
XLA Ops:
  0.0 4.8 %shard_map.145 = (f32[128,1408]{1,0:T(8,128)S(1)}, f32[128,512]{1,0:T(8,128)S(1)}, f32[8,128]{1,0:T(8,128)S(1)}, f32[8,128]{1,0:T(8,128)S(1)}, s32[8,128]{1,0:T(...) custom-call(s32[16]{0:T(128)S(1)} %fusion.3.blocks_ref, s32[1]{0:T(128)} %bitcast.core_ref, ...), custom_call_target="tpu_custom_call" | custom-call | bytes 9964132 | tf_op jit(solution)/shard_map/pallas_call | solution.py:63
  4.9 15.8 %all_to_all.15 = f16[16,8,1408]{2,1,0:T(8,128)(2,1)S(1)} all-to-all(f16[16,8,1408]{2,1,0:T(8,128)(2,1)S(1)} %convert_bitcast_fusion), channel_id=1, replica_groups=mesh['wide'=8,'narrow'=16] {'narrow'}, dimensions={0} | all-to-all | bytes 720896 | tf_op jit(solution)/shard_map/all_to_all | solution.py:330
  21.0 2.0 %shard_map.146 = bf16[16,8,1024]{2,1,0:T(8,128)(2,1)S(1)} custom-call(s32[8,128]{1,0:T(8,128)S(1)} %get-tuple-element.25.lengths_ref, f32[8,1280]{1,0:T(8,128)S(1)} %multiply_reduce_fusion.total_ref, f32[8,128]{1,0:T(8,128)S(1)} %reduce_sum.32.squares_ref, f32[8,128]{1,0:T(8,128)S(1)} %get-tuple-element.27.cos_ref, f32[8,128]{1,0:T(8,128)S(1)} %get-tuple-element.28.sin_ref, ...), custom_call_target="tpu_custom_call" | custom-call | bytes 8445952 | tf_op jit(solution)/shard_map/pallas_call | solution.py:63
  22.9 10.5 %all_to_all.16 = bf16[16,8,1024]{2,1,0:T(8,128)(2,1)S(1)} all-to-all(bf16[16,8,1024]{2,1,0:T(8,128)(2,1)S(1)} %shard_map.146), channel_id=1, replica_groups=mesh['wide'=8,'narrow'=16] {'narrow'}, dimensions={0} | all-to-all | bytes 524288 | tf_op jit(solution)/shard_map/all_to_all | solution.py:330
  33.8 3.1 %collective-permute-start = (f32[128,512]{1,0:T(8,128)S(1)}, f32[128,512]{1,0:T(8,128)S(1)}, u32[]{:S(2)}, u32[]{:S(2)}) collective-permute-start(f32[128,512]{1,0:T(8,128)S(1)} %fusion.1.mine_ref), channel_id=1, source_target_pairs={{0,16},{16,0},{32,48},{48,32},{64,80},{80,64},{96,112},{112,96},{1... | collective-permute-start | bytes 786440 | tf_op jit(solution)/shard_map/ppermute | solution.py:350
  36.9 1.2 %collective-permute-done.other_ref = f32[128,512]{1,0:T(8,128)S(1)} collective-permute-done((f32[128,512]{1,0:T(8,128)S(1)}, f32[128,512]{1,0:T(8,128)S(1)}, u32[]{:S(2)}, u32[]{:S(2)}) %collective-permute-start) | collective-permute-done | bytes 262176 | tf_op jit(solution)/shard_map/ppermute | solution.py:350
  38.1 3.8 %collective-permute-start.1 = (bf16[128,512]{1,0:T(8,128)(2,1)S(1)}, bf16[128,512]{1,0:T(8,128)(2,1)S(1)}, u32[]{:S(2)}, u32[]{:S(2)}) collective-permute-start(bf16[128,512]{1,0:T(8,128)(2,1)S(1)} %get-tuple-element.31.mine_ref), channel_id=1, source_target_pairs={{0,32},{16,112},{32,64},{48,16},{64,96},{80,48},{96,0},{112,80},{1... | collective-permute-start | bytes 393224 | tf_op jit(solution)/shard_map/ppermute | solution.py:353
  42.0 3.3 %collective-permute-done.1.near_ref = bf16[128,512]{1,0:T(8,128)(2,1)S(1)} collective-permute-done((bf16[128,512]{1,0:T(8,128)(2,1)S(1)}, bf16[128,512]{1,0:T(8,128)(2,1)S(1)}, u32[]{:S(2)}, u32[]{:S(2)}) %collective-permute-start.1) | collective-permute-done | bytes 131104 | tf_op jit(solution)/shard_map/ppermute | solution.py:353
  45.6 2.0 %collective-permute-done.3.far_ref = bf16[64,512]{1,0:T(8,128)(2,1)S(1)} collective-permute-done((bf16[64,512]{1,0:T(8,128)(2,1)S(1)}, bf16[64,512]{1,0:T(8,128)(2,1)S(1)}, u32[]{:S(2)}, u32[]{:S(2)}) %collective-permute-start.3) | collective-permute-done | bytes 65568 | tf_op jit(solution)/shard_map/ppermute | solution.py:354
  47.6 0.9 collective-permute-start.4
  48.4 0.9 collective-permute-done.4.other_far_ref
  49.3 1.8 %shard_map.148 = (f32[128,512]{1,0:T(8,128)S(1)}, f32[32,7296]{1,0:T(8,128)S(1)}, f32[32,7296]{1,0:T(8,128)S(1)}, f32[32,7296]{1,0:T(8,128)S(1)}, f32[32,7296]{1,0:T(8,128)S(1)}) custom-call(s32[1]{0:T(128)} %bitcast.core_ref, s32[16]{0:T(128)S(1)} %fusion.3.blocks_ref, bf16[128,512]{1,0:T(8,128)(2,1)S(1)} %get-tuple-element.31.mine_ref, ...), custom_call_target="tpu_custom_call" | custom-call | bytes 8128580 | tf_op jit(solution)/shard_map/pallas_call | solution.py:63
  51.3 0.6 collective-permute-start.7
  51.9 1.0 collective-permute-start.6
  53.0 6.0 %collective-permute-done.7 = f16[32,7296]{1,0:T(8,128)(2,1)S(1)} collective-permute-done((f16[32,7296]{1,0:T(8,128)(2,1)S(1)}, f16[32,7296]{1,0:T(8,128)(2,1)S(1)}, u32[]{:S(2)}, u32[]{:S(2)}) %collective-permute-start.7) | collective-permute-done | bytes 466976 | tf_op jit(solution)/shard_map/ppermute | solution.py:337
  59.1 2.1 %collective-permute-done.6 = f16[32,7296]{1,0:T(8,128)(2,1)S(1)} collective-permute-done((f16[32,7296]{1,0:T(8,128)(2,1)S(1)}, f16[32,7296]{1,0:T(8,128)(2,1)S(1)}, u32[]{:S(2)}, u32[]{:S(2)}) %collective-permute-start.6) | collective-permute-done | bytes 466976 | tf_op jit(solution)/shard_map/ppermute | solution.py:337
  61.2 4.9 %collective-permute-done.5 = f16[32,7296]{1,0:T(8,128)(2,1)S(1)} collective-permute-done((f16[32,7296]{1,0:T(8,128)(2,1)S(1)}, f16[32,7296]{1,0:T(8,128)(2,1)S(1)}, u32[]{:S(2)}, u32[]{:S(2)}) %collective-permute-start.5) | collective-permute-done | bytes 466976 | tf_op jit(solution)/shard_map/ppermute | solution.py:337
  66.8 0.8 collective-permute-start.10
  67.6 1.1 %collective-permute-start.9 = (f16[8,7296]{1,0:T(8,128)(2,1)S(1)}, f16[8,7296]{1,0:T(8,128)(2,1)S(1)}, u32[]{:S(2)}, u32[]{:S(2)}) collective-permute-start(f16[8,7296]{1,0:T(8,128)(2,1)S(1)} %convert_element_type.59), channel_id=1, source_target_pairs={{0,8},{1,9},{2,10},{3,11},{4,12},{5,13},{6,14},{7,15},{8,0},{9,1},... | collective-permute-start | bytes 350216 | tf_op jit(solution)/shard_map/ppermute | solution.py:337
  68.8 1.8 %collective-permute-done.10 = f16[8,7296]{1,0:T(8,128)(2,1)S(1)} collective-permute-done((f16[8,7296]{1,0:T(8,128)(2,1)S(1)}, f16[8,7296]{1,0:T(8,128)(2,1)S(1)}, u32[]{:S(2)}, u32[]{:S(2)}) %collective-permute-start.10) | collective-permute-done | bytes 116768 | tf_op jit(solution)/shard_map/ppermute | solution.py:337
  70.6 2.2 %collective-permute-done.9 = f16[8,7296]{1,0:T(8,128)(2,1)S(1)} collective-permute-done((f16[8,7296]{1,0:T(8,128)(2,1)S(1)}, f16[8,7296]{1,0:T(8,128)(2,1)S(1)}, u32[]{:S(2)}, u32[]{:S(2)}) %collective-permute-start.9) | collective-permute-done | bytes 116768 | tf_op jit(solution)/shard_map/ppermute | solution.py:337
  72.8 1.5 %collective-permute-done.8 = f16[8,7296]{1,0:T(8,128)(2,1)S(1)} collective-permute-done((f16[8,7296]{1,0:T(8,128)(2,1)S(1)}, f16[8,7296]{1,0:T(8,128)(2,1)S(1)}, u32[]{:S(2)}, u32[]{:S(2)}) %collective-permute-start.8) | collective-permute-done | bytes 116768 | tf_op jit(solution)/shard_map/ppermute | solution.py:337
  74.6 15.7 %all_to_all.17 = bf16[16,8,3584]{2,1,0:T(8,128)(2,1)S(1)} all-to-all(bf16[16,8,3584]{2,1,0:T(8,128)(2,1)S(1)} %shard_map.150), channel_id=1, replica_groups=mesh['wide'=8,'narrow'=16] {'narrow'}, dimensions={0} | all-to-all | bytes 1835008 | tf_op jit(solution)/shard_map/all_to_all | solution.py:330
  90.3 0.6 convolution_convert_fusion.mine_ref
  91.0 4.1 %collective-permute-start.11 = (bf16[128,512]{1,0:T(8,128)(2,1)S(1)}, bf16[128,512]{1,0:T(8,128)(2,1)S(1)}, u32[]{:S(2)}, u32[]{:S(2)}) collective-permute-start(bf16[128,512]{1,0:T(8,128)(2,1)S(1)} %convolution_convert_fusion.mine_ref), channel_id=1, source_target_pairs={{0,16},{16,0},{32,48},{48,32},{64,80},{80,64},{96,112},{112,96},{1... | collective-permute-start | bytes 393224 | tf_op jit(solution)/shard_map/ppermute | solution.py:350
  95.0 1.0 collective-permute-done.11.other_ref
  96.1 0.6 collective-permute-start.12
  96.7 0.7 collective-permute-start.14
  97.4 2.6 %collective-permute-done.12.near_ref = bf16[128,512]{1,0:T(8,128)(2,1)S(1)} collective-permute-done((bf16[128,512]{1,0:T(8,128)(2,1)S(1)}, bf16[128,512]{1,0:T(8,128)(2,1)S(1)}, u32[]{:S(2)}, u32[]{:S(2)}) %collective-permute-start.12) | collective-permute-done | bytes 131104 | tf_op jit(solution)/shard_map/ppermute | solution.py:353
  100.0 4.1 %collective-permute-start.13 = (bf16[128,512]{1,0:T(8,128)(2,1)S(1)}, bf16[128,512]{1,0:T(8,128)(2,1)S(1)}, u32[]{:S(2)}, u32[]{:S(2)}) collective-permute-start(bf16[128,512]{1,0:T(8,128)(2,1)S(1)} %collective-permute-done.12.near_ref), channel_id=1, source_target_pairs={{0,16},{16,0},{32,48},{48,32},{64,80},{80,64},{96,112},{112,96},{1... | collective-permute-start | bytes 393224 | tf_op jit(solution)/shard_map/ppermute | solution.py:355
  104.1 1.3 %collective-permute-done.15.other_far_ref = bf16[64,512]{1,0:T(8,128)(2,1)S(1)} collective-permute-done((bf16[64,512]{1,0:T(8,128)(2,1)S(1)}, bf16[64,512]{1,0:T(8,128)(2,1)S(1)}, u32[]{:S(2)}, u32[]{:S(2)}) %collective-permute-start.15) | collective-permute-done | bytes 65568 | tf_op jit(solution)/shard_map/ppermute | solution.py:356
  105.4 0.8 shard_map.152
  (43 shorter events, 2.5 us)
Async XLA Ops:
  0.0 33.5 %copy-start = (bf16[1024,512]{1,0:T(8,128)(2,1)S(1)}, bf16[1024,512]{1,0:T(8,128)(2,1)}, u32[]{:S(2)}) copy-start(bf16[1024,512]{1,0:T(8,128)(2,1)} %param.20) | copy-start | bytes 3145732
  0.0 20.6 %copy-start.5 = (f32[3]{0:T(128)S(1)}, f32[3]{0:T(128)}, u32[]{:S(2)}) copy-start(f32[3]{0:T(128)} %constant.90) | copy-start | bytes 40
  21.0 28.4 %copy-start.1 = (bf16[512,3584]{1,0:T(8,128)(2,1)S(1)}, bf16[512,3584]{1,0:T(8,128)(2,1)}, u32[]{:S(2)}) copy-start(bf16[512,3584]{1,0:T(8,128)(2,1)} %wg_ref.1) | copy-start | bytes 11010052
  21.0 28.4 %copy-start.2 = (bf16[512,3584]{1,0:T(8,128)(2,1)S(1)}, bf16[512,3584]{1,0:T(8,128)(2,1)}, u32[]{:S(2)}) copy-start(bf16[512,3584]{1,0:T(8,128)(2,1)} %wu_ref.1) | copy-start | bytes 11010052
  21.0 28.4 %copy-start.3 = (f32[512]{0:T(512)S(1)}, f32[512]{0:T(512)}, u32[]{:S(2)}) copy-start(f32[512]{0:T(512)} %param.21) | copy-start | bytes 6148
  33.8 4.3 %collective-permute-start = (f32[128,512]{1,0:T(8,128)S(1)}, f32[128,512]{1,0:T(8,128)S(1)}, u32[]{:S(2)}, u32[]{:S(2)}) collective-permute-start(f32[128,512]{1,0:T(8,128)S(1)} %fusion.1.mine_ref), channel_id=1, source_target_pairs={{0,16},{16,0},{32,48},{48,32},{64,80},{80,64},{96,112},{112,96},{1... | collective-permute-start | bytes 786440 | tf_op jit(solution)/shard_map/ppermute | solution.py:350
  38.1 7.1 %collective-permute-start.1 = (bf16[128,512]{1,0:T(8,128)(2,1)S(1)}, bf16[128,512]{1,0:T(8,128)(2,1)S(1)}, u32[]{:S(2)}, u32[]{:S(2)}) collective-permute-start(bf16[128,512]{1,0:T(8,128)(2,1)S(1)} %get-tuple-element.31.mine_ref), channel_id=1, source_target_pairs={{0,32},{16,112},{32,64},{48,16},{64,96},{80,48},{96,0},{112,80},{1... | collective-permute-start | bytes 393224 | tf_op jit(solution)/shard_map/ppermute | solution.py:353
  42.0 5.6 %collective-permute-start.3 = (bf16[64,512]{1,0:T(8,128)(2,1)S(1)}, bf16[64,512]{1,0:T(8,128)(2,1)S(1)}, u32[]{:S(2)}, u32[]{:S(2)}) collective-permute-start(bf16[64,512]{1,0:T(8,128)(2,1)S(1)} %get-tuple-element.32), channel_id=1, source_target_pairs={{0,64},{16,80},{32,96},{48,112},{64,0},{80,16},{96,32},{112,48},{1... | collective-permute-start | bytes 196616 | tf_op jit(solution)/shard_map/ppermute | solution.py:354
  45.3 4.1 %collective-permute-start.2 = (bf16[128,512]{1,0:T(8,128)(2,1)S(1)}, bf16[128,512]{1,0:T(8,128)(2,1)S(1)}, u32[]{:S(2)}, u32[]{:S(2)}) collective-permute-start(bf16[128,512]{1,0:T(8,128)(2,1)S(1)} %collective-permute-done.1.near_ref), channel_id=1, source_target_pairs={{0,16},{16,0},{32,48},{48,32},{64,80},{80,64},{96,112},{112,96},{1... | collective-permute-start | bytes 393224 | tf_op jit(solution)/shard_map/ppermute | solution.py:355
  47.6 1.8 %collective-permute-start.4 = (bf16[64,512]{1,0:T(8,128)(2,1)S(1)}, bf16[64,512]{1,0:T(8,128)(2,1)S(1)}, u32[]{:S(2)}, u32[]{:S(2)}) collective-permute-start(bf16[64,512]{1,0:T(8,128)(2,1)S(1)} %collective-permute-done.3.far_ref), channel_id=1, source_target_pairs={{0,16},{16,0},{32,48},{48,32},{64,80},{80,64},{96,112},{112,96},{1... | collective-permute-start | bytes 196616 | tf_op jit(solution)/shard_map/ppermute | solution.py:356
  51.3 7.8 %collective-permute-start.7 = (f16[32,7296]{1,0:T(8,128)(2,1)S(1)}, f16[32,7296]{1,0:T(8,128)(2,1)S(1)}, u32[]{:S(2)}, u32[]{:S(2)}) collective-permute-start(f16[32,7296]{1,0:T(8,128)(2,1)S(1)} %convert_element_type.55), channel_id=1, source_target_pairs={{0,3},{1,0},{2,1},{3,2},{4,7},{5,4},{6,5},{7,6},{8,11},{9,8},{10,9... | collective-permute-start | bytes 1400840 | tf_op jit(solution)/shard_map/ppermute | solution.py:337
  51.9 9.3 %collective-permute-start.6 = (f16[32,7296]{1,0:T(8,128)(2,1)S(1)}, f16[32,7296]{1,0:T(8,128)(2,1)S(1)}, u32[]{:S(2)}, u32[]{:S(2)}) collective-permute-start(f16[32,7296]{1,0:T(8,128)(2,1)S(1)} %convert_element_type.53), channel_id=1, source_target_pairs={{0,2},{1,3},{2,0},{3,1},{4,6},{5,7},{6,4},{7,5},{8,10},{9,11},{10,... | collective-permute-start | bytes 1400840 | tf_op jit(solution)/shard_map/ppermute | solution.py:337
  52.9 13.2 %collective-permute-start.5 = (f16[32,7296]{1,0:T(8,128)(2,1)S(1)}, f16[32,7296]{1,0:T(8,128)(2,1)S(1)}, u32[]{:S(2)}, u32[]{:S(2)}) collective-permute-start(f16[32,7296]{1,0:T(8,128)(2,1)S(1)} %convert_element_type.51), channel_id=1, source_target_pairs={{0,1},{1,2},{2,3},{3,0},{4,5},{5,6},{6,7},{7,4},{8,9},{9,10},{10,1... | collective-permute-start | bytes 1400840 | tf_op jit(solution)/shard_map/ppermute | solution.py:337
  66.7 23.6 %copy-start.4 = (bf16[3584,512]{1,0:T(8,128)(2,1)S(1)}, bf16[3584,512]{1,0:T(8,128)(2,1)}, u32[]{:S(2)}) copy-start(bf16[3584,512]{1,0:T(8,128)(2,1)} %param.24) | copy-start | bytes 11010052
  66.8 3.7 %collective-permute-start.10 = (f16[8,7296]{1,0:T(8,128)(2,1)S(1)}, f16[8,7296]{1,0:T(8,128)(2,1)S(1)}, u32[]{:S(2)}, u32[]{:S(2)}) collective-permute-start(f16[8,7296]{1,0:T(8,128)(2,1)S(1)} %convert_element_type.61), channel_id=1, source_target_pairs={{0,12},{1,13},{2,14},{3,15},{4,0},{5,1},{6,2},{7,3},{8,4},{9,5},{1... | collective-permute-start | bytes 350216 | tf_op jit(solution)/shard_map/ppermute | solution.py:337
  67.6 5.2 %collective-permute-start.9 = (f16[8,7296]{1,0:T(8,128)(2,1)S(1)}, f16[8,7296]{1,0:T(8,128)(2,1)S(1)}, u32[]{:S(2)}, u32[]{:S(2)}) collective-permute-start(f16[8,7296]{1,0:T(8,128)(2,1)S(1)} %convert_element_type.59), channel_id=1, source_target_pairs={{0,8},{1,9},{2,10},{3,11},{4,12},{5,13},{6,14},{7,15},{8,0},{9,1},... | collective-permute-start | bytes 350216 | tf_op jit(solution)/shard_map/ppermute | solution.py:337
  68.7 5.6 %collective-permute-start.8 = (f16[8,7296]{1,0:T(8,128)(2,1)S(1)}, f16[8,7296]{1,0:T(8,128)(2,1)S(1)}, u32[]{:S(2)}, u32[]{:S(2)}) collective-permute-start(f16[8,7296]{1,0:T(8,128)(2,1)S(1)} %convert_element_type.57), channel_id=1, source_target_pairs={{0,4},{1,5},{2,6},{3,7},{4,8},{5,9},{6,10},{7,11},{8,12},{9,13},{1... | collective-permute-start | bytes 350216 | tf_op jit(solution)/shard_map/ppermute | solution.py:337
  91.0 5.1 %collective-permute-start.11 = (bf16[128,512]{1,0:T(8,128)(2,1)S(1)}, bf16[128,512]{1,0:T(8,128)(2,1)S(1)}, u32[]{:S(2)}, u32[]{:S(2)}) collective-permute-start(bf16[128,512]{1,0:T(8,128)(2,1)S(1)} %convolution_convert_fusion.mine_ref), channel_id=1, source_target_pairs={{0,16},{16,0},{32,48},{48,32},{64,80},{80,64},{96,112},{112,96},{1... | collective-permute-start | bytes 393224 | tf_op jit(solution)/shard_map/ppermute | solution.py:350
  96.1 3.9 %collective-permute-start.12 = (bf16[128,512]{1,0:T(8,128)(2,1)S(1)}, bf16[128,512]{1,0:T(8,128)(2,1)S(1)}, u32[]{:S(2)}, u32[]{:S(2)}) collective-permute-start(bf16[128,512]{1,0:T(8,128)(2,1)S(1)} %get-tuple-element.42.mine_ref), channel_id=1, source_target_pairs={{0,32},{16,112},{32,64},{48,16},{64,96},{80,48},{96,0},{112,80},{1... | collective-permute-start | bytes 393224 | tf_op jit(solution)/shard_map/ppermute | solution.py:353
  96.7 7.4 %collective-permute-start.14 = (bf16[64,512]{1,0:T(8,128)(2,1)S(1)}, bf16[64,512]{1,0:T(8,128)(2,1)S(1)}, u32[]{:S(2)}, u32[]{:S(2)}) collective-permute-start(bf16[64,512]{1,0:T(8,128)(2,1)S(1)} %get-tuple-element.43), channel_id=1, source_target_pairs={{0,64},{16,80},{32,96},{48,112},{64,0},{80,16},{96,32},{112,48},{1... | collective-permute-start | bytes 196616 | tf_op jit(solution)/shard_map/ppermute | solution.py:354
  100.0 5.4 %collective-permute-start.13 = (bf16[128,512]{1,0:T(8,128)(2,1)S(1)}, bf16[128,512]{1,0:T(8,128)(2,1)S(1)}, u32[]{:S(2)}, u32[]{:S(2)}) collective-permute-start(bf16[128,512]{1,0:T(8,128)(2,1)S(1)} %collective-permute-done.12.near_ref), channel_id=1, source_target_pairs={{0,16},{16,0},{32,48},{48,32},{64,80},{80,64},{96,112},{112,96},{1... | collective-permute-start | bytes 393224 | tf_op jit(solution)/shard_map/ppermute | solution.py:355
  104.1 1.3 %collective-permute-start.15 = (bf16[64,512]{1,0:T(8,128)(2,1)S(1)}, bf16[64,512]{1,0:T(8,128)(2,1)S(1)}, u32[]{:S(2)}, u32[]{:S(2)}) collective-permute-start(bf16[64,512]{1,0:T(8,128)(2,1)S(1)} %collective-permute-done.14.far_ref), channel_id=1, source_target_pairs={{0,16},{16,0},{32,48},{48,32},{64,80},{80,64},{96,112},{112,96},{1... | collective-permute-start | bytes 196616 | tf_op jit(solution)/shard_map/ppermute | solution.py:356
